TPU v7x, 128 devices: a whole 4x4x4 slice. The times are simulated.
128 devices in a mesh: dp: 2 (over x_lo), expert: 32 (over y, z, core), tensor: 2 (over x_hi).
Axes of the slice: x: 4 (x_hi: 2, x_lo: 2; x = x_hi * 2 + x_lo), y: 4, z: 4, core: 2. Of those that a mesh axis runs over, the one named last changes fastest.
Arguments:
- hidden_in: bfloat16 [8192, 2048], P(('dp', 'expert')), may hold values from -6 to 6
- prenorm: bfloat16 [2048], P(('dp', 'expert')), may hold values from 0.5 to 1.5
- query_proj: bfloat16 [2048, 3072], P(('dp', 'expert'), 'tensor'), may hold values from -0.125 to 0.125
- latent_proj: bfloat16 [2048, 576], P(('dp', 'expert')), may hold values from -0.125 to 0.125
- midnorm: bfloat16 [512], P(('dp', 'expert')), may hold values from 0.5 to 1.5
- expand_proj: bfloat16 [512, 4096], P(('dp', 'expert'), 'tensor'), may hold values from -0.25 to 0.25
- output_proj: bfloat16 [2048, 2048], P('tensor', ('dp', 'expert')), may hold values from -0.5 to 0.5
- postnorm: bfloat16 [2048], P(('dp', 'expert')), may hold values from 0.5 to 1.5
- shared_gate: bfloat16 [2048, 2816], P(('dp', 'expert'), 'tensor'), may hold values from -0.125 to 0.125
- shared_up: bfloat16 [2048, 2816], P(('dp', 'expert'), 'tensor'), may hold values from -0.125 to 0.125
- shared_down: bfloat16 [2816, 2048], P('tensor', ('dp', 'expert')), may hold values from -0.109375 to 0.109375
- expert_gate: bfloat16 [32, 2048, 1408], P('expert', None, 'tensor'), may hold values from -0.125 to 0.125
- expert_up: bfloat16 [32, 2048, 1408], P('expert', None, 'tensor'), may hold values from -0.125 to 0.125
- expert_down: bfloat16 [32, 1408, 2048], P('expert', 'tensor'), may hold values from -0.15625 to 0.15625
- segments: int32 [8192], replicated, may hold values from 0 to 7, as said below
- routes: int32 [8192, 6], P(('dp', 'expert')), may hold values from 0 to 31, all different within a row; in each aligned block of 128 rows (0 to 127, 128 to 255, ...) at most 30 rows name the same one
- route_weights: float32 [8192, 6], P(('dp', 'expert')), may hold values from 0.3 to 1
- cotangent: bfloat16 [8192, 2048], P(('dp', 'expert')), may hold values from -6 to 6
Outputs:
- block_out: bfloat16 [8192, 2048], P(('dp', 'expert'))
- input_grad: float32 [8192, 2048], P(('dp', 'expert'))
- prenorm_grad: float32 [2048], P(('dp', 'expert'))
- query_grad: float32 [2048, 3072], P(('dp', 'expert'), 'tensor')
- latent_grad: float32 [2048, 576], P(('dp', 'expert'))
- midnorm_grad: float32 [512], P(('dp', 'expert'))
- expand_grad: float32 [512, 4096], P(('dp', 'expert'), 'tensor')
- output_grad: float32 [2048, 2048], P('tensor', ('dp', 'expert'))
- postnorm_grad: float32 [2048], P(('dp', 'expert'))
- shared_gate_grad: float32 [2048, 2816], P(('dp', 'expert'), 'tensor')
- shared_up_grad: float32 [2048, 2816], P(('dp', 'expert'), 'tensor')
- shared_down_grad: float32 [2816, 2048], P('tensor', ('dp', 'expert'))
- expert_gate_grad: float32 [32, 2048, 1408], P('expert', None, 'tensor')
- expert_up_grad: float32 [32, 2048, 1408], P('expert', None, 'tensor')
- expert_down_grad: float32 [32, 1408, 2048], P('expert', 'tensor')
Inputs may be any that keep to these rules, and one draw needn't show every extreme that they name: `segments`: ids never fall along the tokens; the r-th block of 4096 tokens starts with id 4 r and holds ids 4 r to 4 r + 3 only. `routes`: each token names 6 different experts; among the 128 tokens of one device (aligned blocks) no expert is named more than 30 times.
All inputs are finite; a program needn't handle non-finite values.
Results may differ from a plain program's by a relative error of at most 0.023.
Values may be sent and summed in bfloat16 or wider, within the bound.
No kernel may reach another device: no remote copies, remote signals or barrier semaphores. Data moves between devices by JAX's collectives and lax.ppermute only.
A program may use at most 256 MiB of HBM per device.

v0:
```python
import math

import jax
import jax.numpy as jnp
from jax import lax
from jax.sharding import PartitionSpec as P

D = 2048
QN = 128
QR = 64
DV = 128
LATENT = 512
TOPK = 6
WIN = 1024


epsilon = 1e-06
neg_big = -1e30


def shifted(block, axis, distance):
    devices = range(lax.axis_size(axis))
    route = [(i - distance, i) for i in devices if i - distance in devices]
    return lax.ppermute(block, axis, route)


def matmul(left_op, right_op):
    return jnp.dot(left_op, right_op, preferred_element_type=jnp.float32)


def transposed_left_product(left_op, right_op):
    return lax.dot_general(
        left_op, right_op, (((0,), (0,)), ((), ())), preferred_element_type=jnp.float32
    )


def matmul_nt(left_op, right_op):
    return lax.dot_general(
        left_op, right_op, (((1,), (1,)), ((), ())), preferred_element_type=jnp.float32
    )


def rms_forward(values, gain_vec):
    inverse = lax.rsqrt(jnp.mean(values * values, axis=-1, keepdims=True) + epsilon)
    return (values * inverse * gain_vec, inverse)


def rms_backward(values, inverse, gain_vec, upstream):
    scaled = upstream * gain_vec
    inner_mean = jnp.mean(scaled * values, axis=-1, keepdims=True)
    back_values = inverse * (scaled - values * inner_mean * inverse * inverse)
    gain_grad = jnp.sum(upstream * values * inverse, axis=0)
    return (back_values, gain_grad)


def rope_tables(positions, width):
    half_width = width // 2
    frequency = jnp.exp(
        -math.log(10000.0) * jnp.arange(half_width, dtype=jnp.float32) * (2.0 / width)
    )
    angles = positions[:, None] * frequency[None, :]
    return (jnp.cos(angles), jnp.sin(angles))


def rotate(values, cosine, sine_tab):
    half_width = values.shape[-1] // 2
    first_half = values[..., :half_width]
    second_half = values[..., half_width:]
    return jnp.concatenate(
        [
            first_half * cosine - second_half * sine_tab,
            first_half * sine_tab + second_half * cosine,
        ],
        axis=-1,
    )


def shards(
    hidden_in,
    prenorm,
    query_proj,
    latent_proj,
    midnorm,
    expand_proj,
    output_proj,
    postnorm,
    shared_gate,
    shared_up,
    shared_down,
    expert_gate,
    expert_up,
    expert_down,
    segments,
    routes,
    route_weights,
    cotangent,
):
    gathered = (
        lax.all_gather(prenorm, ("dp", "expert"), axis=0, tiled=True),
        lax.all_gather(query_proj, ("dp", "expert"), axis=0, tiled=True),
        lax.all_gather(latent_proj, ("dp", "expert"), axis=0, tiled=True),
        lax.all_gather(midnorm, ("dp", "expert"), axis=0, tiled=True),
        lax.all_gather(expand_proj, ("dp", "expert"), axis=0, tiled=True),
        lax.all_gather(output_proj, ("dp", "expert"), axis=1, tiled=True),
        lax.all_gather(postnorm, ("dp", "expert"), axis=0, tiled=True),
        lax.all_gather(shared_gate, ("dp", "expert"), axis=0, tiled=True),
        lax.all_gather(shared_up, ("dp", "expert"), axis=0, tiled=True),
        lax.all_gather(shared_down, ("dp", "expert"), axis=1, tiled=True),
    )
    gain_one, w_query, w_latent, gain_mid, w_expand, w_output, gain_two, w_sgate, w_sup, w_sdown = (
        gathered
    )
    tok_rows = hidden_in.shape[0]
    head_count = w_query.shape[1] // (QN + QR)
    behind = WIN // tok_rows
    expert_count = lax.axis_size("expert")
    capacity = max(2, min(tok_rows, 5 * tok_rows * TOPK // (4 * expert_count)))
    expert_pos = lax.axis_index("expert")
    row_start = (lax.axis_index("dp") * expert_count + expert_pos) * tok_rows
    score_scale = 1.0 / math.sqrt(QN + QR)
    inputs = hidden_in.astype(jnp.float32)
    normed_one, inverse_one = rms_forward(inputs, gain_one.astype(jnp.float32))
    h_one = normed_one.astype(jnp.bfloat16)
    queries = matmul(h_one, w_query).reshape(tok_rows, head_count, QN + QR)
    q_nope = queries[:, :, :QN].astype(jnp.bfloat16)
    kv_pre = matmul(h_one, w_latent)
    latent_raw = kv_pre[:, :LATENT]
    latent_normed, inverse_mid = rms_forward(latent_raw, gain_mid.astype(jnp.float32))
    positions = (expert_pos * tok_rows + jnp.arange(tok_rows, dtype=jnp.int32)).astype(jnp.float32)
    cosine, sine_tab = rope_tables(positions, QR)
    latent = jnp.concatenate(
        [latent_normed, rotate(kv_pre[:, LATENT:], cosine, sine_tab)], axis=1
    ).astype(jnp.bfloat16)
    w_heads = w_expand.reshape(LATENT, head_count, QN + DV)
    w_key = w_heads[:, :, :QN]
    w_value = w_heads[:, :, QN:]
    q_latent = jnp.einsum("thn,chn->thc", q_nope, w_key, preferred_element_type=jnp.float32)
    q_rotated = rotate(queries[:, :, QN:], cosine[:, None, :], sine_tab[:, None, :])
    q_full = jnp.concatenate([q_latent, q_rotated], axis=2).astype(jnp.bfloat16)
    pieces = []
    for offset in range(behind, 0, -1):
        pieces.append(shifted(latent, "expert", offset))
    window = jnp.concatenate(pieces + [latent], axis=0)
    padded_seg = jnp.concatenate([jnp.full((behind * tok_rows,), -1, jnp.int32), segments], axis=0)
    seg_keys = lax.dynamic_slice_in_dim(padded_seg, row_start, (behind + 1) * tok_rows, 0)
    seg_query = lax.dynamic_slice_in_dim(segments, row_start, tok_rows, 0)
    offsets = (
        jnp.arange(tok_rows, dtype=jnp.int32)[:, None]
        + behind * tok_rows
        - jnp.arange((behind + 1) * tok_rows, dtype=jnp.int32)[None, :]
    )
    visible = (seg_query[:, None] == seg_keys[None, :]) & (offsets >= 0) & (offsets < WIN)

    def score_block():
        raw = (
            jnp.einsum("thc,kc->htk", q_full, window, preferred_element_type=jnp.float32)
            * score_scale
        )
        return jnp.where(visible[None], raw, neg_big)

    logits = score_block()
    row_max = jnp.max(logits, axis=2, keepdims=True)
    expo_vals = jnp.exp(logits - row_max)
    expo_sum = jnp.sum(expo_vals, axis=2, keepdims=True)
    log_total = row_max + jnp.log(expo_sum)
    probs_low = (expo_vals / expo_sum).astype(jnp.bfloat16)
    o_latent = jnp.einsum(
        "htk,kc->thc", probs_low, window[:, :LATENT], preferred_element_type=jnp.float32
    ).astype(jnp.bfloat16)
    o_heads = (
        jnp.einsum("thc,chv->thv", o_latent, w_value, preferred_element_type=jnp.float32)
        .astype(jnp.bfloat16)
        .reshape(tok_rows, head_count * DV)
    )
    attention = lax.psum(matmul(o_heads, w_output), "tensor")
    mid = inputs + attention
    normed_two, inverse_two = rms_forward(mid, gain_two.astype(jnp.float32))
    h_two = normed_two.astype(jnp.bfloat16)
    s_gate = matmul(h_two, w_sgate)
    s_up = matmul(h_two, w_sup)
    s_hidden = (s_gate * jax.nn.sigmoid(s_gate) * s_up).astype(jnp.bfloat16)
    s_part = matmul(s_hidden, w_sdown)
    entries = tok_rows * TOPK
    flat_routes = routes.reshape(entries)
    onehot = (flat_routes[:, None] == jnp.arange(expert_count, dtype=jnp.int32)[None, :]).astype(
        jnp.int32
    )
    earlier = jnp.cumsum(onehot, axis=0) - onehot
    slot_index = jnp.sum(earlier * onehot, axis=1)
    target = flat_routes * capacity + slot_index
    slot_owner = (
        jnp.full((expert_count * capacity,), entries, jnp.int32)
        .at[target]
        .set(jnp.arange(entries, dtype=jnp.int32))
    )
    padded_rows = jnp.concatenate([h_two, jnp.zeros((1, D), jnp.bfloat16)], axis=0)
    send_rows = padded_rows[slot_owner // TOPK].reshape(expert_count, capacity, D)
    arrived = lax.all_to_all(send_rows, "expert", split_axis=0, concat_axis=0, tiled=True)
    expert_rows = arrived.reshape(-1, D)
    gate_pre = matmul(expert_rows, expert_gate[0])
    up_pre = matmul(expert_rows, expert_up[0])
    hidden = (gate_pre * jax.nn.sigmoid(gate_pre) * up_pre).astype(jnp.bfloat16)
    partial_value = matmul(hidden, expert_down[0]).reshape(arrived.shape)
    returned = lax.all_to_all(
        partial_value.astype(jnp.bfloat16), "expert", split_axis=0, concat_axis=0, tiled=True
    ).astype(partial_value.dtype)
    item_shape = (arrived.shape[0], arrived.shape[1], gate_pre.shape[1])
    returned, gate_kept, up_kept, arrived = (
        returned,
        gate_pre.reshape(item_shape),
        up_pre.reshape(item_shape),
        arrived,
    )
    back_routes = returned.reshape(-1, D)[target]
    shared_sum, routed_sum = (
        lax.psum(s_part.astype(jnp.bfloat16), "tensor").astype(jnp.float32),
        lax.psum(back_routes.astype(jnp.bfloat16), "tensor").astype(jnp.float32),
    )
    routed_low = (
        lax.optimization_barrier(routed_sum.astype(jnp.bfloat16))
        .astype(jnp.float32)
        .reshape(tok_rows, TOPK, D)
    )
    routed = jnp.sum(route_weights[:, :, None] * routed_low, axis=1)
    output = mid + shared_sum + routed
    upstream = cotangent.astype(jnp.float32)
    grad_rows = (
        (route_weights[:, :, None] * upstream[:, None, :]).astype(jnp.bfloat16).reshape(entries, D)
    )
    padded_grads = jnp.concatenate([grad_rows, jnp.zeros((1, D), jnp.bfloat16)], axis=0)
    grad_send = padded_grads[slot_owner].reshape(expert_count, capacity, D)
    grad_arrived = lax.all_to_all(grad_send, "expert", split_axis=0, concat_axis=0, tiled=True)
    grad_flat = grad_arrived.reshape(-1, D)
    gate_flat = gate_kept.reshape(grad_flat.shape[0], -1)
    up_flat = up_kept.reshape(grad_flat.shape[0], -1)
    gate_sig = jax.nn.sigmoid(gate_flat)
    active = gate_flat * gate_sig
    hidden = (active * up_flat).astype(jnp.bfloat16)
    back_hidden = matmul_nt(grad_flat, expert_down[0])
    expert_down_weight_gradient = transposed_left_product(hidden, grad_flat)
    back_gate = (back_hidden * up_flat * gate_sig * (1.0 + gate_flat * (1.0 - gate_sig))).astype(
        jnp.bfloat16
    )
    up_output_gradient = (back_hidden * active).astype(jnp.bfloat16)
    flattened_rows = arrived.reshape(-1, D)
    expert_gate_weight_gradient = transposed_left_product(flattened_rows, back_gate)
    expert_up_weight_gradient = transposed_left_product(flattened_rows, up_output_gradient)
    row_grad = (
        matmul_nt(back_gate, expert_gate[0]) + matmul_nt(up_output_gradient, expert_up[0])
    ).reshape(expert_count, capacity, D)
    row_back = lax.all_to_all(row_grad, "expert", split_axis=0, concat_axis=0, tiled=True)
    expert_output_totals = (
        lax.psum(expert_gate_weight_gradient.astype(jnp.bfloat16), "dp").astype(jnp.float32),
        lax.psum(expert_up_weight_gradient.astype(jnp.bfloat16), "dp").astype(jnp.float32),
        lax.psum(expert_down_weight_gradient.astype(jnp.bfloat16), "dp").astype(jnp.float32),
    )
    row_width = row_back.shape[2]
    back_routed = jnp.sum(
        row_back.reshape(-1, row_width)[target].reshape(tok_rows, TOPK, row_width), axis=1
    )
    s_grad_low = upstream.astype(jnp.bfloat16)
    grad_sdown = transposed_left_product(s_hidden, s_grad_low)
    back_shidden = matmul_nt(s_grad_low, w_sdown)
    s_sig = jax.nn.sigmoid(s_gate)
    s_active = s_gate * s_sig
    back_sgate = (back_shidden * s_up * s_sig * (1.0 + s_gate * (1.0 - s_sig))).astype(jnp.bfloat16)
    back_sup = (back_shidden * s_active).astype(jnp.bfloat16)
    grad_sgate = transposed_left_product(h_two, back_sgate)
    grad_sup = transposed_left_product(h_two, back_sup)
    shared_back = matmul_nt(back_sgate, w_sgate) + matmul_nt(back_sup, w_sup)
    local_back = shared_back + back_routed
    back_two = lax.psum(local_back, "tensor")
    back_midnorm, grad_gain_two = rms_backward(
        mid, inverse_two, gain_two.astype(jnp.float32), back_two
    )
    back_mid = upstream + back_midnorm
    back_attn = back_mid.astype(jnp.bfloat16)
    grad_output = transposed_left_product(o_heads, back_attn)
    back_heads = (
        matmul_nt(back_attn, w_output).astype(jnp.bfloat16).reshape(tok_rows, head_count, DV)
    )
    grad_value = jnp.einsum(
        "thc,thv->chv", o_latent, back_heads, preferred_element_type=jnp.float32
    )
    back_olatent = jnp.einsum(
        "thv,chv->thc", back_heads, w_value, preferred_element_type=jnp.float32
    ).astype(jnp.bfloat16)
    probs_back = jnp.exp(score_block() - log_total)
    back_probs = jnp.einsum(
        "thc,kc->htk", back_olatent, window[:, :LATENT], preferred_element_type=jnp.float32
    )
    row_delta = jnp.sum(probs_back * back_probs, axis=2, keepdims=True)
    back_scores = (probs_back * (back_probs - row_delta) * score_scale).astype(jnp.bfloat16)
    back_qfull = jnp.einsum("htk,kc->thc", back_scores, window, preferred_element_type=jnp.float32)
    value_part = jnp.einsum(
        "htk,thc->kc",
        probs_back.astype(jnp.bfloat16),
        back_olatent,
        preferred_element_type=jnp.float32,
    )
    back_window = jnp.einsum("htk,thc->kc", back_scores, q_full, preferred_element_type=jnp.float32)
    back_window = back_window + jnp.pad(value_part, ((0, 0), (0, QR)))
    back_qlatent = back_qfull[:, :, :LATENT].astype(jnp.bfloat16)
    back_qrope = rotate(back_qfull[:, :, LATENT:], cosine[:, None, :], -sine_tab[:, None, :])
    grad_key = jnp.einsum("thc,thn->chn", back_qlatent, q_nope, preferred_element_type=jnp.float32)
    back_qnope = jnp.einsum("thc,chn->thn", back_qlatent, w_key, preferred_element_type=jnp.float32)
    back_queries = (
        jnp.concatenate([back_qnope, back_qrope], axis=2)
        .reshape(tok_rows, head_count * (QN + QR))
        .astype(jnp.bfloat16)
    )
    grad_query = transposed_left_product(h_one, back_queries)
    back_one_part = matmul_nt(back_queries, w_query)
    grad_expand = jnp.concatenate([grad_key, grad_value], axis=2).reshape(
        LATENT, head_count * (QN + DV)
    )
    back_latent = back_window[behind * tok_rows :]
    for offset in range(1, behind + 1):
        lower_row = (behind - offset) * tok_rows
        back_latent = back_latent + shifted(
            back_window[lower_row : lower_row + tok_rows].astype(jnp.bfloat16), "expert", -offset
        ).astype(jnp.float32)
    back_latent, back_one_sum = (
        lax.psum(back_latent.astype(jnp.bfloat16), "tensor").astype(jnp.float32),
        lax.psum(back_one_part.astype(jnp.bfloat16), "tensor").astype(jnp.float32),
    )
    back_raw, grad_gain_mid = rms_backward(
        latent_raw, inverse_mid, gain_mid.astype(jnp.float32), back_latent[:, :LATENT]
    )
    back_kvpre = jnp.concatenate(
        [back_raw, rotate(back_latent[:, LATENT:], cosine, -sine_tab)], axis=1
    ).astype(jnp.bfloat16)
    grad_latent = transposed_left_product(h_one, back_kvpre)
    back_one = back_one_sum + matmul_nt(back_kvpre, w_latent)
    back_innorm, grad_gain_one = rms_backward(
        inputs, inverse_one, gain_one.astype(jnp.float32), back_one
    )
    input_grad = back_mid + back_innorm
    reduced = (
        lax.psum_scatter(grad_gain_one, ("dp", "expert"), scatter_dimension=0, tiled=True),
        lax.psum_scatter(grad_query, ("dp", "expert"), scatter_dimension=0, tiled=True),
        lax.psum_scatter(grad_latent, ("dp", "expert"), scatter_dimension=0, tiled=True),
        lax.psum_scatter(grad_gain_mid, ("dp", "expert"), scatter_dimension=0, tiled=True),
        lax.psum_scatter(grad_expand, ("dp", "expert"), scatter_dimension=0, tiled=True),
        lax.psum_scatter(grad_output, ("dp", "expert"), scatter_dimension=1, tiled=True),
        lax.psum_scatter(grad_gain_two, ("dp", "expert"), scatter_dimension=0, tiled=True),
        lax.psum_scatter(grad_sgate, ("dp", "expert"), scatter_dimension=0, tiled=True),
        lax.psum_scatter(grad_sup, ("dp", "expert"), scatter_dimension=0, tiled=True),
        lax.psum_scatter(grad_sdown, ("dp", "expert"), scatter_dimension=1, tiled=True),
    )
    return (
        output.astype(jnp.bfloat16),
        input_grad,
        reduced[0],
        reduced[1],
        reduced[2],
        reduced[3],
        reduced[4],
        reduced[5],
        reduced[6],
        reduced[7],
        reduced[8],
        reduced[9],
        expert_output_totals[0][None],
        expert_output_totals[1][None],
        expert_output_totals[2][None],
    )


def solution(mesh):
    placed = (
        P(("dp", "expert"), None),
        P(("dp", "expert")),
        P(("dp", "expert"), "tensor"),
        P(("dp", "expert"), None),
        P(("dp", "expert")),
        P(("dp", "expert"), "tensor"),
        P("tensor", ("dp", "expert")),
        P(("dp", "expert")),
        P(("dp", "expert"), "tensor"),
        P(("dp", "expert"), "tensor"),
        P("tensor", ("dp", "expert")),
        P("expert", None, "tensor"),
        P("expert", None, "tensor"),
        P("expert", "tensor", None),
        P(),
        P(("dp", "expert"), None),
        P(("dp", "expert"), None),
        P(("dp", "expert"), None),
    )
    return jax.shard_map(
        shards,
        mesh=mesh,
        in_specs=placed,
        out_specs=(
            P(("dp", "expert"), None),
            P(("dp", "expert"), None),
            P(("dp", "expert")),
            P(("dp", "expert"), "tensor"),
            P(("dp", "expert"), None),
            P(("dp", "expert")),
            P(("dp", "expert"), "tensor"),
            P("tensor", ("dp", "expert")),
            P(("dp", "expert")),
            P(("dp", "expert"), "tensor"),
            P(("dp", "expert"), "tensor"),
            P("tensor", ("dp", "expert")),
            P("expert", None, "tensor"),
            P("expert", None, "tensor"),
            P("expert", "tensor", None),
        ),
        check_vma=False,
    )
```

profile of v0, /device:TPU:0, one launch (start us, length us, event | category | flops | bytes accessed | tf_op | source)
XLA Modules:
  0.0 3600.4 jit_solution(10611524224176701631)
XLA Ops:
  15.2 150.6 %all-reduce.11 = (bf16[2048]{0:T(1024)(128)(2,1)S(1)}, bf16[512]{0:T(512)(128)(2,1)S(1)}, bf16[2048]{0:T(1024)(128)(2,1)}) all-reduce(bf16[2048]{0:T(1024)(128)(2,1)S(1)} %dynamic-update-slice, bf16[512]{0:T(512)(128)(2,1)S(1)} %dynamic-update-slice.1, ...), channel_id=1, replica_groups=mesh['dp'=2,'expert'=32,'tensor'=2] {'dp','expert'}, use_global_device_ids=true, to_apply=%add.4 | all-reduce | flops 4608 | bytes 18432
  178.4 43.7 %all-gather.12.cloned.1.call-done = bf16[512,2048]{1,0:T(8,128)(2,1)} async-done(((bf16[8,2048]{1,0:T(8,128)(2,1)}), bf16[512,2048]{1,0:T(8,128)(2,1)}) %all-gather.12.cloned.1.call-update) | async-done | bytes 2097168 | tf_op jit(solution)/shard_map/all_gather | solution.py:103
  228.8 5.4 collective-permute-start.3
  259.4 75.2 %all-gather.10.cloned.1.call-done = bf16[2048,1536]{1,0:T(8,128)(2,1)} async-done(((bf16[32,1536]{1,0:T(8,128)(2,1)}), bf16[2048,1536]{1,0:T(8,128)(2,1)}) %all-gather.10.cloned.1.call-update) | async-done | bytes 6291472 | tf_op jit(solution)/shard_map/all_gather | solution.py:100
  334.6 5.4 fusion.107
  359.7 82.4 %all-gather.14.cloned.1.call-done = bf16[1024,2048]{0,1:T(8,128)(2,1)} async-done(((bf16[1024,32]{0,1:T(8,128)(2,1)}), bf16[1024,2048]{0,1:T(8,128)(2,1)}) %all-gather.14.cloned.1.call-update) | async-done | bytes 4194320 | tf_op jit(solution)/shard_map/all_gather | solution.py:104
  442.1 4.8 fusion.116
  456.3 5.4 mul.469
  461.7 8.3 mul.470
  478.9 11.2 gather_fusion.2
  490.1 5.0 reshape.330
  495.1 5.5 all-to-all-start.2
  504.1 5.9 gather_fusion
  510.1 5.0 reshape.324
  515.1 44.2 %all-to-all-done.2 = bf16[32,30,2048]{2,1,0:T(8,128)(2,1)} async-done(((bf16[32,30,2048]{2,1,0:T(8,128)(2,1)}), bf16[32,30,2048]{2,1,0:T(8,128)(2,1)}, u32[]{:S(2)}, u32[]{:S(2)}) %all-to-all-start.2) | async-done | bytes 3932192 | tf_op jit(solution)/shard_map/all_to_all | solution.py:232
  559.3 6.4 all-to-all-start
  566.5 5.1 reshape.331
  571.6 51.4 %all-to-all-done = bf16[32,30,2048]{2,1,0:T(8,128)(2,1)} async-done(((bf16[32,30,2048]{2,1,0:T(8,128)(2,1)}), bf16[32,30,2048]{2,1,0:T(8,128)(2,1)}, u32[]{:S(2)}, u32[]{:S(2)}) %all-to-all-start) | async-done | bytes 3932192 | tf_op jit(solution)/shard_map/all_to_all | solution.py:198
  623.0 5.0 reshape.325
  628.0 6.4 fusion.16
  637.7 5.5 multiply_convert_fusion.1
  646.5 5.9 convolution_add_fusion
  652.4 7.1 reshape.332
  659.5 6.7 all-to-all-start.3
  672.3 5.2 convolution_convert_fusion
  681.7 99.4 %all-to-all-done.3 = f32[32,30,2048]{2,1,0:T(8,128)} async-done(((f32[32,30,2048]{2,1,0:T(8,128)}), f32[32,30,2048]{2,1,0:T(8,128)}, u32[]{:S(2)}, u32[]{:S(2)}) %all-to-all-start.3) | async-done | bytes 7864352 | tf_op jit(solution)/shard_map/all_to_all | solution.py:251
  781.1 16.3 all-to-all-start.1
  801.2 78.4 %all-gather.18.cloned.1.call-done = bf16[2048,1408]{1,0:T(8,128)(2,1)} async-done(((bf16[32,1408]{1,0:T(8,128)(2,1)}), bf16[2048,1408]{1,0:T(8,128)(2,1)}) %all-gather.18.cloned.1.call-update) | async-done | bytes 5767184 | tf_op jit(solution)/shard_map/all_gather | solution.py:107
  883.2 109.0 %all-gather.20.cloned.1.call-done = bf16[1408,2048]{0,1:T(8,128)(2,1)} async-done(((bf16[1408,32]{0,1:T(8,128)(2,1)}), bf16[1408,2048]{0,1:T(8,128)(2,1)}) %all-gather.20.cloned.1.call-update) | async-done | bytes 5767184 | tf_op jit(solution)/shard_map/all_gather | solution.py:108
  992.2 4.7 multiply_convert_fusion.5
  996.9 4.7 fusion.119
  1001.6 7.2 reshape.333
  1008.9 10.5 gather_fusion.3
  1019.4 7.9 reshape.334
  1027.3 6.0 reduce_sum.135
  1033.3 5.7 fusion.23
  1039.2 5.5 convolution_convert_fusion.5
  1044.7 5.0 reshape.338
  1049.8 9.8 gather_fusion.1
  1059.6 26.7 all-reduce.21.cloned.1.call-done
  1092.9 4.7 fusion.55
  1097.7 5.3 convolution_bitcast_fusion.1
  1103.0 11.6 fusion.32
  1114.6 11.9 fusion.115
  1143.8 5.8 convolution_convert_fusion.4
  1149.6 6.0 collective-permute-done.15
  1157.9 7.4 fusion.10
  1179.6 5.4 copy.161
  1186.0 5.8 fusion.120
  1192.8 5.9 fusion.121
  1199.7 6.0 fusion.122
  1206.0 78.2 %all-reduce.23.cloned.1.call-done = (bf16[768,2048]{1,0:T(8,128)(2,1)}, bf16[128,2048]{1,0:T(8,128)(2,1)}, bf16[128,2048]{1,0:T(8,128)(2,1)}, bf16[128,576]{0,1:T(8,128)(2,1)}) async-done(((bf16[768,2048]{1,0:T(8,128)(2,1)}, bf16[128,2048]{1,0:T(8,128)(2,1)}, bf16[128,2048]{1,0:T(8,128)(2,1)}, bf16[128,576]{0,1:T(8,128)(2,1)}), (bf16[768,2048]{1,0:T(8,128)(2,1)}, bf16[128,2048]{1,0:T(8,128)(2,1)}, ...) | async-done | bytes 4341776 | tf_op jit(solution)/shard_map/psum | solution.py:217
  1296.7 6.5 fusion.105
  1304.5 194.4 %all-reduce.25.cloned.1.call-done = (bf16[1,2048,704]{1,2,0:T(8,128)(2,1)}, bf16[1,2048,704]{1,2,0:T(8,128)(2,1)}, bf16[1,704,2048]{2,1,0:T(8,128)(2,1)}) async-done(((bf16[1,2048,704]{1,2,0:T(8,128)(2,1)}, bf16[1,2048,704]{1,2,0:T(8,128)(2,1)}, bf16[1,704,2048]{2,1,0:T(8,128)(2,1)}), (bf16[1,2048,704]{1,2,0:T(8,128)(2,1)}, bf16[1,2048,704]{1,2,0:T(8,128)(2,1)}, ...) | async-done | bytes 8650768 | tf_op jit(solution)/shard_map/psum | solution.py:253
  1498.9 5.3 broadcast_in_dim.43
  1512.9 279.5 %all-reduce.10 = (f32[2048]{0:T(1024)S(1)}, f32[512]{0:T(512)S(1)}, f32[2048]{0:T(1024)S(1)}) all-reduce(f32[2048]{0:T(1024)S(1)} %get-tuple-element.17, f32[512]{0:T(512)S(1)} %copy-done.62, f32[2048]{0:T(1024)S(1)} %copy-done.56), channel_id=2, replica_groups=mesh['dp'=2,'expert'=32,'tensor'=2] {'dp','expert'}, use_global_device_ids=true, to_apply=%region_22.23.clone | all-reduce | flops 4608 | bytes 36864
  1793.6 6.5 reshape.340
  1800.7 6.8 multiply_reduce_fusion
  1810.7 284.8 %reduce-scatter.16.cloned.1.call-done = f32[32,1408]{1,0:T(8,128)} async-done(((f32[2048,1408]{1,0:T(8,128)}), f32[32,1408]{1,0:T(8,128)}) %reduce-scatter.16.cloned.1.call-update) | async-done | bytes 180240 | tf_op jit(solution)/shard_map/reduce_scatter | solution.py:347
  2095.5 302.4 %reduce-scatter.18.cloned.1.call-done = f32[32,1408]{1,0:T(8,128)} async-done(((f32[2048,1408]{1,0:T(8,128)}), f32[32,1408]{1,0:T(8,128)}) %reduce-scatter.18.cloned.1.call-update) | async-done | bytes 180240 | tf_op jit(solution)/shard_map/reduce_scatter | solution.py:348
  2397.9 302.3 %reduce-scatter.20.cloned.1.call-done = f32[1408,32]{0,1:T(8,128)} async-done(((f32[1408,2048]{0,1:T(8,128)}), f32[1408,32]{0,1:T(8,128)}) %reduce-scatter.20.cloned.1.call-update) | async-done | bytes 180240 | tf_op jit(solution)/shard_map/reduce_scatter | solution.py:349
  2700.2 292.2 %reduce-scatter.10.cloned.1.call-done = f32[32,576]{1,0:T(8,128)} async-done(((f32[2048,576]{1,0:T(8,128)}), f32[32,576]{1,0:T(8,128)}) %reduce-scatter.10.cloned.1.call-update) | async-done | bytes 73744 | tf_op jit(solution)/shard_map/reduce_scatter | solution.py:342
  2992.5 297.1 %reduce-scatter.14.cloned.1.call-done = f32[1024,32]{0,1:T(8,128)} async-done(((f32[1024,2048]{0,1:T(8,128)}), f32[1024,32]{0,1:T(8,128)}) %reduce-scatter.14.cloned.1.call-update) | async-done | bytes 131088 | tf_op jit(solution)/shard_map/reduce_scatter | solution.py:345
  3289.5 303.8 %reduce-scatter.8.cloned.1.call-done = f32[32,1536]{1,0:T(8,128)} async-done(((f32[2048,1536]{1,0:T(8,128)}), f32[32,1536]{1,0:T(8,128)}) %reduce-scatter.8.cloned.1.call-update) | async-done | bytes 196624 | tf_op jit(solution)/shard_map/reduce_scatter | solution.py:341
  (336 shorter events, 186.5 us)
Async XLA Ops:
  7.2 630.5 %copy-start = (bf16[1,704,2048]{2,1,0:T(8,128)(2,1)S(1)}, bf16[1,704,2048]{2,1,0:T(8,128)(2,1)}, u32[]{:S(2)}) copy-start(bf16[1,704,2048]{2,1,0:T(8,128)(2,1)} %param.31) | copy-start | bytes 8650756
  7.2 161.6 %all-gather.8.cloned.1.call-start = ((), (), s32[]{:S(2)}) async-start(), calls=%async_computation.11 | async-start | bytes 2662400 | tf_op jit(solution)/shard_map/all_gather | solution.py:101
  7.9 214.1 %all-gather.12.cloned.1.call-start = ((), (), s32[]{:S(2)}) async-start(), calls=%async_computation.13 | async-start | bytes 2129920 | tf_op jit(solution)/shard_map/all_gather | solution.py:103
  8.7 325.9 %all-gather.10.cloned.1.call-start = ((), (), s32[]{:S(2)}) async-start(), calls=%async_computation.12 | async-start | bytes 6389760 | tf_op jit(solution)/shard_map/all_gather | solution.py:100
  9.4 432.6 %all-gather.14.cloned.1.call-start = ((), (), s32[]{:S(2)}) async-start(), calls=%async_computation.14 | async-start | bytes 4259840 | tf_op jit(solution)/shard_map/all_gather | solution.py:104
  10.0 490.7 %all-reduce.19.cloned.1.call-start = ((), (), s32[]{:S(2)}) async-start(), calls=%async_computation.15 | async-start | bytes 2097152 | tf_op jit(solution)/shard_map/psum | solution.py:175
  165.9 168.7 %copy-start.39 = (f32[2048]{0:T(1024)}, f32[2048]{0:T(1024)S(1)}, u32[]{:S(2)}) copy-start(f32[2048]{0:T(1024)S(1)} %convert_element_type.180) | copy-start | bytes 24580
  165.9 11.5 copy-start.54
  166.7 10.8 copy-start.67
  166.7 10.7 copy-start.69
  168.7 8.7 copy-start.57
  173.6 67.6 %collective-permute-start = (bf16[128,576]{0,1:T(8,128)(2,1)}, bf16[128,576]{0,1:T(8,128)(2,1)}, u32[]{:S(2)}, u32[]{:S(2)}) collective-permute-start(bf16[128,576]{0,1:T(8,128)(2,1)} %pad_maximum_fusion.5), channel_id=1, source_target_pairs={{0,16},{2,18},{4,20},{6,22},{8,24},{10,26},{12,28},{14,30},{16,32}... | collective-permute-start | bytes 442376 | tf_op jit(solution)/shard_map/ppermute | solution.py:24
  175.5 68.5 %collective-permute-start.1 = (bf16[128,576]{0,1:T(8,128)(2,1)}, bf16[128,576]{0,1:T(8,128)(2,1)}, u32[]{:S(2)}, u32[]{:S(2)}) collective-permute-start(bf16[128,576]{0,1:T(8,128)(2,1)} %pad_maximum_fusion.5), channel_id=1, source_target_pairs={{0,14},{2,16},{4,18},{6,20},{8,22},{10,24},{12,26},{14,28},{16,30}... | collective-permute-start | bytes 442376 | tf_op jit(solution)/shard_map/ppermute | solution.py:24
  178.3 156.3 %copy-start.2 = (bf16[128,2048]{1,0:T(8,128)(2,1)S(1)}, bf16[128,2048]{1,0:T(8,128)(2,1)}, u32[]{:S(2)}) copy-start(bf16[128,2048]{1,0:T(8,128)(2,1)} %param.18) | copy-start | bytes 1572868
  226.0 22.2 collective-permute-start.2
  228.8 23.9 collective-permute-start.3
  234.2 20.0 collective-permute-start.4
  241.1 14.8 collective-permute-start.5
  244.0 12.6 collective-permute-start.6
  248.1 9.2 collective-permute-start.7
  259.4 86.1 %copy-start.42 = (f32[128,32]{1,0:T(8,128)S(1)}, f32[128,32]{1,0:T(8,128)}, u32[]{:S(2)}) copy-start(f32[128,32]{1,0:T(8,128)} %copy.133) | copy-start | bytes 49156
  259.4 86.1 %copy-start.48 = (f32[128,32]{1,0:T(8,128)S(1)}, f32[128,32]{1,0:T(8,128)}, u32[]{:S(2)}) copy-start(f32[128,32]{1,0:T(8,128)} %copy.135) | copy-start | bytes 49156
  442.1 12.5 copy-start.65
  446.9 350.6 %all-gather.16.cloned.1.call-start = ((), (), s32[]{:S(2)}) async-start(), calls=%async_computation.16 | async-start | bytes 5857280 | tf_op jit(solution)/shard_map/all_gather | solution.py:106
  447.5 432.1 %all-gather.18.cloned.1.call-start = ((), (), s32[]{:S(2)}) async-start(), calls=%async_computation.17 | async-start | bytes 5857280 | tf_op jit(solution)/shard_map/all_gather | solution.py:107
  495.1 64.2 %all-to-all-start.2 = ((bf16[32,30,2048]{2,1,0:T(8,128)(2,1)}), bf16[32,30,2048]{2,1,0:T(8,128)(2,1)}, u32[]{:S(2)}, u32[]{:S(2)}) async-start(bf16[32,30,2048]{2,1,0:T(8,128)(2,1)} %reshape.330), calls=%async_computation.2 | async-start | bytes 8388608 | tf_op jit(solution)/shard_map/all_to_all | solution.py:232
  559.3 63.7 %all-to-all-start = ((bf16[32,30,2048]{2,1,0:T(8,128)(2,1)}), bf16[32,30,2048]{2,1,0:T(8,128)(2,1)}, u32[]{:S(2)}, u32[]{:S(2)}) async-start(bf16[32,30,2048]{2,1,0:T(8,128)(2,1)} %reshape.324), calls=%async_computation | async-start | bytes 8388608 | tf_op jit(solution)/shard_map/all_to_all | solution.py:198
  565.8 426.4 %all-gather.20.cloned.1.call-start = ((), (), s32[]{:S(2)}) async-start(), calls=%async_computation.18 | async-start | bytes 5857280 | tf_op jit(solution)/shard_map/all_gather | solution.py:108
  659.5 121.5 %all-to-all-start.3 = ((f32[32,30,2048]{2,1,0:T(8,128)}), f32[32,30,2048]{2,1,0:T(8,128)}, u32[]{:S(2)}, u32[]{:S(2)}) async-start(f32[32,30,2048]{2,1,0:T(8,128)} %reshape.332), calls=%async_computation.3 | async-start | bytes 16777216 | tf_op jit(solution)/shard_map/all_to_all | solution.py:251
  681.7 115.8 %copy-start.8 = (bf16[128,2048]{1,0:T(8,128)(2,1)S(1)}, bf16[128,2048]{1,0:T(8,128)(2,1)}, u32[]{:S(2)}) copy-start(bf16[128,2048]{1,0:T(8,128)(2,1)} %copy-done.7) | copy-start | bytes 1572868
  781.1 263.7 %all-to-all-start.1 = ((bf16[32,30,2048]{2,1,0:T(8,128)(2,1)}), bf16[32,30,2048]{2,1,0:T(8,128)(2,1)}, u32[]{:S(2)}, u32[]{:S(2)}) async-start(bf16[32,30,2048]{2,1,0:T(8,128)(2,1)} %copy.145), calls=%async_computation.1 | async-start | bytes 8388608 | tf_op jit(solution)/shard_map/all_to_all | solution.py:204
  797.4 288.9 %all-reduce.21.cloned.1.call-start = ((), (), s32[]{:S(2)}) async-start(), calls=%async_computation.19 | async-start | bytes 2097152 | tf_op jit(solution)/shard_map/psum | solution.py:272
  801.1 191.1 %copy-start.19 = (bf16[128,2048]{1,0:T(8,128)(2,1)S(1)}, bf16[128,2048]{1,0:T(8,128)(2,1)}, u32[]{:S(2)}) copy-start(bf16[128,2048]{1,0:T(8,128)(2,1)} %param.35) | copy-start | bytes 1572868
  1039.0 245.2 %all-reduce.23.cloned.1.call-start = ((), (), s32[]{:S(2)}) async-start(), calls=%async_computation.27 | async-start | bytes 8683520 | tf_op jit(solution)/shard_map/psum | solution.py:217
  1049.8 36.5 %copy-start.5 = (f32[128,2048]{1,0:T(8,128)S(1)}, f32[128,2048]{1,0:T(8,128)}, u32[]{:S(2)}) copy-start(f32[128,2048]{1,0:T(8,128)} %copy-done.4) | copy-start | bytes 3145732
  1090.2 199.9 %copy-start.10 = (f32[128,2048]{1,0:T(8,128)}, f32[128,2048]{1,0:T(8,128)S(1)}, u32[]{:S(2)}) copy-start(f32[128,2048]{1,0:T(8,128)S(1)} %multiply_add_fusion) | copy-start | bytes 3145732
  1103.0 11.6 copy-start.38
  1126.6 11.2 copy-start.43
  1129.0 10.7 collective-permute-start.10
  1130.2 10.8 collective-permute-start.11
  1131.5 11.0 collective-permute-start.12
  1132.8 16.7 collective-permute-start.13
  1134.1 15.4 collective-permute-start.14
  1139.6 10.0 copy-start.26
  1139.6 16.0 collective-permute-start.15
  1141.0 14.6 collective-permute-start.8
  1142.5 13.1 collective-permute-start.9
  1157.7 341.2 %all-reduce.25.cloned.1.call-start = ((), (), s32[]{:S(2)}) async-start(), calls=%async_computation.28 | async-start | bytes 17301504 | tf_op jit(solution)/shard_map/psum | solution.py:253
  1174.4 636.3 %reduce-scatter.12.cloned.1.call-start = ((), (), s32[]{:S(2)}) async-start(), calls=%async_computation.22 | async-start | bytes 4259840 | tf_op jit(solution)/shard_map/reduce_scatter | solution.py:344
  1185.0 910.5 %reduce-scatter.16.cloned.1.call-start = ((), (), s32[]{:S(2)}) async-start(), calls=%async_computation.24 | async-start | bytes 11714560 | tf_op jit(solution)/shard_map/reduce_scatter | solution.py:347
  1191.9 1206.0 %reduce-scatter.18.cloned.1.call-start = ((), (), s32[]{:S(2)}) async-start(), calls=%async_computation.25 | async-start | bytes 11714560 | tf_op jit(solution)/shard_map/reduce_scatter | solution.py:348
  1198.8 1501.5 %reduce-scatter.20.cloned.1.call-start = ((), (), s32[]{:S(2)}) async-start(), calls=%async_computation.26 | async-start | bytes 11714560 | tf_op jit(solution)/shard_map/reduce_scatter | solution.py:349
  1205.7 79.5 %copy-start.16 = (f32[128,576]{0,1:T(8,128)S(1)}, f32[128,576]{0,1:T(8,128)}, u32[]{:S(2)}) copy-start(f32[128,576]{0,1:T(8,128)} %copy-done.15) | copy-start | bytes 884740
  1205.7 79.5 %copy-start.55 = (f32[512]{0:T(512)S(1)}, f32[512]{0:T(512)}, u32[]{:S(2)}) copy-start(f32[512]{0:T(512)} %copy-done.54) | copy-start | bytes 6148
  1205.7 79.5 %copy-start.64 = (f32[128]{0:T(128)S(1)}, f32[128]{0:T(128)}, u32[]{:S(2)}) copy-start(f32[128]{0:T(128)} %copy-done.63) | copy-start | bytes 1540
  1205.7 80.4 %copy-start.68 = (f32[32]{0:T(128)S(1)}, f32[32]{0:T(128)}, u32[]{:S(2)}) copy-start(f32[32]{0:T(128)} %copy-done.67) | copy-start | bytes 388
  1205.7 80.4 %copy-start.70 = (f32[128]{0:T(128)S(1)}, f32[128]{0:T(128)}, u32[]{:S(2)}) copy-start(f32[128]{0:T(128)} %copy-done.69) | copy-start | bytes 1540
  1205.7 81.1 %copy-start.3 = (bf16[128,2048]{1,0:T(8,128)(2,1)S(1)}, bf16[128,2048]{1,0:T(8,128)(2,1)}, u32[]{:S(2)}) copy-start(bf16[128,2048]{1,0:T(8,128)(2,1)} %param.18) | copy-start | bytes 1572868
  1205.7 81.1 %copy-start.40 = (f32[2048]{0:T(1024)S(1)}, f32[2048]{0:T(1024)}, u32[]{:S(2)}) copy-start(f32[2048]{0:T(1024)} %copy-done.39) | copy-start | bytes 24580
  1205.7 81.1 %copy-start.58 = (f32[128]{0:T(128)S(1)}, f32[128]{0:T(128)}, u32[]{:S(2)}) copy-start(f32[128]{0:T(128)} %copy-done.57) | copy-start | bytes 1540
  1205.8 1786.7 %reduce-scatter.10.cloned.1.call-start = ((), (), s32[]{:S(2)}) async-start(), calls=%async_computation.21 | async-start | bytes 5324800 | tf_op jit(solution)/shard_map/reduce_scatter | solution.py:342
  1290.1 1999.4 %reduce-scatter.14.cloned.1.call-start = ((), (), s32[]{:S(2)}) async-start(), calls=%async_computation.23 | async-start | bytes 8519680 | tf_op jit(solution)/shard_map/reduce_scatter | solution.py:345
  1295.6 2297.7 %reduce-scatter.8.cloned.1.call-start = ((), (), s32[]{:S(2)}) async-start(), calls=%async_computation.20 | async-start | bytes 12779520 | tf_op jit(solution)/shard_map/reduce_scatter | solution.py:341
  1807.5 1785.8 %copy-start.1 = (bf16[1,704,2048]{2,1,0:T(8,128)(2,1)S(1)}, bf16[1,704,2048]{2,1,0:T(8,128)(2,1)}, u32[]{:S(2)}) copy-start(bf16[1,704,2048]{2,1,0:T(8,128)(2,1)} %param.31) | copy-start | bytes 8650756
  (50 other events, 186.2 us)
Sparse Core Ops, SparseCore 0:
  9.7 106.9 all-gather.7
  118.5 103.5 all-gather.11
  223.8 110.8 all-gather.9
  336.2 105.8 all-gather.13
  447.0 47.1 all-reduce.18
  495.9 173.6 all-gather.15
  671.5 208.0 all-gather.17
  881.4 110.7 all-gather.19
  1039.2 47.0 all-reduce.20
  1157.8 126.4 all-reduce.22
  1287.7 211.1 all-reduce.24
  1501.7 291.7 reduce-scatter.11
  1796.6 298.8 reduce-scatter.15
  2098.5 299.3 reduce-scatter.17
  2400.8 299.3 reduce-scatter.19
  2703.2 289.2 reduce-scatter.9
  2995.4 294.0 reduce-scatter.13
  3292.5 300.7 reduce-scatter.7
where the time goes:
time: 3610 us; the launch traced here: 3600 us
  waiting for transfers between devices  2680 us (74%)
  blocking collectives  430 us (12%)
  matrix products  179 us (5%)
  local copies, waits for them, and re-layouts  172 us (5%)
  starting transfers between devices  69.8 us (2%)
  other arithmetic  55.3 us (2%)
    unnamed x2, blocking collectives  430 us
    reduce_scatter x1, waiting for transfers between devices, shards(): lax.psum_scatter(grad_query, ('dp', 'expert'), scatter_dimension=0, tiled...  304 us
    reduce_scatter x1, waiting for transfers between devices, shards(): lax.psum_scatter(grad_sup, ('dp', 'expert'), scatter_dimension=0, tiled=T...  302 us
    reduce_scatter x1, waiting for transfers between devices, shards(): lax.psum_scatter(grad_sdown, ('dp', 'expert'), scatter_dimension=1, tiled...  302 us
    reduce_scatter x1, waiting for transfers between devices, shards(): lax.psum_scatter(grad_output, ('dp', 'expert'), scatter_dimension=1, tile...  297 us
    reduce_scatter x1, waiting for transfers between devices, shards(): lax.psum_scatter(grad_latent, ('dp', 'expert'), scatter_dimension=0, tile...  292 us
    reduce_scatter x1, waiting for transfers between devices, shards(): lax.psum_scatter(grad_sgate, ('dp', 'expert'), scatter_dimension=0, tiled...  285 us
    psum x1, waiting for transfers between devices, shards(): lax.psum(expert_gate_weight_gradient.astype(jnp.bfloat16), 'dp')  194 us
  transfers between devices with their start and end apart: 38, of which 20 were waited for; matrix products, arithmetic and copies ran while one was open for 10% of the time, Pallas kernels for 0%

commit v1 on v0

v1 whole, which is shorter than its diff:
```python
import math

import jax
import jax.numpy as jnp
from jax import lax
from jax.sharding import Mesh, PartitionSpec as P

D = 2048
QN = 128
QR = 64
DV = 128
LATENT = 512
TOPK = 6
WIN = 1024
SLOTS = 32

epsilon = 1e-06
neg_big = -1e30
f32 = jnp.float32
bf16 = jnp.bfloat16
PLANE = ("y", "z")
EXPERT = ("y", "z", "core")


def swapped(block, axis):
    return lax.ppermute(block, axis, [(0, 1), (1, 0)])


def chip_shift(block, distance):
    chips = range(16)
    route = [(i - distance, i) for i in chips if i - distance in chips]
    return lax.ppermute(block, PLANE, route)


def matmul(left_op, right_op):
    return jnp.dot(left_op, right_op, preferred_element_type=f32)


def matmul_tn(left_op, right_op):
    return lax.dot_general(
        left_op, right_op, (((0,), (0,)), ((), ())), preferred_element_type=f32
    )


def matmul_nt(left_op, right_op):
    return lax.dot_general(
        left_op, right_op, (((1,), (1,)), ((), ())), preferred_element_type=f32
    )


def pair_sum(part, axis):
    low = lax.optimization_barrier(part.astype(bf16))
    return low.astype(f32) + swapped(low, axis).astype(f32)


def split_low(values):
    high = values.astype(bf16)
    return high, (values - high.astype(f32)).astype(bf16)


def rms_forward(values, gain_vec):
    inverse = lax.rsqrt(jnp.mean(values * values, axis=-1, keepdims=True) + epsilon)
    return (values * inverse * gain_vec, inverse)


def rms_backward(values, inverse, gain_vec, upstream):
    scaled = upstream * gain_vec
    inner_mean = jnp.mean(scaled * values, axis=-1, keepdims=True)
    back_values = inverse * (scaled - values * inner_mean * inverse * inverse)
    gain_grad = jnp.sum(upstream * values * inverse, axis=0)
    return (back_values, gain_grad)


def rope_tables(positions, width):
    half_width = width // 2
    frequency = jnp.exp(
        -math.log(10000.0) * jnp.arange(half_width, dtype=f32) * (2.0 / width)
    )
    angles = positions[:, None] * frequency[None, :]
    return (jnp.cos(angles), jnp.sin(angles))


def rotate(values, cosine, sine_tab):
    half_width = values.shape[-1] // 2
    first_half = values[..., :half_width]
    second_half = values[..., half_width:]
    return jnp.concatenate(
        [
            first_half * cosine - second_half * sine_tab,
            first_half * sine_tab + second_half * cosine,
        ],
        axis=-1,
    )


def gather_dp(pack, dp):
    other = swapped(pack, "dp")
    return jnp.concatenate(
        [jnp.where(dp == 0, pack, other), jnp.where(dp == 0, other, pack)], axis=0
    )


def gather_plane(pair):
    mine = lax.all_gather(pair, PLANE, axis=0, tiled=True)
    return mine, swapped(mine, "core")


def scatter_rows(partial_rows, dp):
    part = lax.psum_scatter(partial_rows, PLANE, scatter_dimension=0, tiled=True)
    part = part.reshape(2, 32, part.shape[1])
    mine = lax.dynamic_index_in_dim(part, dp, 0, keepdims=False)
    theirs = lax.dynamic_index_in_dim(part, 1 - dp, 0, keepdims=False)
    return mine.astype(f32) + swapped(theirs, "dp").astype(f32)


def both_cores(own, sibling):
    return jnp.concatenate([own, sibling], axis=0)


def shards(
    hidden_in,
    prenorm,
    query_proj,
    latent_proj,
    midnorm,
    expand_proj,
    output_proj,
    postnorm,
    shared_gate,
    shared_up,
    shared_down,
    expert_gate,
    expert_up,
    expert_down,
    segments,
    routes,
    route_weights,
    cotangent,
):
    dp = lax.axis_index("dp")
    core = lax.axis_index("core")
    chip = lax.axis_index("y") * 4 + lax.axis_index("z")
    tok = hidden_in.shape[0]
    heads = query_proj.shape[1] // (QN + QR)
    half = D // 2
    expert_pos = chip * 2 + core
    score_scale = 1.0 / math.sqrt(QN + QR)

    gains = jnp.stack([prenorm, postnorm, jnp.pad(midnorm, (0, 24))], axis=1)
    pack_a = jnp.concatenate(
        [query_proj, latent_proj, jnp.pad(gains, ((0, 0), (0, 61)))], axis=1
    )
    pack_b = jnp.concatenate([expand_proj.reshape(32, 512), output_proj.T], axis=1)
    pack_c = jnp.concatenate([shared_gate, shared_up, shared_down.T], axis=1)
    own_a, sib_a = gather_plane(gather_dp(pack_a, dp))
    own_b, sib_b = gather_plane(gather_dp(pack_b, dp))
    own_c, sib_c = gather_plane(gather_dp(pack_c, dp))

    place = jnp.arange(D, dtype=jnp.int32)
    true_of = (
        (place // 32 % 2) * 1024
        + (place // 64 % 16) * 64
        + ((place // 1024) ^ core) * 32
        + place % 32
    )
    perm = (place[:, None] == true_of[None, :]).astype(bf16)
    place_l = jnp.arange(LATENT, dtype=jnp.int32)
    true_l = (
        (place_l // 8 % 2) * 256
        + (place_l // 16 % 16) * 16
        + ((place_l // 256) ^ core) * 8
        + place_l % 8
    )
    perm_l = (place_l[:, None] == true_l[None, :]).astype(bf16)
    mid_true = (
        (place // 32 % 2) * 256
        + (place // 64 % 16) * 16
        + ((place // 1024) ^ core) * 8
        + place % 32
    )
    perm_m = (
        (mid_true[:, None] == place_l[None, :]) & (place % 32 < 8)[:, None]
    ).astype(bf16)

    def unpermute(values):
        high, low = split_low(values)
        return matmul_nt(high, perm) + matmul_nt(low, perm)

    inputs = matmul(hidden_in, perm)
    upstream = matmul(cotangent, perm)
    up_low = upstream.astype(bf16)

    expert_ids = jnp.arange(32, dtype=jnp.int32)
    hits = routes[:, :, None] == expert_ids[None, None, :]
    named = jnp.sum(hits.astype(f32), axis=1)
    weight_te = jnp.sum(jnp.where(hits, route_weights[:, :, None], 0.0), axis=1)
    order = jnp.arange(tok, dtype=jnp.int32)
    earlier = (order[:, None] > order[None, :]).astype(bf16)
    rank = matmul(earlier, named.astype(bf16))
    rank_et = jnp.where(named > 0.5, rank, -1.0).T
    slot_ids = jnp.arange(SLOTS, dtype=jnp.int32).astype(f32)
    taken = rank_et[:, None, :] == slot_ids[None, :, None]
    slot_pick = taken.astype(bf16).reshape(32 * SLOTS, tok)
    slot_weight = jnp.where(taken, weight_te.T[:, None, :], 0.0).reshape(32 * SLOTS, tok)
    weight_hi, weight_lo = split_low(slot_weight)

    def exchange(rows):
        blocks = rows.reshape(32, SLOTS, D)
        return lax.all_to_all(blocks, EXPERT, split_axis=0, concat_axis=0, tiled=True).reshape(
            32 * SLOTS, D
        )

    grad_send = (matmul(weight_hi, cotangent) + matmul(weight_lo, cotangent)).astype(bf16)
    grad_rows = exchange(grad_send)

    pick = jnp.eye(8, 64, dtype=bf16)
    gain_rows = jnp.concatenate(
        [matmul_nt(pick, own_a[:, 2112:]), matmul_nt(pick, sib_a[:, 2112:])], axis=1
    )
    gain_one = gain_rows[0]
    gain_two = gain_rows[1]
    gain_mid = matmul(gain_rows.astype(bf16), perm_m)[2]

    normed_one, inverse_one = rms_forward(inputs, gain_one)
    h_one = normed_one.astype(bf16)
    projected = matmul(h_one[:, :half], own_a) + matmul(h_one[:, half:], sib_a)
    queries = projected[:, : heads * (QN + QR)].reshape(tok, heads, QN + QR)
    kv_pre = projected[:, heads * (QN + QR) : heads * (QN + QR) + LATENT + QR]
    q_nope = queries[:, :, :QN].astype(bf16)
    latent_raw = kv_pre[:, :LATENT]
    latent_normed, inverse_mid = rms_forward(latent_raw, gain_mid)
    positions = (expert_pos * tok + jnp.arange(tok, dtype=jnp.int32)).astype(f32)
    cosine, sine_tab = rope_tables(positions, QR)
    latent = jnp.concatenate(
        [latent_normed, rotate(kv_pre[:, LATENT:], cosine, sine_tab)], axis=1
    ).astype(bf16)
    expand_rows = jnp.concatenate([own_b[:, :512], sib_b[:, :512]], axis=0)
    w_expand = matmul(perm_l, expand_rows.reshape(LATENT, heads * (QN + DV))).astype(bf16)
    w_heads = w_expand.reshape(LATENT, heads, QN + DV)
    w_key = w_heads[:, :, :QN]
    w_value = w_heads[:, :, QN:]
    w_out_own = own_b[:, 512:]
    w_out_sib = sib_b[:, 512:]
    q_latent = jnp.einsum("thn,chn->thc", q_nope, w_key, preferred_element_type=f32)
    q_rotated = rotate(queries[:, :, QN:], cosine[:, None, :], sine_tab[:, None, :])
    q_full = jnp.concatenate([q_latent, q_rotated], axis=2).astype(bf16)

    own_blocks = jnp.stack([chip_shift(latent, k) for k in (4, 3, 2, 1)] + [latent])
    sib_blocks = swapped(
        lax.dynamic_slice_in_dim(own_blocks, 1 - core, 4, 0), "core"
    )
    window = jnp.concatenate([own_blocks, sib_blocks], axis=0).reshape(9 * tok, LATENT + QR)
    block_chip = jnp.concatenate(
        [chip - 4 + jnp.arange(5, dtype=jnp.int32), chip - 4 + core + jnp.arange(4, dtype=jnp.int32)]
    )
    block_core = jnp.concatenate(
        [jnp.full((5,), core, jnp.int32), jnp.full((4,), 1 - core, jnp.int32)]
    )
    block_id = block_chip * 2 + block_core
    seg_blocks = lax.dynamic_slice_in_dim(segments.reshape(2, 32, tok), dp, 1, 0)[0]
    chosen = jnp.arange(32, dtype=jnp.int32)[None, :, None] == block_id[:, None, None]
    seg_keys = jnp.sum(jnp.where(chosen, seg_blocks[None] + 1, 0), axis=1).reshape(9 * tok) - 1
    seg_query = lax.dynamic_index_in_dim(seg_blocks, expert_pos, 0, keepdims=False)
    key_pos = (block_id[:, None] * tok + jnp.arange(tok, dtype=jnp.int32)[None, :]).reshape(9 * tok)
    query_pos = expert_pos * tok + jnp.arange(tok, dtype=jnp.int32)
    offsets = query_pos[:, None] - key_pos[None, :]
    visible = (seg_query[:, None] == seg_keys[None, :]) & (offsets >= 0) & (offsets < WIN)

    def score_block():
        raw = jnp.einsum("thc,kc->htk", q_full, window, preferred_element_type=f32) * score_scale
        return jnp.where(visible[None], raw, neg_big)

    logits = score_block()
    row_max = jnp.max(logits, axis=2, keepdims=True)
    expo_vals = jnp.exp(logits - row_max)
    expo_sum = jnp.sum(expo_vals, axis=2, keepdims=True)
    log_total = row_max + jnp.log(expo_sum)
    probs_low = (expo_vals / expo_sum).astype(bf16)
    o_latent = jnp.einsum(
        "htk,kc->thc", probs_low, window[:, :LATENT], preferred_element_type=f32
    ).astype(bf16)
    o_heads = (
        jnp.einsum("thc,chv->thv", o_latent, w_value, preferred_element_type=f32)
        .astype(bf16)
        .reshape(tok, heads * DV)
    )
    attention = pair_sum(
        jnp.concatenate([matmul_nt(o_heads, w_out_own), matmul_nt(o_heads, w_out_sib)], axis=1),
        "tensor",
    )
    mid = inputs + attention
    normed_two, inverse_two = rms_forward(mid, gain_two)
    h_two = normed_two.astype(bf16)

    h_two_true = matmul_nt(h_two, perm).astype(bf16)
    expert_rows = exchange(matmul(slot_pick, h_two_true).astype(bf16))

    fs = shared_gate.shape[1]
    s_both = matmul(h_two[:, :half], own_c[:, : 2 * fs]) + matmul(h_two[:, half:], sib_c[:, : 2 * fs])
    s_gate = s_both[:, :fs]
    s_up = s_both[:, fs:]
    s_sig = jax.nn.sigmoid(s_gate)
    s_active = s_gate * s_sig
    s_hidden = (s_active * s_up).astype(bf16)
    s_part = jnp.concatenate(
        [matmul_nt(s_hidden, own_c[:, 2 * fs :]), matmul_nt(s_hidden, sib_c[:, 2 * fs :])], axis=1
    )
    back_shidden = matmul(up_low[:, :half], own_c[:, 2 * fs :]) + matmul(
        up_low[:, half:], sib_c[:, 2 * fs :]
    )
    back_sgate = (back_shidden * s_up * s_sig * (1.0 + s_gate * (1.0 - s_sig))).astype(bf16)
    back_sup = (back_shidden * s_active).astype(bf16)
    back_sboth = jnp.concatenate([back_sgate, back_sup], axis=1)
    shared_back = jnp.concatenate(
        [matmul_nt(back_sboth, own_c[:, : 2 * fs]), matmul_nt(back_sboth, sib_c[:, : 2 * fs])], axis=1
    )
    h_two_pair = both_cores(h_two[:, :half], swapped(h_two[:, half:], "core"))
    up_pair = both_cores(up_low[:, :half], swapped(up_low[:, half:], "core"))
    s_acts = jnp.concatenate([back_sboth, s_hidden], axis=1)
    s_pair = both_cores(s_acts, swapped(s_acts, "core"))
    shared_rows = jnp.concatenate(
        [matmul_tn(h_two_pair, s_pair[:, : 2 * fs]), matmul_tn(up_pair, s_pair[:, 2 * fs :])], axis=1
    ).astype(bf16)
    shared_grads = scatter_rows(shared_rows, dp)

    gate_pre = matmul(expert_rows, expert_gate[0])
    up_pre = matmul(expert_rows, expert_up[0])
    gate_sig = jax.nn.sigmoid(gate_pre)
    active = gate_pre * gate_sig
    hidden = (active * up_pre).astype(bf16)
    back_hidden = matmul_nt(grad_rows, expert_down[0])
    back_gate = (back_hidden * up_pre * gate_sig * (1.0 + gate_pre * (1.0 - gate_sig))).astype(bf16)
    back_up = (back_hidden * active).astype(bf16)
    row_grad = (matmul_nt(back_gate, expert_gate[0]) + matmul_nt(back_up, expert_up[0])).astype(bf16)
    row_back = exchange(row_grad)
    e_part = matmul(hidden, expert_down[0]).astype(bf16)
    e_part, row_back = lax.optimization_barrier((e_part, row_back))
    returned = exchange(e_part)
    expert_grads = tuple(
        pair_sum(g, "dp")
        for g in (
            matmul_tn(expert_rows, back_gate),
            matmul_tn(expert_rows, back_up),
            matmul_tn(hidden, grad_rows),
        )
    )
    routed = matmul_tn(weight_hi, returned) + matmul_tn(weight_lo, returned)
    output = unpermute(mid) + pair_sum(unpermute(s_part) + routed, "tensor")

    back_routed = matmul(matmul_tn(slot_pick, row_back).astype(bf16), perm)
    back_two = pair_sum(shared_back + back_routed, "tensor")
    back_midnorm, grad_gain_two = rms_backward(mid, inverse_two, gain_two, back_two)
    back_mid = upstream + back_midnorm
    back_attn = back_mid.astype(bf16)

    back_heads = (
        (matmul(back_attn[:, :half], w_out_own) + matmul(back_attn[:, half:], w_out_sib))
        .astype(bf16)
        .reshape(tok, heads, DV)
    )
    grad_value = jnp.einsum("thc,thv->chv", o_latent, back_heads, preferred_element_type=f32)
    back_olatent = jnp.einsum(
        "thv,chv->thc", back_heads, w_value, preferred_element_type=f32
    ).astype(bf16)
    probs_back = jnp.exp(score_block() - log_total)
    back_probs = jnp.einsum(
        "thc,kc->htk", back_olatent, window[:, :LATENT], preferred_element_type=f32
    )
    row_delta = jnp.sum(probs_back * back_probs, axis=2, keepdims=True)
    back_scores = (probs_back * (back_probs - row_delta) * score_scale).astype(bf16)
    back_qfull = jnp.einsum("htk,kc->thc", back_scores, window, preferred_element_type=f32)
    value_part = jnp.einsum(
        "htk,thc->kc", probs_back.astype(bf16), back_olatent, preferred_element_type=f32
    )
    back_window = jnp.einsum("htk,thc->kc", back_scores, q_full, preferred_element_type=f32)
    back_window = back_window + jnp.pad(value_part, ((0, 0), (0, QR)))
    back_blocks = back_window.reshape(9, tok, LATENT + QR)
    from_sib = swapped(back_blocks[5:].astype(bf16), "core").astype(f32)
    pad_block = jnp.zeros((1, tok, LATENT + QR), f32)
    from_sib = jnp.where(
        core == 0,
        jnp.concatenate([pad_block, from_sib], axis=0),
        jnp.concatenate([from_sib, pad_block], axis=0),
    )
    chip_blocks = back_blocks[:5] + from_sib
    back_latent = chip_blocks[4]
    for index, k in enumerate((4, 3, 2, 1)):
        back_latent = back_latent + chip_shift(chip_blocks[index].astype(bf16), -k).astype(f32)

    back_qlatent = back_qfull[:, :, :LATENT].astype(bf16)
    back_qrope = rotate(back_qfull[:, :, LATENT:], cosine[:, None, :], -sine_tab[:, None, :])
    grad_key = jnp.einsum("thc,thn->chn", back_qlatent, q_nope, preferred_element_type=f32)
    back_qnope = jnp.einsum("thc,chn->thn", back_qlatent, w_key, preferred_element_type=f32)
    back_queries = (
        jnp.concatenate([back_qnope, back_qrope], axis=2)
        .reshape(tok, heads * (QN + QR))
        .astype(bf16)
    )
    grad_expand = jnp.concatenate([grad_key, grad_value], axis=2).reshape(
        LATENT, heads * (QN + DV)
    )

    back_raw, grad_gain_mid = rms_backward(
        latent_raw, inverse_mid, gain_mid, back_latent[:, :LATENT]
    )
    back_kvpre = jnp.concatenate(
        [back_raw, rotate(back_latent[:, LATENT:], cosine, -sine_tab)], axis=1
    ).astype(bf16)
    back_both = jnp.concatenate(
        [back_queries, back_kvpre, jnp.zeros((tok, 64), bf16)], axis=1
    )
    back_one = pair_sum(
        jnp.concatenate([matmul_nt(back_both, own_a), matmul_nt(back_both, sib_a)], axis=1),
        "tensor",
    )
    back_innorm, grad_gain_one = rms_backward(inputs, inverse_one, gain_one, back_one)
    input_grad = unpermute(back_mid + back_innorm)

    h_one_pair = both_cores(h_one[:, :half], swapped(h_one[:, half:], "core"))
    attn_pair = both_cores(back_attn[:, :half], swapped(back_attn[:, half:], "core"))
    heads_pair = both_cores(o_heads, swapped(o_heads, "core"))
    back_pair = both_cores(back_both[:, :2112], swapped(back_both[:, :2112], "core"))
    rows_ql = matmul_tn(h_one_pair, back_pair)
    rows_out = matmul_tn(attn_pair, heads_pair)
    expand_low = matmul_tn(perm_l, grad_expand.astype(bf16)).astype(bf16)
    rows_expand = expand_low[:256].astype(f32) + swapped(expand_low[256:], "core").astype(f32)
    rows_expand = rows_expand.reshape(1024, 512)
    mid_low = matmul_nt(perm_m, grad_gain_mid.astype(bf16)[None, :])
    gain_cols = jnp.concatenate([grad_gain_one[:, None], grad_gain_two[:, None], mid_low], axis=1)
    gain_low = gain_cols.astype(bf16)
    rows_gain = gain_low[:half].astype(f32) + swapped(gain_low[half:], "core").astype(f32)
    attn_rows = jnp.concatenate(
        [rows_ql, jnp.pad(rows_gain, ((0, 0), (0, 61))), rows_expand, rows_out], axis=1
    ).astype(bf16)
    attn_grads = scatter_rows(attn_rows, dp)
    latent_gain = attn_grads[:, 1536:2176]
    replicated = latent_gain.at[:, 577].multiply(0.5).at[:, 576].multiply(0.5)
    replicated = pair_sum(replicated, "tensor")

    return (
        output.astype(bf16),
        input_grad,
        replicated[:, 576],
        attn_grads[:, :1536],
        replicated[:, :576],
        replicated[:8, 578],
        attn_grads[:, 2176:2688].reshape(8, 2048),
        attn_grads[:, 2688:].T,
        replicated[:, 577],
        shared_grads[:, :fs],
        shared_grads[:, fs : 2 * fs],
        shared_grads[:, 2 * fs :].T,
        expert_grads[0][None],
        expert_grads[1][None],
        expert_grads[2][None],
    )


def solution(mesh):
    fine = Mesh(
        mesh.devices.reshape(2, 4, 4, 2, 2), ("dp", "y", "z", "core", "tensor")
    )
    rows = ("dp", "y", "z", "core")
    placed = (
        P(rows, None),
        P(rows),
        P(rows, "tensor"),
        P(rows, None),
        P(rows),
        P(rows, "tensor"),
        P("tensor", rows),
        P(rows),
        P(rows, "tensor"),
        P(rows, "tensor"),
        P("tensor", rows),
        P(EXPERT, None, "tensor"),
        P(EXPERT, None, "tensor"),
        P(EXPERT, "tensor", None),
        P(),
        P(rows, None),
        P(rows, None),
        P(rows, None),
    )
    return jax.shard_map(
        shards,
        mesh=fine,
        in_specs=placed,
        out_specs=(
            P(rows, None),
            P(rows, None),
            P(rows),
            P(rows, "tensor"),
            P(rows, None),
            P(rows),
            P(rows, "tensor"),
            P("tensor", rows),
            P(rows),
            P(rows, "tensor"),
            P(rows, "tensor"),
            P("tensor", rows),
            P(EXPERT, None, "tensor"),
            P(EXPERT, None, "tensor"),
            P(EXPERT, "tensor", None),
        ),
        check_vma=False,
    )
```

time: 3610 us -> 901 us (0.25)
  waiting for transfers between devices: 2680 us -> 438 us
  blocking collectives: 430 us -> 0 us
  local copies, waits for them, and re-layouts: 172 us -> 66.2 us
  matrix products: 179 us -> 230 us
    reduce_scatter x7 -> x2, waiting for transfers between devices: 1780 us -> 0.01 us  [scatter_rows(): lax.psum_scatter(partial_rows, PLANE, scatter_dimension=0, tiled=True)]
    unnamed x2 -> x0, blocking collectives: 430 us -> none
    psum x4 -> x0, waiting for transfers between devices: 299 us -> none  [the longest x1 194 us: shards(): lax.psum(expert_gate_weight_gradient.astype(jnp.bfloat16), 'dp')]
    all_gather x7 -> x3, waiting for transfers between devices: 389 us -> 93.7 us  [gather_plane(): mine = lax.all_gather(pair, PLANE, axis=0, tiled=True)]
    ppermute x16 -> x35, waiting for transfers between devices: 6.35 us -> 218 us  [the longest x27 197 us: swapped(): return lax.ppermute(block, axis, [(0, 1), (1, 0)])]
    all_to_all x4, waiting for transfers between devices: 195 us -> 126 us  [exchange(): lax.all_to_all(blocks, EXPERT, split_axis=0, concat_axis=0, tiled=True)]
    reshape x11 -> x6, local copies, waits for them, and re-layouts: 59.5 us -> 11.7 us  [the longest x2 4.78 us: shards(): rows_expand = rows_expand.reshape(1024, 512)]
    gather x4 -> x0, local copies, waits for them, and re-layouts: 37.6 us -> none  [the longest x1 11.2 us: shards(): grad_send = padded_grads[slot_owner].reshape(expert_count, capacity, D)]
  transfers between devices with their start and end apart: 38 -> 44, of which waited for: 20 -> 24; matrix products, arithmetic and copies ran while one was open for 10% -> 35% of each run, Pallas kernels for 0% -> 0%
where the time goes in v1:
time: 901 us; the launch traced here: 888 us
  waiting for transfers between devices  438 us (49%)
  matrix products  230 us (26%)
  starting transfers between devices  72.2 us (8%)
  local copies, waits for them, and re-layouts  66.2 us (7%)
  other arithmetic  65.4 us (7%)
  between operations  16 us (2%)
    ppermute x27, waiting for transfers between devices, swapped(): return lax.ppermute(block, axis, [(0, 1), (1, 0)])  197 us
    all_to_all x4, waiting for transfers between devices, exchange(): lax.all_to_all(blocks, EXPERT, split_axis=0, concat_axis=0, tiled=True)  126 us
    all_gather x3, waiting for transfers between devices, gather_plane(): mine = lax.all_gather(pair, PLANE, axis=0, tiled=True)  93.7 us
    dot_general x20, matrix products, matmul(): return jnp.dot(left_op, right_op, preferred_element_type=f32)  76.9 us
    dot_general x20, matrix products, matmul_nt(): lax.dot_general(left_op, right_op, (((1,), (1,)), ((), ())), preferred_el...  73.4 us
    dot_general x10, matrix products, matmul_tn(): lax.dot_general(left_op, right_op, (((0,), (0,)), ((), ())), preferred_el...  36.9 us
    ppermute x27, starting transfers between devices, swapped(): return lax.ppermute(block, axis, [(0, 1), (1, 0)])  29.3 us
    all_to_all x4, starting transfers between devices, exchange(): lax.all_to_all(blocks, EXPERT, split_axis=0, concat_axis=0, tiled=True)  25.2 us
  transfers between devices with their start and end apart: 44, of which 24 were waited for; matrix products, arithmetic and copies ran while one was open for 35% of the time, Pallas kernels for 0%

profile of v1, /device:TPU:0, one launch (start us, length us, event | category | flops | bytes accessed | tf_op | source)
XLA Modules:
  0.0 888.2 jit_solution(12547207173039851816)
XLA Ops:
  11.6 3.7 collective-permute-done.2
  28.4 43.5 %all-gather.6.cloned.1.call-done = bf16[1024,2176]{1,0:T(8,128)(2,1)} async-done(((bf16[64,2176]{1,0:T(8,128)(2,1)}), bf16[1024,2176]{1,0:T(8,128)(2,1)}) %all-gather.6.cloned.1.call-update) | async-done | bytes 4456464 | tf_op jit(solution)/shard_map/all_gather | solution.py:104
  72.1 50.2 %all-gather.4.cloned.1.call-done = bf16[1024,1536]{1,0:T(8,128)(2,1)} async-done(((bf16[64,1536]{1,0:T(8,128)(2,1)}), bf16[1024,1536]{1,0:T(8,128)(2,1)}) %all-gather.4.cloned.1.call-update) | async-done | bytes 3145744 | tf_op jit(solution)/shard_map/all_gather | solution.py:104
  122.4 5.2 multiply_reduce_fusion.5
  136.6 4.4 reshape.663
  141.0 3.1 convolution_convert_fusion.9
  147.2 4.2 fusion.284
  157.9 3.4 collective-permute-start.5
  161.3 3.5 collective-permute-start.6
  168.9 3.2 collective-permute-done.6
  172.8 5.2 collective-permute-done.7
  194.5 3.8 fusion.297
  213.7 11.6 %collective-permute-done.9 = bf16[128,2048]{1,0:T(8,128)(2,1)} collective-permute-done((bf16[128,2048]{1,0:T(8,128)(2,1)}, bf16[128,2048]{1,0:T(8,128)(2,1)}, u32[]{:S(2)}, u32[]{:S(2)}) %collective-permute-start.9) | collective-permute-done | bytes 524320 | tf_op jit(solution)/shard_map/ppermute | solution.py:26
  229.1 7.9 convolution_convert_fusion.4
  237.0 7.1 all-to-all-start
  246.9 3.2 add_convert_fusion.1
  250.1 46.7 %all-to-all-done = bf16[32,32,2048]{2,1,0:T(8,128)(2,1)} async-done(((bf16[32,32,2048]{2,1,0:T(8,128)(2,1)}), bf16[32,32,2048]{2,1,0:T(8,128)(2,1)}, u32[]{:S(2)}, u32[]{:S(2)}) %all-to-all-start) | async-done | bytes 4194336 | tf_op jit(solution)/shard_map/all_to_all | solution.py:209
  296.8 6.6 all-to-all-start.1
  303.8 8.0 fusion.58
  311.7 7.0 fusion.54
  318.8 37.5 %all-to-all-done.1 = bf16[32,32,2048]{2,1,0:T(8,128)(2,1)} async-done(((bf16[32,32,2048]{2,1,0:T(8,128)(2,1)}), bf16[32,32,2048]{2,1,0:T(8,128)(2,1)}, u32[]{:S(2)}, u32[]{:S(2)}) %all-to-all-start.1) | async-done | bytes 4194336 | tf_op jit(solution)/shard_map/all_to_all | solution.py:209
  356.2 8.7 multiply_convert_fusion
  364.9 3.5 fusion.56
  368.5 5.3 add_convert_fusion
  373.9 6.6 all-to-all-start.2
  380.5 5.5 fusion.298
  386.1 5.5 convolution_convert_fusion.3
  391.5 41.7 %all-to-all-done.2 = bf16[32,32,2048]{2,1,0:T(8,128)(2,1)} async-done(((bf16[32,32,2048]{2,1,0:T(8,128)(2,1)}), bf16[32,32,2048]{2,1,0:T(8,128)(2,1)}, u32[]{:S(2)}, u32[]{:S(2)}) %all-to-all-start.2) | async-done | bytes 4194336 | tf_op jit(solution)/shard_map/all_to_all | solution.py:209
  433.3 3.8 fusion.28
  437.1 4.3 fusion.45
  445.4 4.9 fusion.26
  453.1 6.7 fusion.83
  464.4 10.5 %collective-permute-done.13 = bf16[128,2048]{1,0:T(8,128)(2,1)S(1)} collective-permute-done((bf16[128,2048]{1,0:T(8,128)(2,1)S(1)}, bf16[128,2048]{1,0:T(8,128)(2,1)S(1)}, u32[]{:S(2)}, u32[]{:S(2)}) %collective-permute-start.13) | collective-permute-done | bytes 524320 | tf_op jit(solution)/shard_map/ppermute | solution.py:26
  481.8 5.0 fusion.139
  489.8 11.0 %fusion.105 = f32[128,8,576]{0,2,1:T(8,128)} fusion(bf16[1152,576,1]{1,0,2:T(8,128)(2,1)} %bitcast.259, f32[1152,128,8]{1,0,2:T(8,128)} %fusion.139, f32[8,128,1152]{1,2,0:T(8,128)} %copy-done.16, f32[8,128]{1,0:T(8,128)S(1)} %log_add_fusion), kind=kOutput, calls=%fused_computation.138 | convolution fusion | flops 1367214208 | bytes 13127680 | tf_op jit(solution)/shard_map/htk,kc->thc/dot_general | solution.py:371
  500.8 11.2 %fusion.49 = f32[1152,576]{0,1:T(8,128)} fusion(f32[1152,512]{0,1:T(8,128)} %convolution_bitcast_fusion.1, f32[1152,128,8]{1,0,2:T(8,128)} %fusion.139, f32[8,128,1152]{1,2,0:T(8,128)} %copy-done.16, f32[8,128]{1,0:T(8,128)S(1)} %log_add_fusion, bf16[128,8,32]{0,2,1:T(8,128)(2,1)S(1)} %copy-done.59, bf16[128,8,32]{0,2,1:T(8,128)(2,1)S(1)} %copy-done.58, ...), kind=kOutput, calls=%fused_computation.68 | convolution fusion | flops 1371416704 | bytes 15634432 | tf_op jit(solution)/shard_map/htk,thc->kc/dot_general | solution.py:375
  524.0 3.2 copy.280
  537.8 3.1 convolution_convert_fusion.11
  541.0 4.3 collective-permute-done.18
  548.9 4.8 collective-permute-done.15
  556.5 3.8 convolution_convert_fusion.18
  567.3 9.1 %collective-permute-done.19 = bf16[128,2048]{1,0:T(8,128)(2,1)S(1)} collective-permute-done((bf16[128,2048]{1,0:T(8,128)(2,1)S(1)}, bf16[128,2048]{1,0:T(8,128)(2,1)S(1)}, u32[]{:S(2)}, u32[]{:S(2)}) %collective-permute-start.19) | collective-permute-done | bytes 524320 | tf_op jit(solution)/shard_map/ppermute | solution.py:26
  587.1 4.0 fusion.25
  591.1 10.1 %copy.303 = bf16[1024,3712]{1,0:T(8,128)(2,1)} copy(bf16[1024,3712]{0,1:T(8,128)(2,1)} %fusion.25) | data formatting | bytes 15204352
  609.1 3.8 pad_maximum_fusion
  613.0 7.5 convolution_convert_fusion.6
  621.9 6.9 convolution_convert_fusion.5
  629.2 6.7 convolution_convert_fusion.7
  637.6 4.9 all-to-all-start.3
  643.9 4.6 fusion.8
  648.5 37.6 %collective-permute-done.32 = bf16[2048,704]{0,1:T(8,128)(2,1)} collective-permute-done((bf16[2048,704]{0,1:T(8,128)(2,1)}, bf16[2048,704]{0,1:T(8,128)(2,1)}, u32[]{:S(2)}, u32[]{:S(2)}) %collective-permute-start.32) | collective-permute-done | bytes 2883616 | tf_op jit(solution)/shard_map/ppermute | solution.py:26
  686.1 6.4 add_bitcast_fusion.2
  692.5 55.4 %collective-permute-done.33 = bf16[2048,704]{0,1:T(8,128)(2,1)} collective-permute-done((bf16[2048,704]{0,1:T(8,128)(2,1)}, bf16[2048,704]{0,1:T(8,128)(2,1)}, u32[]{:S(2)}, u32[]{:S(2)}) %collective-permute-start.33) | collective-permute-done | bytes 2883616 | tf_op jit(solution)/shard_map/ppermute | solution.py:26
  747.9 6.5 add_bitcast_fusion.1
  754.4 54.5 %collective-permute-done.34 = bf16[704,2048]{1,0:T(8,128)(2,1)} collective-permute-done((bf16[704,2048]{1,0:T(8,128)(2,1)}, bf16[704,2048]{1,0:T(8,128)(2,1)}, u32[]{:S(2)}, u32[]{:S(2)}) %collective-permute-start.34) | collective-permute-done | bytes 2883616 | tf_op jit(solution)/shard_map/ppermute | solution.py:26
  808.9 6.5 add_bitcast_fusion
  822.0 4.6 fusion.6
  829.7 3.1 fusion.80
  832.8 4.0 fusion.82
  840.4 4.6 fusion.1
  845.1 6.5 collective-permute-done.12
  851.6 4.6 fusion.81
  859.0 6.3 fusion.77
  874.8 4.6 collective-permute-done.31
  (454 shorter events, 186.8 us)
Async XLA Ops:
  7.2 349.1 %copy-start = (bf16[1,704,2048]{2,1,0:T(8,128)(2,1)S(1)}, bf16[1,704,2048]{2,1,0:T(8,128)(2,1)}, u32[]{:S(2)}) copy-start(bf16[1,704,2048]{2,1,0:T(8,128)(2,1)} %param.35) | copy-start | bytes 8650756
  7.2 21.2 %copy-start.65 = (s32[8192]{0:T(1024)S(1)}, s32[8192]{0:T(1024)}, u32[]{:S(2)}) copy-start(s32[8192]{0:T(1024)} %param.36) | copy-start | bytes 98308
  7.2 64.6 %all-gather.6.cloned.1.call-start = ((), (), s32[]{:S(2)}) async-start(), calls=%async_computation.7 | async-start | bytes 4734976 | tf_op jit(solution)/shard_map/all_gather | solution.py:104
  10.0 5.3 collective-permute-start.2
  16.1 106.2 %all-gather.4.cloned.1.call-start = ((), (), s32[]{:S(2)}) async-start(), calls=%async_computation.6 | async-start | bytes 3342336 | tf_op jit(solution)/shard_map/all_gather | solution.py:104
  17.8 4.6 collective-permute-start
  24.0 279.5 %all-gather.8.cloned.1.call-start = ((), (), s32[]{:S(2)}) async-start(), calls=%async_computation.8 | async-start | bytes 9191424 | tf_op jit(solution)/shard_map/all_gather | solution.py:104
  24.8 104.6 %collective-permute-start.10 = (bf16[32,4224]{1,0:T(8,128)(2,1)}, bf16[32,4224]{1,0:T(8,128)(2,1)}, u32[]{:S(2)}, u32[]{:S(2)}) collective-permute-start(bf16[32,4224]{1,0:T(8,128)(2,1)} %pad_maximum_fusion.18), channel_id=1, source_target_pairs={{0,64},{64,0},{1,65},{65,1},{2,66},{66,2},{3,67},{67,3},{4,68},{68... | collective-permute-start | bytes 811016 | tf_op jit(solution)/shard_map/ppermute | solution.py:26
  27.2 113.8 %copy-start.83 = (s32[512]{0:T(512)}, s32[512]{0:T(512)S(1)}, u32[]{:S(2)}) copy-start(s32[512]{0:T(512)S(1)} %fusion.247) | copy-start | bytes 6148
  27.8 99.8 %copy-start.66 = (s32[2048]{0:T(1024)}, s32[2048]{0:T(1024)S(1)}, u32[]{:S(2)}) copy-start(s32[2048]{0:T(1024)S(1)} %fusion.226) | copy-start | bytes 24580
  71.9 73.0 %collective-permute-start.3 = (bf16[1024,2176]{1,0:T(8,128)(2,1)}, bf16[1024,2176]{1,0:T(8,128)(2,1)}, u32[]{:S(2)}, u32[]{:S(2)}) collective-permute-start(bf16[1024,2176]{1,0:T(8,128)(2,1)} %all-gather.6.cloned.1.call-done), channel_id=1, source_target_pairs={{0,2},{2,0},{1,3},{3,1},{4,6},{6,4},{5,7},{7,5},{8,10},{10,8},{9,1... | collective-permute-start | bytes 13369352 | tf_op jit(solution)/shard_map/ppermute | solution.py:26
  122.3 11.5 %collective-permute-start.1 = (bf16[1024,1536]{1,0:T(8,128)(2,1)}, bf16[1024,1536]{1,0:T(8,128)(2,1)}, u32[]{:S(2)}, u32[]{:S(2)}) collective-permute-start(bf16[1024,1536]{1,0:T(8,128)(2,1)} %all-gather.4.cloned.1.call-done), channel_id=1, source_target_pairs={{0,2},{2,0},{1,3},{3,1},{4,6},{6,4},{5,7},{7,5},{8,10},{10,8},{9,1... | collective-permute-start | bytes 9437192 | tf_op jit(solution)/shard_map/ppermute | solution.py:26
  153.3 26.1 %copy-start.6 = (f32[128,2176]{0,1:T(8,128)}, f32[128,2176]{0,1:T(8,128)S(1)}, u32[]{:S(2)}) copy-start(f32[128,2176]{0,1:T(8,128)S(1)} %convolution_add_fusion) | copy-start | bytes 3342340
  153.4 26.8 %copy-start.70 = (f32[128]{0:T(128)}, f32[128]{0:T(128)S(1)}, u32[]{:S(2)}) copy-start(f32[128]{0:T(128)S(1)} %add_rsqrt_fusion.1) | copy-start | bytes 1540
  154.4 27.8 %copy-start.61 = (f32[1,512]{1,0:T(1,128)}, f32[1,512]{1,0:T(1,128)S(1)}, u32[]{:S(2)}) copy-start(f32[1,512]{1,0:T(1,128)S(1)} %fusion.41) | copy-start | bytes 6148
  155.3 12.2 %collective-permute-start.4 = (bf16[128,576]{0,1:T(8,128)(2,1)S(1)}, bf16[128,576]{0,1:T(8,128)(2,1)S(1)}, u32[]{:S(2)}, u32[]{:S(2)}) collective-permute-start(bf16[128,576]{0,1:T(8,128)(2,1)S(1)} %pad_maximum_fusion.20), channel_id=1, source_target_pairs={{0,16},{4,20},{8,24},{12,28},{16,32},{20,36},{24,40},{28,44},{32,4... | collective-permute-start | bytes 442376 | tf_op jit(solution)/shard_map/ppermute | solution.py:32
  157.9 10.4 %collective-permute-start.5 = (bf16[128,576]{0,1:T(8,128)(2,1)S(1)}, bf16[128,576]{0,1:T(8,128)(2,1)S(1)}, u32[]{:S(2)}, u32[]{:S(2)}) collective-permute-start(bf16[128,576]{0,1:T(8,128)(2,1)S(1)} %pad_maximum_fusion.20), channel_id=1, source_target_pairs={{0,12},{4,16},{8,20},{12,24},{16,28},{20,32},{24,36},{28,40},{32,4... | collective-permute-start | bytes 442376 | tf_op jit(solution)/shard_map/ppermute | solution.py:32
  161.3 10.8 %collective-permute-start.6 = (bf16[128,576]{0,1:T(8,128)(2,1)S(1)}, bf16[128,576]{0,1:T(8,128)(2,1)S(1)}, u32[]{:S(2)}, u32[]{:S(2)}) collective-permute-start(bf16[128,576]{0,1:T(8,128)(2,1)S(1)} %pad_maximum_fusion.20), channel_id=1, source_target_pairs={{0,8},{4,12},{8,16},{12,20},{16,24},{20,28},{24,32},{28,36},{32,40... | collective-permute-start | bytes 442376 | tf_op jit(solution)/shard_map/ppermute | solution.py:32
  164.8 13.2 %collective-permute-start.7 = (bf16[128,576]{0,1:T(8,128)(2,1)S(1)}, bf16[128,576]{0,1:T(8,128)(2,1)S(1)}, u32[]{:S(2)}, u32[]{:S(2)}) collective-permute-start(bf16[128,576]{0,1:T(8,128)(2,1)S(1)} %pad_maximum_fusion.20), channel_id=1, source_target_pairs={{0,4},{4,8},{8,12},{12,16},{16,20},{20,24},{24,28},{28,32},{32,36}... | collective-permute-start | bytes 442376 | tf_op jit(solution)/shard_map/ppermute | solution.py:32
  180.2 9.8 %collective-permute-start.8 = (bf16[4,128,576]{1,2,0:T(8,128)(2,1)}, bf16[4,128,576]{1,2,0:T(8,128)(2,1)}, u32[]{:S(2)}, u32[]{:S(2)}) collective-permute-start(bf16[4,128,576]{1,2,0:T(8,128)(2,1)} %constant_dynamic-slice_fusion.1), channel_id=1, source_target_pairs={{0,2},{2,0},{1,3},{3,1},{4,6},{6,4},{5,7},{7,5},{8,10},{10,8},{9,1... | collective-permute-start | bytes 1769480 | tf_op jit(solution)/shard_map/ppermute | solution.py:26
  208.3 19.8 %copy-start.57 = (f32[1,2048]{1,0:T(1,128)S(1)}, f32[1,2048]{1,0:T(1,128)}, u32[]{:S(2)}) copy-start(f32[1,2048]{1,0:T(1,128)} %get-tuple-element.112) | copy-start | bytes 24580
  208.3 20.8 %copy-start.67 = (s32[2048]{0:T(1024)S(1)}, s32[2048]{0:T(1024)}, u32[]{:S(2)}) copy-start(s32[2048]{0:T(1024)} %copy-done.66) | copy-start | bytes 24580
  209.1 16.1 %collective-permute-start.9 = (bf16[128,2048]{1,0:T(8,128)(2,1)}, bf16[128,2048]{1,0:T(8,128)(2,1)}, u32[]{:S(2)}, u32[]{:S(2)}) collective-permute-start(bf16[128,2048]{1,0:T(8,128)(2,1)} %pad_maximum_fusion.10), channel_id=1, source_target_pairs={{0,1},{1,0},{2,3},{3,2},{4,5},{5,4},{6,7},{7,6},{8,9},{9,8},{10,11... | collective-permute-start | bytes 1572872 | tf_op jit(solution)/shard_map/ppermute | solution.py:26
  212.7 31.6 %copy-start.42 = (f32[128,32]{0,1:T(8,128)}, f32[128,32]{0,1:T(8,128)S(1)}, u32[]{:S(2)}) copy-start(f32[128,32]{0,1:T(8,128)S(1)} %get-tuple-element.51) | copy-start | bytes 49156
  212.8 31.5 %copy-start.38 = (f32[32,128]{1,0:T(8,128)}, f32[32,128]{1,0:T(8,128)S(1)}, u32[]{:S(2)}) copy-start(f32[32,128]{1,0:T(8,128)S(1)} %convolution_select_fusion) | copy-start | bytes 49156
  237.0 59.9 %all-to-all-start = ((bf16[32,32,2048]{2,1,0:T(8,128)(2,1)}), bf16[32,32,2048]{2,1,0:T(8,128)(2,1)}, u32[]{:S(2)}, u32[]{:S(2)}) async-start(bf16[32,32,2048]{2,1,0:T(8,128)(2,1)} %bitcast.264), calls=%async_computation | async-start | bytes 8388608 | tf_op jit(solution)/shard_map/all_to_all | solution.py:209
  296.8 59.4 %all-to-all-start.1 = ((bf16[32,32,2048]{2,1,0:T(8,128)(2,1)}), bf16[32,32,2048]{2,1,0:T(8,128)(2,1)}, u32[]{:S(2)}, u32[]{:S(2)}) async-start(bf16[32,32,2048]{2,1,0:T(8,128)(2,1)} %bitcast.251), calls=%async_computation.1 | async-start | bytes 8388608 | tf_op jit(solution)/shard_map/all_to_all | solution.py:209
  303.5 129.8 %collective-permute-start.11 = (bf16[1024,4224]{1,0:T(8,128)(2,1)}, bf16[1024,4224]{1,0:T(8,128)(2,1)}, u32[]{:S(2)}, u32[]{:S(2)}) collective-permute-start(bf16[1024,4224]{1,0:T(8,128)(2,1)} %all-gather.8.cloned.1.call-done), channel_id=1, source_target_pairs={{0,2},{2,0},{1,3},{3,1},{4,6},{6,4},{5,7},{7,5},{8,10},{10,8},{9,1... | collective-permute-start | bytes 25952264 | tf_op jit(solution)/shard_map/ppermute | solution.py:26
  373.9 59.4 %all-to-all-start.2 = ((bf16[32,32,2048]{2,1,0:T(8,128)(2,1)}), bf16[32,32,2048]{2,1,0:T(8,128)(2,1)}, u32[]{:S(2)}, u32[]{:S(2)}) async-start(bf16[32,32,2048]{2,1,0:T(8,128)(2,1)} %bitcast.265), calls=%async_computation.2 | async-start | bytes 8388608 | tf_op jit(solution)/shard_map/all_to_all | solution.py:209
  380.5 475.8 %reduce-scatter.7.cloned.1.call-start = ((), (), s32[]{:S(2)}) async-start(), calls=%async_computation.10 | async-start | bytes 8077312 | tf_op jit(solution)/shard_map/reduce_scatter | solution.py:109
  453.1 21.8 %copy-start.5 = (f32[128,2048]{1,0:T(8,128)S(1)}, f32[128,2048]{1,0:T(8,128)}, u32[]{:S(2)}) copy-start(f32[128,2048]{1,0:T(8,128)} %copy-done.4) | copy-start | bytes 3145732
  459.8 15.0 %collective-permute-start.13 = (bf16[128,2048]{1,0:T(8,128)(2,1)S(1)}, bf16[128,2048]{1,0:T(8,128)(2,1)S(1)}, u32[]{:S(2)}, u32[]{:S(2)}) collective-permute-start(bf16[128,2048]{1,0:T(8,128)(2,1)S(1)} %fusion.83), channel_id=1, source_target_pairs={{0,1},{1,0},{2,3},{3,2},{4,5},{5,4},{6,7},{7,6},{8,9},{9,8},{10,11... | collective-permute-start | bytes 1572872 | tf_op jit(solution)/shard_map/ppermute | solution.py:26
  463.7 120.8 %collective-permute-start.20 = (bf16[128,1024]{1,0:T(8,128)(2,1)}, bf16[128,1024]{1,0:T(8,128)(2,1)}, u32[]{:S(2)}, u32[]{:S(2)}) collective-permute-start(bf16[128,1024]{1,0:T(8,128)(2,1)} %get-tuple-element.95), channel_id=1, source_target_pairs={{0,2},{2,0},{1,3},{3,1},{4,6},{6,4},{5,7},{7,5},{8,10},{10,8},{9,1... | collective-permute-start | bytes 786440 | tf_op jit(solution)/shard_map/ppermute | solution.py:26
  463.7 71.5 %collective-permute-start.25 = (bf16[128,1024]{0,1:T(8,128)(2,1)}, bf16[128,1024]{0,1:T(8,128)(2,1)}, u32[]{:S(2)}, u32[]{:S(2)}) collective-permute-start(bf16[128,1024]{0,1:T(8,128)(2,1)} %bitcast.26), channel_id=1, source_target_pairs={{0,2},{2,0},{1,3},{3,1},{4,6},{6,4},{5,7},{7,5},{8,10},{10,8},{9,1... | collective-permute-start | bytes 786440 | tf_op jit(solution)/shard_map/ppermute | solution.py:26
  527.3 4.6 collective-permute-start.14
  527.3 9.2 %collective-permute-start.24 = (bf16[128,1024]{1,0:T(8,128)(2,1)}, bf16[128,1024]{1,0:T(8,128)(2,1)S(1)}, u32[]{:S(2)}, u32[]{:S(2)}) collective-permute-start(bf16[128,1024]{1,0:T(8,128)(2,1)} %get-tuple-element.97), channel_id=1, source_target_pairs={{0,2},{2,0},{1,3},{3,1},{4,6},{6,4},{5,7},{7,5},{8,10},{10,8},{9,1... | collective-permute-start | bytes 786440 | tf_op jit(solution)/shard_map/ppermute | solution.py:26
  532.0 28.3 %slice-start.2 = ((s8[4456448]{0:T(1024)(128)(4,1)}), s8[4194304]{0:T(1024)(128)(4,1)S(1)}, s32[]{:S(2)}) async-start(s8[4456448]{0:T(1024)(128)(4,1)} %bitcast.249), calls=%async_computation.13 | async-start | bytes 8388608
  532.3 21.6 %copy-start.62 = (f32[1,512]{1,0:T(1,128)S(1)}, f32[1,512]{1,0:T(1,128)}, u32[]{:S(2)}) copy-start(f32[1,512]{1,0:T(1,128)} %copy-done.61) | copy-start | bytes 6148
  532.3 21.6 %copy-start.71 = (f32[128]{0:T(128)S(1)}, f32[128]{0:T(128)}, u32[]{:S(2)}) copy-start(f32[128]{0:T(128)} %copy-done.70) | copy-start | bytes 1540
  532.3 23.8 %copy-start.73 = (f32[32]{0:T(128)S(1)}, f32[32]{0:T(128)}, u32[]{:S(2)}) copy-start(f32[32]{0:T(128)} %multiply_exponential_fusion) | copy-start | bytes 388
  532.3 23.8 %copy-start.75 = (f32[128]{0:T(128)S(1)}, f32[128]{0:T(128)}, u32[]{:S(2)}) copy-start(f32[128]{0:T(128)} %fusion.277) | copy-start | bytes 1540
  532.4 12.9 %collective-permute-start.18 = (bf16[128,576]{0,1:T(8,128)(2,1)S(1)}, bf16[128,576]{0,1:T(8,128)(2,1)S(1)}, u32[]{:S(2)}, u32[]{:S(2)}) collective-permute-start(bf16[128,576]{0,1:T(8,128)(2,1)S(1)} %get-tuple-element.82), channel_id=1, source_target_pairs={{4,0},{8,4},{12,8},{16,12},{20,16},{24,20},{28,24},{32,28},{36,32}... | collective-permute-start | bytes 442376 | tf_op jit(solution)/shard_map/ppermute | solution.py:32
  533.9 11.9 %collective-permute-start.17 = (bf16[128,576]{0,1:T(8,128)(2,1)S(1)}, bf16[128,576]{0,1:T(8,128)(2,1)S(1)}, u32[]{:S(2)}, u32[]{:S(2)}) collective-permute-start(bf16[128,576]{0,1:T(8,128)(2,1)S(1)} %get-tuple-element.83), channel_id=1, source_target_pairs={{8,0},{12,4},{16,8},{20,12},{24,16},{28,20},{32,24},{36,28},{40,32... | collective-permute-start | bytes 442376 | tf_op jit(solution)/shard_map/ppermute | solution.py:32
  535.2 13.7 %collective-permute-start.16 = (bf16[128,576]{0,1:T(8,128)(2,1)S(1)}, bf16[128,576]{0,1:T(8,128)(2,1)S(1)}, u32[]{:S(2)}, u32[]{:S(2)}) collective-permute-start(bf16[128,576]{0,1:T(8,128)(2,1)S(1)} %get-tuple-element.84), channel_id=1, source_target_pairs={{12,0},{16,4},{20,8},{24,12},{28,16},{32,20},{36,24},{40,28},{44,3... | collective-permute-start | bytes 442376 | tf_op jit(solution)/shard_map/ppermute | solution.py:32
  536.5 17.2 %collective-permute-start.15 = (bf16[128,576]{0,1:T(8,128)(2,1)S(1)}, bf16[128,576]{0,1:T(8,128)(2,1)S(1)}, u32[]{:S(2)}, u32[]{:S(2)}) collective-permute-start(bf16[128,576]{0,1:T(8,128)(2,1)S(1)} %get-tuple-element.81), channel_id=1, source_target_pairs={{16,0},{20,4},{24,8},{28,12},{32,16},{36,20},{40,24},{44,28},{48,3... | collective-permute-start | bytes 442376 | tf_op jit(solution)/shard_map/ppermute | solution.py:32
  537.8 22.6 %slice-start.3 = ((s8[4456448]{0:T(1024)(128)(4,1)}), s8[262144]{0:T(1024)(128)(4,1)S(1)}, s32[]{:S(2)}) async-start(s8[4456448]{0:T(1024)(128)(4,1)} %bitcast.249), calls=%async_computation.14 | async-start | bytes 524288
  545.2 33.0 %collective-permute-start.23 = (bf16[256,2048]{1,0:T(8,128)(2,1)S(1)}, bf16[256,2048]{1,0:T(8,128)(2,1)S(1)}, u32[]{:S(2)}, u32[]{:S(2)}) collective-permute-start(bf16[256,2048]{1,0:T(8,128)(2,1)S(1)} %slice.384), channel_id=1, source_target_pairs={{0,2},{2,0},{1,3},{3,1},{4,6},{6,4},{5,7},{7,5},{8,10},{10,8},{9,1... | collective-permute-start | bytes 3145736 | tf_op jit(solution)/shard_map/ppermute | solution.py:26
  562.1 14.3 %collective-permute-start.19 = (bf16[128,2048]{1,0:T(8,128)(2,1)S(1)}, bf16[128,2048]{1,0:T(8,128)(2,1)S(1)}, u32[]{:S(2)}, u32[]{:S(2)}) collective-permute-start(bf16[128,2048]{1,0:T(8,128)(2,1)S(1)} %pad_maximum_fusion.11), channel_id=1, source_target_pairs={{0,1},{1,0},{2,3},{3,2},{4,5},{5,4},{6,7},{7,6},{8,9},{9,8},{10,11... | collective-permute-start | bytes 1572872 | tf_op jit(solution)/shard_map/ppermute | solution.py:26
  567.3 17.1 %collective-permute-start.21 = (bf16[128,2112]{0,1:T(8,128)(2,1)}, bf16[128,2112]{0,1:T(8,128)(2,1)}, u32[]{:S(2)}, u32[]{:S(2)}) collective-permute-start(bf16[128,2112]{0,1:T(8,128)(2,1)} %pad_maximum_fusion.9), channel_id=1, source_target_pairs={{0,2},{2,0},{1,3},{3,1},{4,6},{6,4},{5,7},{7,5},{8,10},{10,8},{9,1... | collective-permute-start | bytes 1622024 | tf_op jit(solution)/shard_map/ppermute | solution.py:26
  578.2 6.3 collective-permute-start.22
  601.3 270.7 %reduce-scatter.5.cloned.1.call-start = ((), (), s32[]{:S(2)}) async-start(), calls=%async_computation.9 | async-start | bytes 9191424 | tf_op jit(solution)/shard_map/reduce_scatter | solution.py:109
  602.7 2.9 collective-permute-start.29
  604.4 2.0 collective-permute-start.30
  604.9 2.5 collective-permute-start.28
  620.5 65.6 %collective-permute-start.32 = (bf16[2048,704]{0,1:T(8,128)(2,1)}, bf16[2048,704]{0,1:T(8,128)(2,1)}, u32[]{:S(2)}, u32[]{:S(2)}) collective-permute-start(bf16[2048,704]{0,1:T(8,128)(2,1)} %convolution_convert_fusion.6), channel_id=1, source_target_pairs={{0,64},{64,0},{1,65},{65,1},{2,66},{66,2},{3,67},{67,3},{4,68},{68... | collective-permute-start | bytes 8650760 | tf_op jit(solution)/shard_map/ppermute | solution.py:26
  628.8 119.1 %collective-permute-start.33 = (bf16[2048,704]{0,1:T(8,128)(2,1)}, bf16[2048,704]{0,1:T(8,128)(2,1)}, u32[]{:S(2)}, u32[]{:S(2)}) collective-permute-start(bf16[2048,704]{0,1:T(8,128)(2,1)} %convolution_convert_fusion.5), channel_id=1, source_target_pairs={{0,64},{64,0},{1,65},{65,1},{2,66},{66,2},{3,67},{67,3},{4,68},{68... | collective-permute-start | bytes 8650760 | tf_op jit(solution)/shard_map/ppermute | solution.py:26
  635.9 173.0 %collective-permute-start.34 = (bf16[704,2048]{1,0:T(8,128)(2,1)}, bf16[704,2048]{1,0:T(8,128)(2,1)}, u32[]{:S(2)}, u32[]{:S(2)}) collective-permute-start(bf16[704,2048]{1,0:T(8,128)(2,1)} %convolution_convert_fusion.7), channel_id=1, source_target_pairs={{0,64},{64,0},{1,65},{65,1},{2,66},{66,2},{3,67},{67,3},{4,68},{68... | collective-permute-start | bytes 8650760 | tf_op jit(solution)/shard_map/ppermute | solution.py:26
  637.6 189.0 %all-to-all-start.3 = ((bf16[32,32,2048]{2,1,0:T(8,128)(2,1)}), bf16[32,32,2048]{2,1,0:T(8,128)(2,1)}, u32[]{:S(2)}, u32[]{:S(2)}) async-start(bf16[32,32,2048]{2,1,0:T(8,128)(2,1)} %bitcast.263), calls=%async_computation.3 | async-start | bytes 8388608 | tf_op jit(solution)/shard_map/all_to_all | solution.py:209
  754.4 61.0 %copy-start.29 = (bf16[128,1408]{1,0:T(8,128)(2,1)S(1)}, bf16[128,1408]{1,0:T(8,128)(2,1)}, u32[]{:S(2)}) copy-start(bf16[128,1408]{1,0:T(8,128)(2,1)} %get-tuple-element.76) | copy-start | bytes 1081348
  836.8 14.8 %collective-permute-start.12 = (bf16[128,2048]{1,0:T(8,128)(2,1)S(1)}, bf16[128,2048]{1,0:T(8,128)(2,1)S(1)}, u32[]{:S(2)}, u32[]{:S(2)}) collective-permute-start(bf16[128,2048]{1,0:T(8,128)(2,1)S(1)} %fusion.82), channel_id=1, source_target_pairs={{0,1},{1,0},{2,3},{3,2},{4,5},{5,4},{6,7},{7,6},{8,9},{9,8},{10,11... | collective-permute-start | bytes 1572872 | tf_op jit(solution)/shard_map/ppermute | solution.py:26
  857.2 8.1 collective-permute-start.26
  859.0 22.3 %copy-start.1 = (bf16[1,704,2048]{2,1,0:T(8,128)(2,1)S(1)}, bf16[1,704,2048]{2,1,0:T(8,128)(2,1)}, u32[]{:S(2)}) copy-start(bf16[1,704,2048]{2,1,0:T(8,128)(2,1)} %param.35) | copy-start | bytes 8650756
  867.8 5.6 collective-permute-start.27
  872.9 6.5 collective-permute-start.31
  (89 other events, 521.2 us)
Sparse Core Ops, SparseCore 0:
  16.2 55.5 all-gather.5
  74.6 47.6 all-gather.3
  131.5 73.3 all-gather.7
  601.4 123.7 reduce-scatter.6
  728.8 84.7 reduce-scatter.4

commit v2 on v1

--- a/solution.py
+++ b/solution.py
@@ -1,8 +1,11 @@
+import functools
 import math
 
 import jax
 import jax.numpy as jnp
 from jax import lax
+from jax.experimental import pallas as pl
+from jax.experimental.pallas import tpu as pltpu
 from jax.sharding import Mesh, PartitionSpec as P
 
 D = 2048
@@ -105,8 +108,7 @@
     return mine, swapped(mine, "core")
 
 
-def scatter_rows(partial_rows, dp):
-    part = lax.psum_scatter(partial_rows, PLANE, scatter_dimension=0, tiled=True)
+def finish_rows(part, dp):
     part = part.reshape(2, 32, part.shape[1])
     mine = lax.dynamic_index_in_dim(part, dp, 0, keepdims=False)
     theirs = lax.dynamic_index_in_dim(part, 1 - dp, 0, keepdims=False)
@@ -115,6 +117,152 @@
 
 def both_cores(own, sibling):
     return jnp.concatenate([own, sibling], axis=0)
+
+
+WIDE = 640
+VMEM_BYTES = 48 * 1024 * 1024
+
+
+def rope_places(head):
+    row = lax.broadcasted_iota(jnp.int32, (512, 128), 0)
+    lane = lax.broadcasted_iota(jnp.int32, (512, 128), 1)
+    wanted = lax.shift_right_logical(lane, 5) * 256 + head * 32 + (lane & 31)
+    return jnp.where((lane < 64) & (row == wanted), 1.0, 0.0).astype(bf16)
+
+
+def attend_kernel(scale, qn_ref, rope_ref, w_ref, win_ref, bias_ref, qf_ref, ol_ref, oh_ref, lse_ref):
+    q_latent = matmul_nt(qn_ref[...], w_ref[:, :QN]).astype(bf16)
+    q_rope = matmul(rope_ref[...], rope_places(pl.program_id(0))).astype(bf16)
+    qf_ref[0, :, :LATENT] = q_latent
+    qf_ref[0, :, LATENT:] = q_rope
+    scores = matmul_nt(q_latent, win_ref[:, :LATENT]) + matmul_nt(q_rope, win_ref[:, LATENT:])
+    logits = scores * scale + bias_ref[...]
+    row_max = jnp.max(logits, axis=1, keepdims=True)
+    expo = jnp.exp(logits - row_max)
+    total = jnp.sum(expo, axis=1, keepdims=True)
+    probs = (expo / total).astype(bf16)
+    o_latent = matmul(probs, win_ref[:, :LATENT]).astype(bf16)
+    ol_ref[0] = o_latent
+    oh_ref[...] = matmul(o_latent, w_ref[:, QN:]).astype(bf16)
+    lse_ref[0] = jnp.broadcast_to(row_max + jnp.log(total), lse_ref.shape[1:])
+
+
+def attend_back_kernel(
+    scale,
+    bh_ref,
+    w_ref,
+    win_ref,
+    bias_ref,
+    qf_ref,
+    qn_ref,
+    ol_ref,
+    lse_ref,
+    cos_ref,
+    sin_ref,
+    ge_ref,
+    bqn_ref,
+    rope_ref,
+    bwin_ref,
+):
+    head = pl.program_id(0)
+
+    @pl.when(head == 0)
+    def _():
+        bwin_ref[...] = jnp.zeros_like(bwin_ref)
+        rope_ref[...] = jnp.zeros_like(rope_ref)
+
+    back_heads = bh_ref[...]
+    ge_ref[:, QN:] = matmul_tn(ol_ref[0], back_heads).astype(bf16)
+    back_olatent = matmul_nt(back_heads, w_ref[:, QN:]).astype(bf16)
+    scores = matmul_nt(qf_ref[0], win_ref[...])
+    probs = jnp.exp(scores * scale + bias_ref[...] - lse_ref[0][:, :1])
+    back_probs = matmul_nt(back_olatent, win_ref[:, :LATENT])
+    delta = jnp.sum(probs * back_probs, axis=1, keepdims=True)
+    back_scores = (probs * (back_probs - delta) * scale).astype(bf16)
+    bwin_ref[...] += matmul_tn(back_scores, qf_ref[0])
+    bwin_ref[:, :LATENT] += matmul_tn(probs.astype(bf16), back_olatent)
+    back_q = matmul(back_scores, win_ref[...])
+    back_qlatent = back_q[:, :LATENT].astype(bf16)
+    ge_ref[:, :QN] = matmul_tn(back_qlatent, qn_ref[...]).astype(bf16)
+    bqn_ref[...] = matmul(back_qlatent, w_ref[:, :QN]).astype(bf16)
+    halves = back_q[:, LATENT:]
+    lane = lax.broadcasted_iota(jnp.int32, halves.shape, 1)
+    crossed = jnp.where(lane < 32, pltpu.roll(halves, 96, 1), pltpu.roll(halves, 32, 1))
+    turned = (halves * cos_ref[...] + crossed * sin_ref[...]).astype(bf16)
+    rope_ref[...] += matmul_nt(turned, rope_places(head)).astype(bf16)
+
+
+def whole(shape):
+    return pl.BlockSpec(shape, lambda h: (0,) * len(shape))
+
+
+def attend(scale, q_nope, rope, w_expand, window, bias):
+    tok, heads, keys = q_nope.shape[0], q_nope.shape[1] // QN, window.shape[0]
+    return pl.pallas_call(
+        functools.partial(attend_kernel, scale),
+        grid=(heads,),
+        in_specs=[
+            pl.BlockSpec((tok, QN), lambda h: (0, h)),
+            whole((tok, 512)),
+            pl.BlockSpec((LATENT, QN + DV), lambda h: (0, h)),
+            whole((keys, WIDE)),
+            whole((tok, keys)),
+        ],
+        out_specs=[
+            pl.BlockSpec((1, tok, WIDE), lambda h: (h, 0, 0)),
+            pl.BlockSpec((1, tok, LATENT), lambda h: (h, 0, 0)),
+            pl.BlockSpec((tok, DV), lambda h: (0, h)),
+            pl.BlockSpec((1, tok, 128), lambda h: (h, 0, 0)),
+        ],
+        out_shape=[
+            jax.ShapeDtypeStruct((heads, tok, WIDE), bf16),
+            jax.ShapeDtypeStruct((heads, tok, LATENT), bf16),
+            jax.ShapeDtypeStruct((tok, heads * DV), bf16),
+            jax.ShapeDtypeStruct((heads, tok, 128), f32),
+        ],
+        compiler_params=pltpu.CompilerParams(vmem_limit_bytes=VMEM_BYTES),
+        cost_estimate=pl.CostEstimate(
+            flops=heads * tok * keys * 2400, bytes_accessed=12 << 20, transcendentals=heads * tok * keys
+        ),
+        name="attend",
+    )(q_nope, rope, w_expand, window, bias)
+
+
+def attend_back(scale, back_heads, w_expand, window, bias, q_full, q_nope, o_latent, log_total, cos, sin):
+    tok, heads, keys = q_nope.shape[0], q_nope.shape[1] // QN, window.shape[0]
+    return pl.pallas_call(
+        functools.partial(attend_back_kernel, scale),
+        grid=(heads,),
+        in_specs=[
+            pl.BlockSpec((tok, DV), lambda h: (0, h)),
+            pl.BlockSpec((LATENT, QN + DV), lambda h: (0, h)),
+            whole((keys, WIDE)),
+            whole((tok, keys)),
+            pl.BlockSpec((1, tok, WIDE), lambda h: (h, 0, 0)),
+            pl.BlockSpec((tok, QN), lambda h: (0, h)),
+            pl.BlockSpec((1, tok, LATENT), lambda h: (h, 0, 0)),
+            pl.BlockSpec((1, tok, 128), lambda h: (h, 0, 0)),
+            whole((tok, 128)),
+            whole((tok, 128)),
+        ],
+        out_specs=[
+            pl.BlockSpec((LATENT, QN + DV), lambda h: (0, h)),
+            pl.BlockSpec((tok, QN), lambda h: (0, h)),
+            whole((tok, 512)),
+            whole((keys, WIDE)),
+        ],
+        out_shape=[
+            jax.ShapeDtypeStruct((LATENT, heads * (QN + DV)), bf16),
+            jax.ShapeDtypeStruct((tok, heads * QN), bf16),
+            jax.ShapeDtypeStruct((tok, 512), bf16),
+            jax.ShapeDtypeStruct((keys, WIDE), f32),
+        ],
+        compiler_params=pltpu.CompilerParams(vmem_limit_bytes=VMEM_BYTES),
+        cost_estimate=pl.CostEstimate(
+            flops=heads * tok * keys * 6400, bytes_accessed=20 << 20, transcendentals=heads * tok * keys
+        ),
+        name="attend_back",
+    )(back_heads, w_expand, window, bias, q_full, q_nope, o_latent, log_total, cos, sin)
 
 
 def shards(
@@ -147,14 +295,23 @@
     score_scale = 1.0 / math.sqrt(QN + QR)
 
     gains = jnp.stack([prenorm, postnorm, jnp.pad(midnorm, (0, 24))], axis=1)
+    q_cols = query_proj.reshape(32, heads, QN + QR)
+    l_cols = latent_proj[:, :LATENT].reshape(32, 2, 16, 2, 8).transpose(0, 3, 2, 1, 4)
     pack_a = jnp.concatenate(
-        [query_proj, latent_proj, jnp.pad(gains, ((0, 0), (0, 61)))], axis=1
+        [
+            q_cols[:, :, :QN].reshape(32, heads * QN),
+            q_cols[:, :, QN : QN + 32].reshape(32, heads * 32),
+            q_cols[:, :, QN + 32 :].reshape(32, heads * 32),
+            l_cols.reshape(32, LATENT),
+            latent_proj[:, LATENT:],
+            jnp.pad(gains, ((0, 0), (0, 61))),
+        ],
+        axis=1,
     )
     pack_b = jnp.concatenate([expand_proj.reshape(32, 512), output_proj.T], axis=1)
     pack_c = jnp.concatenate([shared_gate, shared_up, shared_down.T], axis=1)
     own_a, sib_a = gather_plane(gather_dp(pack_a, dp))
     own_b, sib_b = gather_plane(gather_dp(pack_b, dp))
-    own_c, sib_c = gather_plane(gather_dp(pack_c, dp))
 
     place = jnp.arange(D, dtype=jnp.int32)
     true_of = (
@@ -165,22 +322,8 @@
     )
     perm = (place[:, None] == true_of[None, :]).astype(bf16)
     place_l = jnp.arange(LATENT, dtype=jnp.int32)
-    true_l = (
-        (place_l // 8 % 2) * 256
-        + (place_l // 16 % 16) * 16
-        + ((place_l // 256) ^ core) * 8
-        + place_l % 8
-    )
-    perm_l = (place_l[:, None] == true_l[None, :]).astype(bf16)
-    mid_true = (
-        (place // 32 % 2) * 256
-        + (place // 64 % 16) * 16
-        + ((place // 1024) ^ core) * 8
-        + place % 32
-    )
-    perm_m = (
-        (mid_true[:, None] == place_l[None, :]) & (place % 32 < 8)[:, None]
-    ).astype(bf16)
+    mid_at = ((place // 1024) ^ core) * 256 + (place // 32 % 32) * 8 + place % 32
+    perm_m = ((mid_at[:, None] == place_l[None, :]) & (place % 32 < 8)[:, None]).astype(bf16)
 
     def unpermute(values):
         high, low = split_low(values)
@@ -212,6 +355,9 @@
 
     grad_send = (matmul(weight_hi, cotangent) + matmul(weight_lo, cotangent)).astype(bf16)
     grad_rows = exchange(grad_send)
+    own_b, sib_b, grad_rows = lax.optimization_barrier((own_b, sib_b, grad_rows))
+    pack_c, own_a = lax.optimization_barrier((pack_c, own_a))
+    own_c, sib_c = gather_plane(gather_dp(pack_c, dp))
 
     pick = jnp.eye(8, 64, dtype=bf16)
     gain_rows = jnp.concatenate(
@@ -224,32 +370,40 @@
     normed_one, inverse_one = rms_forward(inputs, gain_one)
     h_one = normed_one.astype(bf16)
     projected = matmul(h_one[:, :half], own_a) + matmul(h_one[:, half:], sib_a)
-    queries = projected[:, : heads * (QN + QR)].reshape(tok, heads, QN + QR)
-    kv_pre = projected[:, heads * (QN + QR) : heads * (QN + QR) + LATENT + QR]
-    q_nope = queries[:, :, :QN].astype(bf16)
+    q_nope = projected[:, : heads * QN].astype(bf16)
+    q_first = projected[:, 1024:1280]
+    q_second = projected[:, 1280:1536]
+    kv_pre = projected[:, 1536:2112]
     latent_raw = kv_pre[:, :LATENT]
     latent_normed, inverse_mid = rms_forward(latent_raw, gain_mid)
     positions = (expert_pos * tok + jnp.arange(tok, dtype=jnp.int32)).astype(f32)
     cosine, sine_tab = rope_tables(positions, QR)
     latent = jnp.concatenate(
-        [latent_normed, rotate(kv_pre[:, LATENT:], cosine, sine_tab)], axis=1
+        [
+            latent_normed,
+            rotate(kv_pre[:, LATENT:], cosine, sine_tab),
+            jnp.zeros((tok, WIDE - LATENT - QR), f32),
+        ],
+        axis=1,
     ).astype(bf16)
-    expand_rows = jnp.concatenate([own_b[:, :512], sib_b[:, :512]], axis=0)
-    w_expand = matmul(perm_l, expand_rows.reshape(LATENT, heads * (QN + DV))).astype(bf16)
-    w_heads = w_expand.reshape(LATENT, heads, QN + DV)
-    w_key = w_heads[:, :, :QN]
-    w_value = w_heads[:, :, QN:]
+    cos_all = jnp.tile(cosine, (1, heads))
+    sin_all = jnp.tile(sine_tab, (1, heads))
+    rope = jnp.concatenate(
+        [q_first * cos_all - q_second * sin_all, q_first * sin_all + q_second * cos_all], axis=1
+    ).astype(bf16)
+    own_x = own_b[:, :512].reshape(256, heads * (QN + DV))
+    sib_x = sib_b[:, :512].reshape(256, heads * (QN + DV))
+    w_expand = jnp.concatenate(
+        [jnp.where(core == 0, own_x, sib_x), jnp.where(core == 0, sib_x, own_x)], axis=0
+    )
     w_out_own = own_b[:, 512:]
     w_out_sib = sib_b[:, 512:]
-    q_latent = jnp.einsum("thn,chn->thc", q_nope, w_key, preferred_element_type=f32)
-    q_rotated = rotate(queries[:, :, QN:], cosine[:, None, :], sine_tab[:, None, :])
-    q_full = jnp.concatenate([q_latent, q_rotated], axis=2).astype(bf16)
 
     own_blocks = jnp.stack([chip_shift(latent, k) for k in (4, 3, 2, 1)] + [latent])
     sib_blocks = swapped(
         lax.dynamic_slice_in_dim(own_blocks, 1 - core, 4, 0), "core"
     )
-    window = jnp.concatenate([own_blocks, sib_blocks], axis=0).reshape(9 * tok, LATENT + QR)
+    window = jnp.concatenate([own_blocks, sib_blocks], axis=0).reshape(9 * tok, WIDE)
     block_chip = jnp.concatenate(
         [chip - 4 + jnp.arange(5, dtype=jnp.int32), chip - 4 + core + jnp.arange(4, dtype=jnp.int32)]
     )
@@ -266,23 +420,9 @@
     offsets = query_pos[:, None] - key_pos[None, :]
     visible = (seg_query[:, None] == seg_keys[None, :]) & (offsets >= 0) & (offsets < WIN)
 
-    def score_block():
-        raw = jnp.einsum("thc,kc->htk", q_full, window, preferred_element_type=f32) * score_scale
-        return jnp.where(visible[None], raw, neg_big)
-
-    logits = score_block()
-    row_max = jnp.max(logits, axis=2, keepdims=True)
-    expo_vals = jnp.exp(logits - row_max)
-    expo_sum = jnp.sum(expo_vals, axis=2, keepdims=True)
-    log_total = row_max + jnp.log(expo_sum)
-    probs_low = (expo_vals / expo_sum).astype(bf16)
-    o_latent = jnp.einsum(
-        "htk,kc->thc", probs_low, window[:, :LATENT], preferred_element_type=f32
-    ).astype(bf16)
-    o_heads = (
-        jnp.einsum("thc,chv->thv", o_latent, w_value, preferred_element_type=f32)
-        .astype(bf16)
-        .reshape(tok, heads * DV)
+    bias = jnp.where(visible, 0.0, neg_big)
+    q_full, o_latent, o_heads, log_total = attend(
+        score_scale, q_nope, rope, w_expand, window, bias
     )
     attention = pair_sum(
         jnp.concatenate([matmul_nt(o_heads, w_out_own), matmul_nt(o_heads, w_out_sib)], axis=1),
@@ -321,7 +461,6 @@
     shared_rows = jnp.concatenate(
         [matmul_tn(h_two_pair, s_pair[:, : 2 * fs]), matmul_tn(up_pair, s_pair[:, 2 * fs :])], axis=1
     ).astype(bf16)
-    shared_grads = scatter_rows(shared_rows, dp)
 
     gate_pre = matmul(expert_rows, expert_gate[0])
     up_pre = matmul(expert_rows, expert_up[0])
@@ -334,49 +473,43 @@
     row_grad = (matmul_nt(back_gate, expert_gate[0]) + matmul_nt(back_up, expert_up[0])).astype(bf16)
     row_back = exchange(row_grad)
     e_part = matmul(hidden, expert_down[0]).astype(bf16)
-    e_part, row_back = lax.optimization_barrier((e_part, row_back))
+    expert_low = (
+        matmul_tn(expert_rows, back_gate).astype(bf16),
+        matmul_tn(expert_rows, back_up).astype(bf16),
+        matmul_tn(hidden, grad_rows).astype(bf16),
+    )
+    row_back = lax.optimization_barrier((row_back, shared_rows, expert_low, shared_back))[0]
+    shared_part = lax.psum_scatter(shared_rows, PLANE, scatter_dimension=0, tiled=True)
+    expert_other = tuple(swapped(g, "dp") for g in expert_low)
+    e_part = lax.optimization_barrier((e_part, row_back))[0]
     returned = exchange(e_part)
-    expert_grads = tuple(
-        pair_sum(g, "dp")
-        for g in (
-            matmul_tn(expert_rows, back_gate),
-            matmul_tn(expert_rows, back_up),
-            matmul_tn(hidden, grad_rows),
-        )
-    )
-    routed = matmul_tn(weight_hi, returned) + matmul_tn(weight_lo, returned)
-    output = unpermute(mid) + pair_sum(unpermute(s_part) + routed, "tensor")
-
     back_routed = matmul(matmul_tn(slot_pick, row_back).astype(bf16), perm)
     back_two = pair_sum(shared_back + back_routed, "tensor")
     back_midnorm, grad_gain_two = rms_backward(mid, inverse_two, gain_two, back_two)
     back_mid = upstream + back_midnorm
     back_attn = back_mid.astype(bf16)
+    first_other, back_attn = lax.optimization_barrier((expert_other[0], back_attn))
 
     back_heads = (
-        (matmul(back_attn[:, :half], w_out_own) + matmul(back_attn[:, half:], w_out_sib))
-        .astype(bf16)
-        .reshape(tok, heads, DV)
-    )
-    grad_value = jnp.einsum("thc,thv->chv", o_latent, back_heads, preferred_element_type=f32)
-    back_olatent = jnp.einsum(
-        "thv,chv->thc", back_heads, w_value, preferred_element_type=f32
+        matmul(back_attn[:, :half], w_out_own) + matmul(back_attn[:, half:], w_out_sib)
     ).astype(bf16)
-    probs_back = jnp.exp(score_block() - log_total)
-    back_probs = jnp.einsum(
-        "thc,kc->htk", back_olatent, window[:, :LATENT], preferred_element_type=f32
-    )
-    row_delta = jnp.sum(probs_back * back_probs, axis=2, keepdims=True)
-    back_scores = (probs_back * (back_probs - row_delta) * score_scale).astype(bf16)
-    back_qfull = jnp.einsum("htk,kc->thc", back_scores, window, preferred_element_type=f32)
-    value_part = jnp.einsum(
-        "htk,thc->kc", probs_back.astype(bf16), back_olatent, preferred_element_type=f32
-    )
-    back_window = jnp.einsum("htk,thc->kc", back_scores, q_full, preferred_element_type=f32)
-    back_window = back_window + jnp.pad(value_part, ((0, 0), (0, QR)))
-    back_blocks = back_window.reshape(9, tok, LATENT + QR)
+    pad_lanes = jnp.zeros((tok, 64), f32)
+    grad_expand, back_qnope, back_rope, back_window = attend_back(
+        score_scale,
+        back_heads,
+        w_expand,
+        window,
+        bias,
+        q_full,
+        q_nope,
+        o_latent,
+        log_total,
+        jnp.concatenate([cosine, cosine, pad_lanes], axis=1),
+        jnp.concatenate([sine_tab, -sine_tab, pad_lanes], axis=1),
+    )
+    back_blocks = back_window.reshape(9, tok, WIDE)
     from_sib = swapped(back_blocks[5:].astype(bf16), "core").astype(f32)
-    pad_block = jnp.zeros((1, tok, LATENT + QR), f32)
+    pad_block = jnp.zeros((1, tok, WIDE), f32)
     from_sib = jnp.where(
         core == 0,
         jnp.concatenate([pad_block, from_sib], axis=0),
@@ -387,25 +520,17 @@
     for index, k in enumerate((4, 3, 2, 1)):
         back_latent = back_latent + chip_shift(chip_blocks[index].astype(bf16), -k).astype(f32)
 
-    back_qlatent = back_qfull[:, :, :LATENT].astype(bf16)
-    back_qrope = rotate(back_qfull[:, :, LATENT:], cosine[:, None, :], -sine_tab[:, None, :])
-    grad_key = jnp.einsum("thc,thn->chn", back_qlatent, q_nope, preferred_element_type=f32)
-    back_qnope = jnp.einsum("thc,chn->thn", back_qlatent, w_key, preferred_element_type=f32)
-    back_queries = (
-        jnp.concatenate([back_qnope, back_qrope], axis=2)
-        .reshape(tok, heads * (QN + QR))
-        .astype(bf16)
-    )
-    grad_expand = jnp.concatenate([grad_key, grad_value], axis=2).reshape(
-        LATENT, heads * (QN + DV)
-    )
+    back_queries = jnp.concatenate([back_qnope, back_rope], axis=1)
 
     back_raw, grad_gain_mid = rms_backward(
         latent_raw, inverse_mid, gain_mid, back_latent[:, :LATENT]
     )
     back_kvpre = jnp.concatenate(
-        [back_raw, rotate(back_latent[:, LATENT:], cosine, -sine_tab)], axis=1
+        [back_raw, rotate(back_latent[:, LATENT : LATENT + QR], cosine, -sine_tab)], axis=1
     ).astype(bf16)
+    shared_part, second_other, returned, back_queries = lax.optimization_barrier(
+        (shared_part, expert_other[1], returned, back_queries)
+    )
     back_both = jnp.concatenate(
         [back_queries, back_kvpre, jnp.zeros((tok, 64), bf16)], axis=1
     )
@@ -415,6 +540,9 @@
     )
     back_innorm, grad_gain_one = rms_backward(inputs, inverse_one, gain_one, back_one)
     input_grad = unpermute(back_mid + back_innorm)
+
+    routed = matmul_tn(weight_hi, returned) + matmul_tn(weight_lo, returned)
+    output = unpermute(mid) + pair_sum(unpermute(s_part) + routed, "tensor")
 
     h_one_pair = both_cores(h_one[:, :half], swapped(h_one[:, half:], "core"))
     attn_pair = both_cores(back_attn[:, :half], swapped(back_attn[:, half:], "core"))
@@ -422,8 +550,9 @@
     back_pair = both_cores(back_both[:, :2112], swapped(back_both[:, :2112], "core"))
     rows_ql = matmul_tn(h_one_pair, back_pair)
     rows_out = matmul_tn(attn_pair, heads_pair)
-    expand_low = matmul_tn(perm_l, grad_expand.astype(bf16)).astype(bf16)
-    rows_expand = expand_low[:256].astype(f32) + swapped(expand_low[256:], "core").astype(f32)
+    expand_mine = lax.dynamic_slice_in_dim(grad_expand, core * 256, 256, 0)
+    expand_theirs = lax.dynamic_slice_in_dim(grad_expand, 256 - core * 256, 256, 0)
+    rows_expand = expand_mine.astype(f32) + swapped(expand_theirs, "core").astype(f32)
     rows_expand = rows_expand.reshape(1024, 512)
     mid_low = matmul_nt(perm_m, grad_gain_mid.astype(bf16)[None, :])
     gain_cols = jnp.concatenate([grad_gain_one[:, None], grad_gain_two[:, None], mid_low], axis=1)
@@ -432,17 +561,36 @@
     attn_rows = jnp.concatenate(
         [rows_ql, jnp.pad(rows_gain, ((0, 0), (0, 61))), rows_expand, rows_out], axis=1
     ).astype(bf16)
-    attn_grads = scatter_rows(attn_rows, dp)
+    attn_part = lax.psum_scatter(attn_rows, PLANE, scatter_dimension=0, tiled=True)
+    attn_part, third_other = lax.optimization_barrier((attn_part, expert_other[2]))
+    attn_grads = finish_rows(attn_part, dp)
+    shared_grads = finish_rows(shared_part, dp)
+    expert_grads = tuple(
+        mine.astype(f32) + other.astype(f32)
+        for mine, other in zip(expert_low, (first_other, second_other, third_other))
+    )
     latent_gain = attn_grads[:, 1536:2176]
     replicated = latent_gain.at[:, 577].multiply(0.5).at[:, 576].multiply(0.5)
     replicated = pair_sum(replicated, "tensor")
+    query_grad = jnp.concatenate(
+        [
+            attn_grads[:, :1024].reshape(32, heads, QN),
+            attn_grads[:, 1024:1280].reshape(32, heads, 32),
+            attn_grads[:, 1280:1536].reshape(32, heads, 32),
+        ],
+        axis=2,
+    ).reshape(32, heads * (QN + QR))
+    latent_cols = replicated[:, :LATENT].reshape(32, 2, 16, 2, 8).transpose(0, 3, 2, 1, 4)
+    latent_grad = jnp.concatenate(
+        [latent_cols.reshape(32, LATENT), replicated[:, LATENT : LATENT + QR]], axis=1
+    )
 
     return (
         output.astype(bf16),
         input_grad,
         replicated[:, 576],
-        attn_grads[:, :1536],
-        replicated[:, :576],
+        query_grad,
+        latent_grad,
         replicated[:8, 578],
         attn_grads[:, 2176:2688].reshape(8, 2048),
         attn_grads[:, 2688:].T,

time: 901 us -> 864 us (0.959)
  matrix products: 230 us -> 172 us
  Pallas kernels: 0 us -> 36.6 us
  waiting for transfers between devices: 438 us -> 408 us
  other arithmetic: 65.4 us -> 75.3 us
    all_gather x3, waiting for transfers between devices: 93.7 us -> 181 us  [gather_plane(): mine = lax.all_gather(pair, PLANE, axis=0, tiled=True)]
    ppermute x27, waiting for transfers between devices: 197 us -> 133 us  [swapped(): return lax.ppermute(block, axis, [(0, 1), (1, 0)])]
    all_to_all x4, waiting for transfers between devices: 126 us -> 78.9 us  [exchange(): lax.all_to_all(blocks, EXPERT, split_axis=0, concat_axis=0, tiled=True)]
    dot_general x12 -> x0, matrix products: 43.2 us -> none  [the longest x1 11.2 us: shards(): jnp.einsum('htk,thc->kc', back_scores, q_full, preferred_element_type=f32)]
    pallas_call x0 -> x2, Pallas kernels: none -> 36.6 us  [the longest x1 23.7 us: attend_back(): pl.pallas_call(functools.partial(attend_back_kernel, scale), grid=(heads,...]
    dot_general x20 -> x19, matrix products: 76.9 us -> 63.1 us  [matmul(): return jnp.dot(left_op, right_op, preferred_element_type=f32)]
    unnamed x227 -> x218, local copies, waits for them, and re-layouts: 22 us -> 18.8 us
    dot_general x10 -> x9, matrix products: 36.9 us -> 37.7 us  [matmul_tn(): lax.dot_general(left_op, right_op, (((0,), (0,)), ((), ())), preferred_el...]
  transfers between devices with their start and end apart: 44 -> 44, of which waited for: 24 -> 19; matrix products, arithmetic and copies ran while one was open for 35% -> 33% of each run, Pallas kernels for 0% -> 4%
where the time goes in v2:
time: 864 us; the launch traced here: 851 us
  waiting for transfers between devices  408 us (47%)
  matrix products  172 us (20%)
  other arithmetic  75.3 us (9%)
  local copies, waits for them, and re-layouts  74.4 us (9%)
  starting transfers between devices  69 us (8%)
  Pallas kernels  36.6 us (4%)
  between operations  16 us (2%)
    all_gather x3, waiting for transfers between devices, gather_plane(): mine = lax.all_gather(pair, PLANE, axis=0, tiled=True)  181 us
    ppermute x27, waiting for transfers between devices, swapped(): return lax.ppermute(block, axis, [(0, 1), (1, 0)])  133 us
    all_to_all x4, waiting for transfers between devices, exchange(): lax.all_to_all(blocks, EXPERT, split_axis=0, concat_axis=0, tiled=True)  78.9 us
    dot_general x20, matrix products, matmul_nt(): lax.dot_general(left_op, right_op, (((1,), (1,)), ((), ())), preferred_el...  71.1 us
    dot_general x19, matrix products, matmul(): return jnp.dot(left_op, right_op, preferred_element_type=f32)  63.1 us
    dot_general x9, matrix products, matmul_tn(): lax.dot_general(left_op, right_op, (((0,), (0,)), ((), ())), preferred_el...  37.7 us
    all_to_all x4, starting transfers between devices, exchange(): lax.all_to_all(blocks, EXPERT, split_axis=0, concat_axis=0, tiled=True)  27.6 us
    pallas_call x1, Pallas kernels, attend_back(): pl.pallas_call(functools.partial(attend_back_kernel, scale), grid=(heads,...  23.7 us
  transfers between devices with their start and end apart: 44, of which 19 were waited for; matrix products, arithmetic and copies ran while one was open for 33% of the time, Pallas kernels for 4%

profile of v2, /device:TPU:0, one launch (start us, length us, event | category | flops | bytes accessed | tf_op | source)
XLA Modules:
  0.0 850.9 jit_solution(7989740893308496075)
XLA Ops:
  13.8 3.7 collective-permute-done
  25.6 48.4 %all-gather.4.cloned.1.call-done = bf16[1024,2176]{1,0:T(8,128)(2,1)} async-done(((bf16[64,2176]{1,0:T(8,128)(2,1)}), bf16[1024,2176]{1,0:T(8,128)(2,1)}) %all-gather.4.cloned.1.call-update) | async-done | bytes 4456464 | tf_op jit(solution)/shard_map/all_gather | solution.py:107
  75.4 7.0 collective-permute-done.10
  86.4 3.3 add_convert_fusion.1
  89.7 5.9 all-to-all-start
  95.6 65.0 %all-gather.6.cloned.1.call-done = bf16[1024,1536]{1,0:T(8,128)(2,1)} async-done(((bf16[64,1536]{1,0:T(8,128)(2,1)}), bf16[1024,1536]{1,0:T(8,128)(2,1)}) %all-gather.6.cloned.1.call-update) | async-done | bytes 3145744 | tf_op jit(solution)/shard_map/all_gather | solution.py:107
  162.3 3.4 multiply_reduce_fusion.5
  166.1 67.3 %all-gather.8.cloned.1.call-done = bf16[1024,4224]{1,0:T(8,128)(2,1)} async-done(((bf16[64,4224]{1,0:T(8,128)(2,1)}), bf16[1024,4224]{1,0:T(8,128)(2,1)}) %all-gather.8.cloned.1.call-update) | async-done | bytes 8650768 | tf_op jit(solution)/shard_map/all_gather | solution.py:107
  235.3 3.0 broadcast_select_fusion
  244.2 3.3 fusion.219
  247.5 3.1 convolution_add_fusion
  252.9 3.3 collective-permute-start.7
  256.2 4.8 collective-permute-start.6
  263.9 3.2 collective-permute-start.4
  267.2 3.2 collective-permute-done.4
  293.5 12.9 %attend.1 = (bf16[8,128,640]{2,1,0:T(8,128)(2,1)S(1)}, bf16[8,128,512]{2,1,0:T(8,128)(2,1)S(1)}, bf16[128,1024]{1,0:T(8,128)(2,1)S(1)}, f32[8,128,128]{2,1,0:T(8,128)S(1)}) custom-call(bf16[128,1024]{1,0:T(8,128)(2,1)S(1)} %copy-done.5, bf16[128,512]{1,0:T(8,128)(2,1)S(1)} %pad_maximum_fusion.17.rope_ref, ...), custom_call_target="tpu_custom_call" | custom-call | flops 2831155200 | bytes 12582912 | tf_op jit(solution)/shard_map/attend/pallas_call | solution.py:201
  306.5 3.4 fusion.101
  310.8 3.3 collective-permute-start.9
  314.1 3.4 fusion.232
  317.5 9.4 %collective-permute-done.9 = bf16[128,2048]{0,1:T(8,128)(2,1)S(1)} collective-permute-done((bf16[128,2048]{0,1:T(8,128)(2,1)S(1)}, bf16[128,2048]{0,1:T(8,128)(2,1)S(1)}, u32[]{:S(2)}, u32[]{:S(2)}) %collective-permute-start.9) | collective-permute-done | bytes 524320 | tf_op jit(solution)/shard_map/ppermute | solution.py:29
  330.2 3.6 fusion.30
  340.1 7.9 convolution_convert_fusion.4
  348.0 9.5 %all-to-all-start.1 = ((bf16[32,32,2048]{2,1,0:T(8,128)(2,1)}), bf16[32,32,2048]{2,1,0:T(8,128)(2,1)}, u32[]{:S(2)}, u32[]{:S(2)}) async-start(bf16[32,32,2048]{2,1,0:T(8,128)(2,1)} %bitcast.186), calls=%async_computation.2 | async-start | bytes 8388608 | tf_op jit(solution)/shard_map/all_to_all | solution.py:352
  364.2 3.8 pad_maximum_fusion
  368.0 52.5 %all-to-all-done.1 = bf16[32,32,2048]{2,1,0:T(8,128)(2,1)} async-done(((bf16[32,32,2048]{2,1,0:T(8,128)(2,1)}), bf16[32,32,2048]{2,1,0:T(8,128)(2,1)}, u32[]{:S(2)}, u32[]{:S(2)}) %all-to-all-start.1) | async-done | bytes 4194336 | tf_op jit(solution)/shard_map/all_to_all | solution.py:352
  420.5 6.1 fusion.45
  426.6 5.0 fusion.49
  431.7 7.6 multiply_convert_fusion
  439.3 3.5 fusion.47
  442.9 5.3 add_convert_fusion
  448.3 6.0 all-to-all-start.2
  456.0 7.5 convolution_convert_fusion.6
  464.3 6.8 convolution_convert_fusion.5
  472.4 6.8 convolution_convert_fusion.7
  479.3 5.1 fusion.28
  486.8 26.4 %all-to-all-done.2 = bf16[32,32,2048]{2,1,0:T(8,128)(2,1)} async-done(((bf16[32,32,2048]{2,1,0:T(8,128)(2,1)}), bf16[32,32,2048]{2,1,0:T(8,128)(2,1)}, u32[]{:S(2)}, u32[]{:S(2)}) %all-to-all-start.2) | async-done | bytes 4194336 | tf_op jit(solution)/shard_map/all_to_all | solution.py:352
  513.3 8.1 fusion.79
  524.1 6.4 convolution_convert_fusion.3
  530.4 6.1 all-to-all-start.3
  536.9 66.2 %collective-permute-done.17 = bf16[128,2048]{0,1:T(8,128)(2,1)} collective-permute-done((bf16[128,2048]{0,1:T(8,128)(2,1)}, bf16[128,2048]{0,1:T(8,128)(2,1)}, u32[]{:S(2)}, u32[]{:S(2)}) %collective-permute-start.17) | collective-permute-done | bytes 524320 | tf_op jit(solution)/shard_map/ppermute | solution.py:29
  605.2 3.4 fusion.224
  611.5 23.7 %attend_back.1 = (bf16[512,2048]{1,0:T(8,128)(2,1)}, bf16[128,1024]{1,0:T(8,128)(2,1)S(1)}, bf16[128,512]{1,0:T(8,128)(2,1)S(1)}, f32[1152,640]{1,0:T(8,128)}) custom-call(bf16[128,1024]{1,0:T(8,128)(2,1)S(1)} %fusion.104.bh_ref, bf16[512,2048]{1,0:T(8,128)(2,1)} %constant_dynamic-update-slice_fusion.w_ref, bf16[1152,640]{1,0:T(8,128)(2,1)} %bitcast.26.win_ref, ...), custom_call_target="tpu_custom_call" | custom-call | flops 7549747200 | bytes 20971520 | tf_op jit(solution)/shard_map/attend_back/pallas_call | solution.py:233
  649.3 3.2 collective-permute-done.20
  653.9 3.7 collective-permute-done.22
  657.6 3.4 collective-permute-done.21
  666.8 3.8 convolution_convert_fusion.11
  670.6 3.6 convolution_convert_fusion.10
  676.9 3.1 convolution_convert_fusion.9
  684.1 6.7 collective-permute-done.24
  706.0 3.9 fusion.27
  709.9 10.3 %copy.160 = bf16[1024,3712]{1,0:T(8,128)(2,1)} copy(bf16[1024,3712]{0,1:T(8,128)(2,1)} %fusion.27) | data formatting | bytes 15204352
  721.5 5.3 fusion.6
  730.2 3.2 fusion.61
  733.4 3.7 fusion.4
  737.0 3.7 fusion.74
  740.8 6.6 add_bitcast_fusion.2
  749.3 3.0 fusion.234
  752.3 3.0 fusion.80
  756.1 6.6 add_bitcast_fusion.1
  762.6 35.8 %collective-permute-done.34 = bf16[32,4224]{1,0:T(8,128)(2,1)S(1)} collective-permute-done((bf16[32,4224]{1,0:T(8,128)(2,1)S(1)}, bf16[32,4224]{1,0:T(8,128)(2,1)S(1)}, u32[]{:S(2)}, u32[]{:S(2)}) %collective-permute-start.34) | collective-permute-done | bytes 270368 | tf_op jit(solution)/shard_map/ppermute | solution.py:29
  800.9 3.7 fusion
  804.6 4.7 fusion.75
  809.9 4.6 fusion.78
  818.8 6.4 add_bitcast_fusion
  (456 shorter events, 165.1 us)
Async XLA Ops:
  7.2 424.5 %copy-start = (bf16[1,704,2048]{2,1,0:T(8,128)(2,1)S(1)}, bf16[1,704,2048]{2,1,0:T(8,128)(2,1)}, u32[]{:S(2)}) copy-start(bf16[1,704,2048]{2,1,0:T(8,128)(2,1)} %param.35) | copy-start | bytes 8650756
  7.2 66.8 %all-gather.4.cloned.1.call-start = ((), (), s32[]{:S(2)}) async-start(), calls=%async_computation.6 | async-start | bytes 4734976 | tf_op jit(solution)/shard_map/all_gather | solution.py:107
  12.0 72.4 %copy-start.83 = (s32[128,6]{0,1:T(8,128)S(1)}, s32[128,6]{0,1:T(8,128)}, u32[]{:S(2)}) copy-start(s32[128,6]{0,1:T(8,128)} %param.37) | copy-start | bytes 9220
  12.0 72.4 %copy-start.84 = (f32[128,6]{0,1:T(8,128)S(1)}, f32[128,6]{0,1:T(8,128)}, u32[]{:S(2)}) copy-start(f32[128,6]{0,1:T(8,128)} %param.38) | copy-start | bytes 9220
  12.1 5.3 collective-permute-start
  17.5 67.5 %copy-start.47 = (bf16[128,2048]{1,0:T(8,128)(2,1)S(1)}, bf16[128,2048]{1,0:T(8,128)(2,1)}, u32[]{:S(2)}) copy-start(bf16[128,2048]{1,0:T(8,128)(2,1)} %param.39) | copy-start | bytes 1572868
  18.3 142.4 %all-gather.6.cloned.1.call-start = ((), (), s32[]{:S(2)}) async-start(), calls=%async_computation.7 | async-start | bytes 3342336 | tf_op jit(solution)/shard_map/all_gather | solution.py:107
  18.4 4.7 collective-permute-start.2
  23.8 209.6 %all-gather.8.cloned.1.call-start = ((), (), s32[]{:S(2)}) async-start(), calls=%async_computation.8 | async-start | bytes 9191424 | tf_op jit(solution)/shard_map/all_gather | solution.py:107
  74.0 8.4 collective-permute-start.10
  86.3 154.5 %collective-permute-start.1 = (bf16[1024,2176]{1,0:T(8,128)(2,1)}, bf16[1024,2176]{1,0:T(8,128)(2,1)}, u32[]{:S(2)}, u32[]{:S(2)}) collective-permute-start(bf16[1024,2176]{1,0:T(8,128)(2,1)} %all-gather.4.cloned.1.call-done), channel_id=1, source_target_pairs={{0,2},{2,0},{1,3},{3,1},{4,6},{6,4},{5,7},{7,5},{8,10},{10,8},{9,1... | collective-permute-start | bytes 13369352 | tf_op jit(solution)/shard_map/ppermute | solution.py:29
  89.7 72.2 %copy-start.69 = (s32[8192]{0:T(1024)S(1)}, s32[8192]{0:T(1024)}, u32[]{:S(2)}) copy-start(s32[8192]{0:T(1024)} %param.36) | copy-start | bytes 98308
  89.7 72.6 %copy-start.93 = (bf16[128,2048]{1,0:T(8,128)(2,1)S(1)}, bf16[128,2048]{1,0:T(8,128)(2,1)}, u32[]{:S(2)}) copy-start(bf16[128,2048]{1,0:T(8,128)(2,1)} %param.22) | copy-start | bytes 1572868
  89.7 145.6 %all-to-all-start = ((bf16[32,32,2048]{2,1,0:T(8,128)(2,1)}), bf16[32,32,2048]{2,1,0:T(8,128)(2,1)}, u32[]{:S(2)}, u32[]{:S(2)}) async-start(bf16[32,32,2048]{2,1,0:T(8,128)(2,1)} %bitcast.183), calls=%async_computation | async-start | bytes 8388608 | tf_op jit(solution)/shard_map/all_to_all | solution.py:352
  160.6 74.7 %collective-permute-start.3 = (bf16[1024,1536]{1,0:T(8,128)(2,1)}, bf16[1024,1536]{1,0:T(8,128)(2,1)}, u32[]{:S(2)}, u32[]{:S(2)}) collective-permute-start(bf16[1024,1536]{1,0:T(8,128)(2,1)} %all-gather.6.cloned.1.call-done), channel_id=1, source_target_pairs={{0,2},{2,0},{1,3},{3,1},{4,6},{6,4},{5,7},{7,5},{8,10},{10,8},{9,1... | collective-permute-start | bytes 9437192 | tf_op jit(solution)/shard_map/ppermute | solution.py:29
  162.0 88.7 %copy-start.89 = (pred[2048]{0:T(1024)(128)(4,1)}, pred[2048]{0:T(1024)(128)(4,1)S(1)}, u32[]{:S(2)}) copy-start(pred[2048]{0:T(1024)(128)(4,1)S(1)} %fusion.191) | copy-start | bytes 6148
  162.0 88.7 %copy-start.75 = (s32[2048]{0:T(1024)}, s32[2048]{0:T(1024)S(1)}, u32[]{:S(2)}) copy-start(s32[2048]{0:T(1024)S(1)} %fusion.189) | copy-start | bytes 24580
  165.7 76.9 %copy-start.79 = (f32[128]{0:T(128)}, f32[128]{0:T(128)S(1)}, u32[]{:S(2)}) copy-start(f32[128]{0:T(128)S(1)} %add_rsqrt_fusion.2) | copy-start | bytes 1540
  233.4 94.2 %collective-permute-start.11 = (bf16[1024,4224]{1,0:T(8,128)(2,1)}, bf16[1024,4224]{1,0:T(8,128)(2,1)}, u32[]{:S(2)}, u32[]{:S(2)}) collective-permute-start(bf16[1024,4224]{1,0:T(8,128)(2,1)} %all-gather.8.cloned.1.call-done), channel_id=1, source_target_pairs={{0,2},{2,0},{1,3},{3,1},{4,6},{6,4},{5,7},{7,5},{8,10},{10,8},{9,1... | collective-permute-start | bytes 25952264 | tf_op jit(solution)/shard_map/ppermute | solution.py:29
  250.6 23.4 %copy-start.20 = (f32[128,2176]{1,0:T(8,128)}, f32[128,2176]{1,0:T(8,128)S(1)}, u32[]{:S(2)}) copy-start(f32[128,2176]{1,0:T(8,128)S(1)} %convolution_add_fusion) | copy-start | bytes 3342340
  250.6 22.6 %copy-start.70 = (bf16[640]{0:T(1024)(128)(2,1)S(1)}, bf16[640]{0:T(1024)(128)(2,1)}, u32[]{:S(2)}) copy-start(bf16[640]{0:T(1024)(128)(2,1)} %pad.81.clone) | copy-start | bytes 3844
  250.8 23.2 %copy-start.77 = (f32[128]{0:T(128)}, f32[128]{0:T(128)S(1)}, u32[]{:S(2)}) copy-start(f32[128]{0:T(128)S(1)} %add_rsqrt_fusion.1) | copy-start | bytes 1540
  251.7 24.2 %copy-start.66 = (f32[1,512]{1,0:T(1,128)}, f32[1,512]{1,0:T(1,128)S(1)}, u32[]{:S(2)}) copy-start(f32[1,512]{1,0:T(1,128)S(1)} %fusion.39) | copy-start | bytes 6148
  251.7 23.1 %copy-start.30 = (bf16[256,2048]{1,0:T(8,128)(2,1)S(1)}, bf16[256,2048]{1,0:T(8,128)(2,1)}, u32[]{:S(2)}) copy-start(bf16[256,2048]{1,0:T(8,128)(2,1)} %select_n.214) | copy-start | bytes 3145732
  252.7 29.8 %copy-start.54 = (f32[128,32]{1,0:T(8,128)}, f32[128,32]{1,0:T(8,128)S(1)}, u32[]{:S(2)}) copy-start(f32[128,32]{1,0:T(8,128)S(1)} %get-tuple-element.172) | copy-start | bytes 49156
  252.9 19.5 %collective-permute-start.7 = (bf16[128,640]{1,0:T(8,128)(2,1)S(1)}, bf16[128,640]{1,0:T(8,128)(2,1)S(1)}, u32[]{:S(2)}, u32[]{:S(2)}) collective-permute-start(bf16[128,640]{1,0:T(8,128)(2,1)S(1)} %pad_maximum_fusion.16), channel_id=1, source_target_pairs={{0,4},{4,8},{8,12},{12,16},{16,20},{20,24},{24,28},{28,32},{32,36}... | collective-permute-start | bytes 491528 | tf_op jit(solution)/shard_map/ppermute | solution.py:35
  256.2 15.6 %collective-permute-start.6 = (bf16[128,640]{1,0:T(8,128)(2,1)S(1)}, bf16[128,640]{1,0:T(8,128)(2,1)S(1)}, u32[]{:S(2)}, u32[]{:S(2)}) collective-permute-start(bf16[128,640]{1,0:T(8,128)(2,1)S(1)} %pad_maximum_fusion.16), channel_id=1, source_target_pairs={{0,8},{4,12},{8,16},{12,20},{16,24},{20,28},{24,32},{28,36},{32,40... | collective-permute-start | bytes 491528 | tf_op jit(solution)/shard_map/ppermute | solution.py:35
  261.0 10.1 %collective-permute-start.5 = (bf16[128,640]{1,0:T(8,128)(2,1)S(1)}, bf16[128,640]{1,0:T(8,128)(2,1)S(1)}, u32[]{:S(2)}, u32[]{:S(2)}) collective-permute-start(bf16[128,640]{1,0:T(8,128)(2,1)S(1)} %pad_maximum_fusion.16), channel_id=1, source_target_pairs={{0,12},{4,16},{8,20},{12,24},{16,28},{20,32},{24,36},{28,40},{32,4... | collective-permute-start | bytes 491528 | tf_op jit(solution)/shard_map/ppermute | solution.py:35
  263.9 6.4 collective-permute-start.4
  274.8 15.7 %collective-permute-start.8 = (bf16[4,128,640]{2,1,0:T(8,128)(2,1)}, bf16[4,128,640]{2,1,0:T(8,128)(2,1)}, u32[]{:S(2)}, u32[]{:S(2)}) collective-permute-start(bf16[4,128,640]{2,1,0:T(8,128)(2,1)} %constant_dynamic-slice_fusion.2), channel_id=1, source_target_pairs={{0,2},{2,0},{1,3},{3,1},{4,6},{6,4},{5,7},{7,5},{8,10},{10,8},{9,1... | collective-permute-start | bytes 1966088 | tf_op jit(solution)/shard_map/ppermute | solution.py:29
  310.8 16.1 %collective-permute-start.9 = (bf16[128,2048]{0,1:T(8,128)(2,1)S(1)}, bf16[128,2048]{0,1:T(8,128)(2,1)S(1)}, u32[]{:S(2)}, u32[]{:S(2)}) collective-permute-start(bf16[128,2048]{0,1:T(8,128)(2,1)S(1)} %pad_maximum_fusion.7), channel_id=1, source_target_pairs={{0,1},{1,0},{2,3},{3,2},{4,5},{5,4},{6,7},{7,6},{8,9},{9,8},{10,11... | collective-permute-start | bytes 1572872 | tf_op jit(solution)/shard_map/ppermute | solution.py:29
  337.0 20.6 %collective-permute-start.13 = (bf16[128,4224]{1,0:T(8,128)(2,1)}, bf16[128,4224]{1,0:T(8,128)(2,1)}, u32[]{:S(2)}, u32[]{:S(2)}) collective-permute-start(bf16[128,4224]{1,0:T(8,128)(2,1)} %pad_maximum_fusion.2), channel_id=1, source_target_pairs={{0,2},{2,0},{1,3},{3,1},{4,6},{6,4},{5,7},{7,5},{8,10},{10,8},{9,1... | collective-permute-start | bytes 3244040 | tf_op jit(solution)/shard_map/ppermute | solution.py:29
  337.8 21.6 %collective-permute-start.14 = (bf16[128,1024]{0,1:T(8,128)(2,1)}, bf16[128,1024]{0,1:T(8,128)(2,1)}, u32[]{:S(2)}, u32[]{:S(2)}) collective-permute-start(bf16[128,1024]{0,1:T(8,128)(2,1)} %get-tuple-element.146), channel_id=1, source_target_pairs={{0,2},{2,0},{1,3},{3,1},{4,6},{6,4},{5,7},{7,5},{8,10},{10,8},{9,1... | collective-permute-start | bytes 786440 | tf_op jit(solution)/shard_map/ppermute | solution.py:29
  340.0 21.5 %collective-permute-start.12 = (bf16[128,1024]{0,1:T(8,128)(2,1)}, bf16[128,1024]{0,1:T(8,128)(2,1)}, u32[]{:S(2)}, u32[]{:S(2)}) collective-permute-start(bf16[128,1024]{0,1:T(8,128)(2,1)} %get-tuple-element.144), channel_id=1, source_target_pairs={{0,2},{2,0},{1,3},{3,1},{4,6},{6,4},{5,7},{7,5},{8,10},{10,8},{9,1... | collective-permute-start | bytes 786440 | tf_op jit(solution)/shard_map/ppermute | solution.py:29
  348.0 72.5 %all-to-all-start.1 = ((bf16[32,32,2048]{2,1,0:T(8,128)(2,1)}), bf16[32,32,2048]{2,1,0:T(8,128)(2,1)}, u32[]{:S(2)}, u32[]{:S(2)}) async-start(bf16[32,32,2048]{2,1,0:T(8,128)(2,1)} %bitcast.186), calls=%async_computation.2 | async-start | bytes 8388608 | tf_op jit(solution)/shard_map/all_to_all | solution.py:352
  357.5 307.5 %reduce-scatter.5.cloned.1.call-start = ((), (), s32[]{:S(2)}) async-start(), calls=%async_computation.9 | async-start | bytes 9191424 | tf_op jit(solution)/shard_map/reduce_scatter | solution.py:482
  448.3 65.0 %all-to-all-start.2 = ((bf16[32,32,2048]{2,1,0:T(8,128)(2,1)}), bf16[32,32,2048]{2,1,0:T(8,128)(2,1)}, u32[]{:S(2)}, u32[]{:S(2)}) async-start(bf16[32,32,2048]{2,1,0:T(8,128)(2,1)} %bitcast.187), calls=%async_computation.3 | async-start | bytes 8388608 | tf_op jit(solution)/shard_map/all_to_all | solution.py:352
  463.5 201.4 %collective-permute-start.15 = (bf16[2048,704]{0,1:T(8,128)(2,1)}, bf16[2048,704]{0,1:T(8,128)(2,1)}, u32[]{:S(2)}, u32[]{:S(2)}) collective-permute-start(bf16[2048,704]{0,1:T(8,128)(2,1)} %convolution_convert_fusion.6), channel_id=1, source_target_pairs={{0,64},{64,0},{1,65},{65,1},{2,66},{66,2},{3,67},{67,3},{4,68},{68... | collective-permute-start | bytes 8650760 | tf_op jit(solution)/shard_map/ppermute | solution.py:29
  471.2 137.5 %collective-permute-start.16 = (bf16[2048,704]{0,1:T(8,128)(2,1)}, bf16[2048,704]{0,1:T(8,128)(2,1)}, u32[]{:S(2)}, u32[]{:S(2)}) collective-permute-start(bf16[2048,704]{0,1:T(8,128)(2,1)} %convolution_convert_fusion.5), channel_id=1, source_target_pairs={{0,64},{64,0},{1,65},{65,1},{2,66},{66,2},{3,67},{67,3},{4,68},{68... | collective-permute-start | bytes 8650760 | tf_op jit(solution)/shard_map/ppermute | solution.py:29
  484.4 28.9 %copy-start.73 = (s32[2048]{0:T(1024)S(1)}, s32[2048]{0:T(1024)}, u32[]{:S(2)}) copy-start(s32[2048]{0:T(1024)} %copy-done.71) | copy-start | bytes 24580
  521.4 81.6 %collective-permute-start.17 = (bf16[128,2048]{0,1:T(8,128)(2,1)}, bf16[128,2048]{0,1:T(8,128)(2,1)}, u32[]{:S(2)}, u32[]{:S(2)}) collective-permute-start(bf16[128,2048]{0,1:T(8,128)(2,1)} %fusion.79), channel_id=1, source_target_pairs={{0,1},{1,0},{2,3},{3,2},{4,5},{5,4},{6,7},{7,6},{8,9},{9,8},{10,11... | collective-permute-start | bytes 1572872 | tf_op jit(solution)/shard_map/ppermute | solution.py:29
  530.4 72.6 %copy-start.63 = (f32[1,2048]{1,0:T(1,128)S(1)}, f32[1,2048]{1,0:T(1,128)}, u32[]{:S(2)}) copy-start(f32[1,2048]{1,0:T(1,128)} %get-tuple-element.169) | copy-start | bytes 24580
  530.4 72.6 %copy-start.82 = (f32[128]{0:T(128)S(1)}, f32[128]{0:T(128)}, u32[]{:S(2)}) copy-start(f32[128]{0:T(128)} %copy-done.81) | copy-start | bytes 1540
  530.4 134.5 %all-to-all-start.3 = ((bf16[32,32,2048]{2,1,0:T(8,128)(2,1)}), bf16[32,32,2048]{2,1,0:T(8,128)(2,1)}, u32[]{:S(2)}, u32[]{:S(2)}) async-start(bf16[32,32,2048]{2,1,0:T(8,128)(2,1)} %bitcast.185), calls=%async_computation.4 | async-start | bytes 8388608 | tf_op jit(solution)/shard_map/all_to_all | solution.py:352
  536.6 277.9 %reduce-scatter.7.cloned.1.call-start = ((), (), s32[]{:S(2)}) async-start(), calls=%async_computation.10 | async-start | bytes 8077312
  638.9 3.6 collective-permute-start.19
  644.1 8.5 collective-permute-start.20
  645.4 8.5 collective-permute-start.23
  646.7 10.9 %collective-permute-start.22 = (bf16[128,640]{1,0:T(8,128)(2,1)S(1)}, bf16[128,640]{1,0:T(8,128)(2,1)S(1)}, u32[]{:S(2)}, u32[]{:S(2)}) collective-permute-start(bf16[128,640]{1,0:T(8,128)(2,1)S(1)} %get-tuple-element.132), channel_id=1, source_target_pairs={{8,0},{12,4},{16,8},{20,12},{24,16},{28,20},{32,24},{36,28},{40,32... | collective-permute-start | bytes 491528 | tf_op jit(solution)/shard_map/ppermute | solution.py:35
  648.0 13.0 %collective-permute-start.21 = (bf16[128,640]{1,0:T(8,128)(2,1)S(1)}, bf16[128,640]{1,0:T(8,128)(2,1)S(1)}, u32[]{:S(2)}, u32[]{:S(2)}) collective-permute-start(bf16[128,640]{1,0:T(8,128)(2,1)S(1)} %get-tuple-element.133), channel_id=1, source_target_pairs={{12,0},{16,4},{20,8},{24,12},{28,16},{32,20},{36,24},{40,28},{44,3... | collective-permute-start | bytes 491528 | tf_op jit(solution)/shard_map/ppermute | solution.py:35
  652.6 24.2 %collective-permute-start.30 = (bf16[128,1024]{1,0:T(8,128)(2,1)S(1)}, bf16[128,1024]{1,0:T(8,128)(2,1)}, u32[]{:S(2)}, u32[]{:S(2)}) collective-permute-start(bf16[128,1024]{1,0:T(8,128)(2,1)S(1)} %copy-done.2), channel_id=1, source_target_pairs={{0,2},{2,0},{1,3},{3,1},{4,6},{6,4},{5,7},{7,5},{8,10},{10,8},{9,1... | collective-permute-start | bytes 786440 | tf_op jit(solution)/shard_map/ppermute | solution.py:29
  653.9 23.0 %collective-permute-start.29 = (bf16[128,1024]{0,1:T(8,128)(2,1)}, bf16[128,1024]{0,1:T(8,128)(2,1)}, u32[]{:S(2)}, u32[]{:S(2)}) collective-permute-start(bf16[128,1024]{0,1:T(8,128)(2,1)} %get-tuple-element.142), channel_id=1, source_target_pairs={{0,2},{2,0},{1,3},{3,1},{4,6},{6,4},{5,7},{7,5},{8,10},{10,8},{9,1... | collective-permute-start | bytes 786440 | tf_op jit(solution)/shard_map/ppermute | solution.py:29
  657.6 35.9 %collective-permute-start.28 = (bf16[256,2048]{1,0:T(8,128)(2,1)}, bf16[256,2048]{1,0:T(8,128)(2,1)}, u32[]{:S(2)}, u32[]{:S(2)}) collective-permute-start(bf16[256,2048]{1,0:T(8,128)(2,1)} %constant_dynamic-slice_fusion), channel_id=1, source_target_pairs={{0,2},{2,0},{1,3},{3,1},{4,6},{6,4},{5,7},{7,5},{8,10},{10,8},{9,1... | collective-permute-start | bytes 3145736 | tf_op jit(solution)/shard_map/ppermute | solution.py:29
  675.1 15.7 %collective-permute-start.24 = (bf16[128,2048]{0,1:T(8,128)(2,1)}, bf16[128,2048]{0,1:T(8,128)(2,1)}, u32[]{:S(2)}, u32[]{:S(2)}) collective-permute-start(bf16[128,2048]{0,1:T(8,128)(2,1)} %pad_maximum_fusion.8), channel_id=1, source_target_pairs={{0,1},{1,0},{2,3},{3,2},{4,5},{5,4},{6,7},{7,6},{8,9},{9,8},{10,11... | collective-permute-start | bytes 1572872 | tf_op jit(solution)/shard_map/ppermute | solution.py:29
  676.8 26.5 %collective-permute-start.25 = (bf16[128,1024]{0,1:T(8,128)(2,1)}, bf16[128,1024]{0,1:T(8,128)(2,1)}, u32[]{:S(2)}, u32[]{:S(2)}) collective-permute-start(bf16[128,1024]{0,1:T(8,128)(2,1)} %get-tuple-element.140), channel_id=1, source_target_pairs={{0,2},{2,0},{1,3},{3,1},{4,6},{6,4},{5,7},{7,5},{8,10},{10,8},{9,1... | collective-permute-start | bytes 786440 | tf_op jit(solution)/shard_map/ppermute | solution.py:29
  683.6 17.6 %collective-permute-start.26 = (bf16[128,2112]{0,1:T(8,128)(2,1)}, bf16[128,2112]{0,1:T(8,128)(2,1)}, u32[]{:S(2)}, u32[]{:S(2)}) collective-permute-start(bf16[128,2112]{0,1:T(8,128)(2,1)} %copy.145), channel_id=1, source_target_pairs={{0,2},{2,0},{1,3},{3,1},{4,6},{6,4},{5,7},{7,5},{8,10},{10,8},{9,1... | collective-permute-start | bytes 1622024 | tf_op jit(solution)/shard_map/ppermute | solution.py:29
  693.0 8.2 collective-permute-start.27
  726.8 90.0 %collective-permute-start.31 = (bf16[704,2048]{1,0:T(8,128)(2,1)}, bf16[704,2048]{1,0:T(8,128)(2,1)}, u32[]{:S(2)}, u32[]{:S(2)}) collective-permute-start(bf16[704,2048]{1,0:T(8,128)(2,1)} %convolution_convert_fusion.7), channel_id=1, source_target_pairs={{0,64},{64,0},{1,65},{65,1},{2,66},{66,2},{3,67},{67,3},{4,68},{68... | collective-permute-start | bytes 8650760 | tf_op jit(solution)/shard_map/ppermute | solution.py:29
  747.4 51.0 %collective-permute-start.34 = (bf16[32,4224]{1,0:T(8,128)(2,1)S(1)}, bf16[32,4224]{1,0:T(8,128)(2,1)S(1)}, u32[]{:S(2)}, u32[]{:S(2)}) collective-permute-start(bf16[32,4224]{1,0:T(8,128)(2,1)S(1)} %dynamic-slice_bitcast_fusion), channel_id=1, source_target_pairs={{0,64},{64,0},{1,65},{65,1},{2,66},{66,2},{3,67},{67,3},{4,68},{68... | collective-permute-start | bytes 811016 | tf_op jit(solution)/shard_map/ppermute | solution.py:29
  755.3 43.9 %copy-start.17 = (f32[128,2048]{0,1:T(8,128)S(1)}, f32[128,2048]{0,1:T(8,128)}, u32[]{:S(2)}) copy-start(f32[128,2048]{0,1:T(8,128)} %get-tuple-element.179) | copy-start | bytes 3145732
  755.3 43.9 %copy-start.29 = (f32[128,2048]{0,1:T(8,128)S(1)}, f32[128,2048]{0,1:T(8,128)}, u32[]{:S(2)}) copy-start(f32[128,2048]{0,1:T(8,128)} %get-tuple-element.113) | copy-start | bytes 3145732
  755.4 54.5 %collective-permute-start.18 = (bf16[128,2048]{1,0:T(8,128)(2,1)S(1)}, bf16[128,2048]{1,0:T(8,128)(2,1)S(1)}, u32[]{:S(2)}, u32[]{:S(2)}) collective-permute-start(bf16[128,2048]{1,0:T(8,128)(2,1)S(1)} %fusion.80), channel_id=1, source_target_pairs={{0,1},{1,0},{2,3},{3,2},{4,5},{5,4},{6,7},{7,6},{8,9},{9,8},{10,11... | collective-permute-start | bytes 1572872 | tf_op jit(solution)/shard_map/ppermute | solution.py:29
  818.4 7.7 collective-permute-start.32
  830.2 10.7 %collective-permute-start.33 = (bf16[32,640]{1,0:T(8,128)(2,1)S(1)}, bf16[32,640]{1,0:T(8,128)(2,1)}, u32[]{:S(2)}, u32[]{:S(2)}) collective-permute-start(bf16[32,640]{1,0:T(8,128)(2,1)S(1)} %convert_element_type.342), channel_id=1, source_target_pairs={{0,1},{1,0},{2,3},{3,2},{4,5},{5,4},{6,7},{7,6},{8,9},{9,8},{10,11... | collective-permute-start | bytes 122888 | tf_op jit(solution)/shard_map/ppermute | solution.py:29
  (84 other events, 598.4 us)
Sparse Core Ops, SparseCore 0:
  18.4 55.5 all-gather.3
  76.7 83.8 all-gather.5
  163.4 69.9 all-gather.7
  368.2 140.3 reduce-scatter.4
  720.4 85.3 reduce-scatter.6

commit v3 on v2

--- a/solution.py
+++ b/solution.py
@@ -96,6 +96,59 @@
     )
 
 
+def xored(block, axis, k):
+    return lax.ppermute(block, axis, [(i, i ^ k) for i in range(4)])
+
+
+def merged(own, other, upper, dim):
+    return jnp.concatenate(
+        [jnp.where(upper, other, own), jnp.where(upper, own, other)], axis=dim
+    )
+
+
+def joined(own, other, pos, cross, dim):
+    if not cross:
+        return merged(own, other, pos >= 2, dim)
+    outer = (pos == 0) | (pos == 3)
+    ends = jnp.where(outer, own, other)
+    middle = jnp.where(outer, other, own)
+    low, high = jnp.split(ends, 2, axis=dim)
+    return jnp.concatenate([low, middle, high], axis=dim)
+
+
+def together(*trees):
+    return lax.optimization_barrier(trees)
+
+
+def gather_step(blocks, axes, second):
+    return [
+        xored(block, axis, 1 if cross == second else 3)
+        for block, (axis, _, _, cross) in zip(blocks, axes)
+    ]
+
+
+def steps_of(axis, cross):
+    return ((axis, 3), (axis, 1)) if cross else ((axis, 1), (axis, 3))
+
+
+def stream_places(size, first, cross, y_pos, z_pos):
+    index = jnp.arange(size, dtype=jnp.int32)
+    part = size // 16
+    order = jnp.asarray((3, 2, 0, 1) if cross else (1, 2, 0, 3), jnp.int32)
+    one, two = order[index // (4 * part)], index // part % 4
+    y_at, z_at = (two, one ^ z_pos) if first == "z" else (one ^ y_pos, two)
+    at = (y_at * 4 + z_at) * part + index % part
+    return (index[:, None] == at[None, :]).astype(bf16)
+
+
+def summed(mine, other, dim):
+    return jnp.concatenate(mine, axis=dim).astype(f32) + jnp.concatenate(other, axis=dim).astype(f32)
+
+
+def add_low(left, right):
+    return (left.astype(f32) + right.astype(f32)).astype(bf16)
+
+
 def gather_dp(pack, dp):
     other = swapped(pack, "dp")
     return jnp.concatenate(
@@ -103,9 +156,12 @@
     )
 
 
-def gather_plane(pair):
-    mine = lax.all_gather(pair, PLANE, axis=0, tiled=True)
-    return mine, swapped(mine, "core")
+def mine_of(part, dp):
+    return lax.dynamic_index_in_dim(part, dp, 0, keepdims=False)
+
+
+def theirs_of(part, dp):
+    return lax.dynamic_index_in_dim(part, 1 - dp, 0, keepdims=False)
 
 
 def finish_rows(part, dp):
@@ -162,6 +218,8 @@
     ge_ref,
     bqn_ref,
     rope_ref,
+    own_ref,
+    sib_ref,
     bwin_ref,
 ):
     head = pl.program_id(0)
@@ -191,6 +249,121 @@
     turned = (halves * cos_ref[...] + crossed * sin_ref[...]).astype(bf16)
     rope_ref[...] += matmul_nt(turned, rope_places(head)).astype(bf16)
 
+    @pl.when(head == pl.num_programs(0) - 1)
+    def _():
+        own_ref[...] = bwin_ref[: own_ref.shape[0]]
+        sib_ref[...] = bwin_ref[own_ref.shape[0] :].astype(bf16)
+
+
+def to_chip_order(values, core):
+    lane = lax.broadcasted_iota(jnp.int32, (values.shape[0], 128), 1)
+    low = (lane & 32) == 0
+    sides = ([], [])
+    for at in range(0, 1024, 128):
+        first, second = values[:, at : at + 128], values[:, 1024 + at : 1152 + at]
+        sides[0].append(jnp.where(low, first, pltpu.roll(second, 32, 1)))
+        sides[1].append(jnp.where(low, pltpu.roll(first, 96, 1), second))
+    side0, side1 = (jnp.concatenate(side, axis=1) for side in sides)
+    mine = core == 0
+    return jnp.where(mine, side0, side1), jnp.where(mine, side1, side0)
+
+
+def from_chip_order(own, sibling, core):
+    lane = lax.broadcasted_iota(jnp.int32, (own.shape[0], 128), 1)
+    low = (lane & 32) == 0
+    mine = core == 0
+    side0, side1 = jnp.where(mine, own, sibling), jnp.where(mine, sibling, own)
+    rows = ([], [])
+    for at in range(0, 1024, 128):
+        first, second = side0[:, at : at + 128], side1[:, at : at + 128]
+        rows[0].append(jnp.where(low, first, pltpu.roll(second, 32, 1)))
+        rows[1].append(jnp.where(low, pltpu.roll(first, 96, 1), second))
+    return jnp.concatenate(rows[0] + rows[1], axis=1)
+
+
+def enter_kernel(core_ref, x_ref, g_ref, x_out, inverse_out, g_out):
+    values = x_ref[...].astype(f32)
+    mean = jnp.mean(values * values, axis=1, keepdims=True)
+    inverse_out[...] = jnp.broadcast_to(lax.rsqrt(mean + epsilon), inverse_out.shape)
+    own, sibling = to_chip_order(values, core_ref[0])
+    x_out[:, :1024] = own
+    x_out[:, 1024:] = sibling
+    own, sibling = to_chip_order(g_ref[...].astype(f32), core_ref[0])
+    g_out[:, :1024] = own.astype(bf16)
+    g_out[:, 1024:] = sibling.astype(bf16)
+
+
+def dispatch_kernel(core_ref, mid_ref, gain_ref, pick_ref, h_ref, inverse_ref, rows_ref, true_ref):
+    @pl.when(pl.program_id(0) == 0)
+    def _():
+        mid = mid_ref[...]
+        inverse = lax.rsqrt(jnp.mean(mid * mid, axis=1, keepdims=True) + epsilon)
+        inverse_ref[...] = jnp.broadcast_to(inverse, inverse_ref.shape)
+        low = (mid * inverse * gain_ref[...]).astype(bf16)
+        h_ref[...] = low
+        wide = low.astype(f32)
+        true_ref[...] = from_chip_order(wide[:, :1024], wide[:, 1024:], core_ref[0]).astype(bf16)
+
+    rows_ref[...] = matmul(pick_ref[...], true_ref[...]).astype(bf16)
+
+
+def combine_kernel(core_ref, pick_ref, rows_ref, base_ref, out_ref, total_ref):
+    step = pl.program_id(0)
+
+    @pl.when(step == 0)
+    def _():
+        total_ref[...] = jnp.zeros_like(total_ref)
+
+    total_ref[...] += matmul_tn(pick_ref[...], rows_ref[...])
+
+    @pl.when(step == pl.num_programs(0) - 1)
+    def _():
+        own, sibling = to_chip_order(total_ref[...], core_ref[0])
+        out_ref[:, :1024] = (own + base_ref[:, :1024]).astype(bf16)
+        out_ref[:, 1024:] = (sibling + base_ref[:, 1024:]).astype(bf16)
+
+
+def routed_kernel(core_ref, weight_ref, rows_ref, base_ref, out_ref, total_ref):
+    step = pl.program_id(0)
+
+    @pl.when(step == 0)
+    def _():
+        total_ref[...] = from_chip_order(base_ref[:, :1024], base_ref[:, 1024:], core_ref[0])
+
+    high, low = split_low(weight_ref[...])
+    total_ref[...] += matmul_tn(high, rows_ref[...]) + matmul_tn(low, rows_ref[...])
+
+    @pl.when(step == pl.num_programs(0) - 1)
+    def _():
+        out_ref[...] = total_ref[...].astype(bf16)
+
+
+def leave_kernel(core_ref, mid_ref, part_ref, other_ref, out_ref):
+    true = from_chip_order(mid_ref[:, :1024], mid_ref[:, 1024:], core_ref[0])
+    out_ref[...] = (true + (part_ref[...].astype(f32) + other_ref[...].astype(f32))).astype(bf16)
+
+
+def grad_kernel(core_ref, grad_ref, out_ref):
+    out_ref[...] = from_chip_order(grad_ref[:, :1024], grad_ref[:, 1024:], core_ref[0])
+
+
+def scalar_spec():
+    return pl.BlockSpec(memory_space=pltpu.SMEM)
+
+
+def local_kernel(body, name, grid, in_specs, out_specs, out_shape, scratch=(), flops=0, moved=4 << 20):
+    return pl.pallas_call(
+        body,
+        grid=(grid,),
+        in_specs=in_specs,
+        out_specs=out_specs,
+        out_shape=out_shape,
+        scratch_shapes=scratch,
+        compiler_params=pltpu.CompilerParams(vmem_limit_bytes=VMEM_BYTES),
+        cost_estimate=pl.CostEstimate(flops=flops, bytes_accessed=moved, transcendentals=0),
+        name=name,
+    )
+
 
 def whole(shape):
     return pl.BlockSpec(shape, lambda h: (0,) * len(shape))
@@ -249,14 +422,17 @@
             pl.BlockSpec((LATENT, QN + DV), lambda h: (0, h)),
             pl.BlockSpec((tok, QN), lambda h: (0, h)),
             whole((tok, 512)),
-            whole((keys, WIDE)),
+            whole((5 * tok, WIDE)),
+            whole((4 * tok, WIDE)),
         ],
         out_shape=[
             jax.ShapeDtypeStruct((LATENT, heads * (QN + DV)), bf16),
             jax.ShapeDtypeStruct((tok, heads * QN), bf16),
             jax.ShapeDtypeStruct((tok, 512), bf16),
-            jax.ShapeDtypeStruct((keys, WIDE), f32),
-        ],
+            jax.ShapeDtypeStruct((5 * tok, WIDE), f32),
+            jax.ShapeDtypeStruct((4 * tok, WIDE), bf16),
+        ],
+        scratch_shapes=[pltpu.VMEM((keys, WIDE), f32)],
         compiler_params=pltpu.CompilerParams(vmem_limit_bytes=VMEM_BYTES),
         cost_estimate=pl.CostEstimate(
             flops=heads * tok * keys * 6400, bytes_accessed=20 << 20, transcendentals=heads * tok * keys
@@ -294,10 +470,16 @@
     expert_pos = chip * 2 + core
     score_scale = 1.0 / math.sqrt(QN + QR)
 
+    y_pos = lax.axis_index("y")
+    z_pos = lax.axis_index("z")
+    y_low = y_pos < 2
+    y_outer = (y_pos == 0) | (y_pos == 3)
+    fs = shared_gate.shape[1]
+
     gains = jnp.stack([prenorm, postnorm, jnp.pad(midnorm, (0, 24))], axis=1)
     q_cols = query_proj.reshape(32, heads, QN + QR)
     l_cols = latent_proj[:, :LATENT].reshape(32, 2, 16, 2, 8).transpose(0, 3, 2, 1, 4)
-    pack_a = jnp.concatenate(
+    pack = jnp.concatenate(
         [
             q_cols[:, :, :QN].reshape(32, heads * QN),
             q_cols[:, :, QN : QN + 32].reshape(32, heads * 32),
@@ -305,33 +487,78 @@
             l_cols.reshape(32, LATENT),
             latent_proj[:, LATENT:],
             jnp.pad(gains, ((0, 0), (0, 61))),
+            output_proj.T,
+            expand_proj.reshape(32, 512),
         ],
         axis=1,
     )
-    pack_b = jnp.concatenate([expand_proj.reshape(32, 512), output_proj.T], axis=1)
+    pair = gather_dp(pack, dp)
     pack_c = jnp.concatenate([shared_gate, shared_up, shared_down.T], axis=1)
-    own_a, sib_a = gather_plane(gather_dp(pack_a, dp))
-    own_b, sib_b = gather_plane(gather_dp(pack_b, dp))
 
     place = jnp.arange(D, dtype=jnp.int32)
-    true_of = (
-        (place // 32 % 2) * 1024
-        + (place // 64 % 16) * 64
-        + ((place // 1024) ^ core) * 32
-        + place % 32
-    )
-    perm = (place[:, None] == true_of[None, :]).astype(bf16)
     place_l = jnp.arange(LATENT, dtype=jnp.int32)
     mid_at = ((place // 1024) ^ core) * 256 + (place // 32 % 32) * 8 + place % 32
     perm_m = ((mid_at[:, None] == place_l[None, :]) & (place % 32 < 8)[:, None]).astype(bf16)
-
-    def unpermute(values):
-        high, low = split_low(values)
-        return matmul_nt(high, perm) + matmul_nt(low, perm)
-
-    inputs = matmul(hidden_in, perm)
-    upstream = matmul(cotangent, perm)
-    up_low = upstream.astype(bf16)
+    core_at = core.reshape(1)
+
+    def near_low(values):
+        low, high = values[:, :512], values[:, 512:]
+        return jnp.where(y_low, low, high), jnp.where(y_low, high, low)
+
+    def near_outer(values):
+        ends = jnp.concatenate([values[:, :256], values[:, 768:]], axis=1)
+        middle = values[:, 256:768]
+        return jnp.where(y_outer, ends, middle), jnp.where(y_outer, middle, ends)
+
+    def join_low(own, other):
+        return jnp.concatenate(
+            [jnp.where(y_low, own, other), jnp.where(y_low, other, own)], axis=1
+        )
+
+    def join_outer(own, other):
+        ends = jnp.where(y_outer, own, other)
+        middle = jnp.where(y_outer, other, own)
+        return jnp.concatenate([ends[:, :256], middle, ends[:, 256:]], axis=1)
+
+    cuts = (0, 1024, 2176, 3200)
+    chip_rows = [pair[:, a:b].reshape(1, 1, 64, b - a) for a, b in zip(cuts, cuts[1:])]
+    chip_rows.append(pair[:, 3200:].reshape(1, 1, 16, 2048))
+    along_z, along_y = ("z", z_pos, 1), ("y", y_pos, 0)
+    firsts = [along_z + (False,), along_z + (True,), along_y + (False,), along_y + (True,)]
+    seconds = [along_y + (False,), along_y + (True,), along_z + (False,), along_z + (True,)]
+
+    def pairs(blocks, got, axes):
+        return [
+            merged(own, other, pos >= 2 if cross else pos % 2 == 1, dim)
+            for own, other, (_, pos, dim, cross) in zip(blocks, got, axes)
+        ]
+
+    pair_c = gather_dp(pack_c, dp)
+    blocks, got, pair_c, core_at, hidden_in, cotangent, routes, segments, y_late, z_late = together(
+        chip_rows, gather_step(chip_rows, firsts, False), pair_c, core_at, hidden_in, cotangent,
+        routes, segments, y_pos, z_pos,
+    )
+    blocks = pairs(blocks, got, firsts)
+    blocks, got = together(blocks, gather_step(blocks, firsts, True))
+    blocks = [joined(o, g, p, c, d) for o, g, (_, p, d, c) in zip(blocks, got, firsts)]
+    blocks, got = together(blocks, gather_step(blocks, seconds, False))
+    blocks = pairs(blocks, got, seconds)
+    got = gather_step(blocks, seconds, True)
+    near_sib = [swapped(block, "core") for block in blocks[:2]]
+
+    inputs, inverse_one, up_low = local_kernel(
+        enter_kernel,
+        "enter",
+        1,
+        [scalar_spec(), whole((tok, D)), whole((tok, D))],
+        [whole((tok, D)), whole((tok, 128)), whole((tok, D))],
+        [
+            jax.ShapeDtypeStruct((tok, D), f32),
+            jax.ShapeDtypeStruct((tok, 128), f32),
+            jax.ShapeDtypeStruct((tok, D), bf16),
+        ],
+    )(core_at, hidden_in, cotangent)
+    inverse_one = inverse_one[:, :1]
 
     expert_ids = jnp.arange(32, dtype=jnp.int32)
     hits = routes[:, :, None] == expert_ids[None, None, :]
@@ -345,65 +572,24 @@
     taken = rank_et[:, None, :] == slot_ids[None, :, None]
     slot_pick = taken.astype(bf16).reshape(32 * SLOTS, tok)
     slot_weight = jnp.where(taken, weight_te.T[:, None, :], 0.0).reshape(32 * SLOTS, tok)
+    slot_pick, slot_weight = together(slot_pick, slot_weight)
     weight_hi, weight_lo = split_low(slot_weight)
 
     def exchange(rows):
-        blocks = rows.reshape(32, SLOTS, D)
+        blocks = rows.reshape(32, SLOTS, rows.shape[1])
         return lax.all_to_all(blocks, EXPERT, split_axis=0, concat_axis=0, tiled=True).reshape(
-            32 * SLOTS, D
+            rows.shape
         )
 
-    grad_send = (matmul(weight_hi, cotangent) + matmul(weight_lo, cotangent)).astype(bf16)
-    grad_rows = exchange(grad_send)
-    own_b, sib_b, grad_rows = lax.optimization_barrier((own_b, sib_b, grad_rows))
-    pack_c, own_a = lax.optimization_barrier((pack_c, own_a))
-    own_c, sib_c = gather_plane(gather_dp(pack_c, dp))
-
-    pick = jnp.eye(8, 64, dtype=bf16)
-    gain_rows = jnp.concatenate(
-        [matmul_nt(pick, own_a[:, 2112:]), matmul_nt(pick, sib_a[:, 2112:])], axis=1
-    )
-    gain_one = gain_rows[0]
-    gain_two = gain_rows[1]
-    gain_mid = matmul(gain_rows.astype(bf16), perm_m)[2]
-
-    normed_one, inverse_one = rms_forward(inputs, gain_one)
-    h_one = normed_one.astype(bf16)
-    projected = matmul(h_one[:, :half], own_a) + matmul(h_one[:, half:], sib_a)
-    q_nope = projected[:, : heads * QN].astype(bf16)
-    q_first = projected[:, 1024:1280]
-    q_second = projected[:, 1280:1536]
-    kv_pre = projected[:, 1536:2112]
-    latent_raw = kv_pre[:, :LATENT]
-    latent_normed, inverse_mid = rms_forward(latent_raw, gain_mid)
-    positions = (expert_pos * tok + jnp.arange(tok, dtype=jnp.int32)).astype(f32)
-    cosine, sine_tab = rope_tables(positions, QR)
-    latent = jnp.concatenate(
-        [
-            latent_normed,
-            rotate(kv_pre[:, LATENT:], cosine, sine_tab),
-            jnp.zeros((tok, WIDE - LATENT - QR), f32),
-        ],
-        axis=1,
-    ).astype(bf16)
-    cos_all = jnp.tile(cosine, (1, heads))
-    sin_all = jnp.tile(sine_tab, (1, heads))
-    rope = jnp.concatenate(
-        [q_first * cos_all - q_second * sin_all, q_first * sin_all + q_second * cos_all], axis=1
-    ).astype(bf16)
-    own_x = own_b[:, :512].reshape(256, heads * (QN + DV))
-    sib_x = sib_b[:, :512].reshape(256, heads * (QN + DV))
-    w_expand = jnp.concatenate(
-        [jnp.where(core == 0, own_x, sib_x), jnp.where(core == 0, sib_x, own_x)], axis=0
-    )
-    w_out_own = own_b[:, 512:]
-    w_out_sib = sib_b[:, 512:]
-
-    own_blocks = jnp.stack([chip_shift(latent, k) for k in (4, 3, 2, 1)] + [latent])
-    sib_blocks = swapped(
-        lax.dynamic_slice_in_dim(own_blocks, 1 - core, 4, 0), "core"
-    )
-    window = jnp.concatenate([own_blocks, sib_blocks], axis=0).reshape(9 * tok, WIDE)
+    second = lax.axis_index("tensor") == 1
+    grad_cols = jnp.where(second, cotangent[:, half:], cotangent[:, :half])
+    grad_send = (matmul(weight_hi, grad_cols) + matmul(weight_lo, grad_cols)).astype(bf16)
+    places = [
+        stream_places(half, first, cross, y_late, z_late)
+        for first, cross in (("z", False), ("z", True), ("y", False))
+    ]
+    x_places = stream_places(256, "y", True, y_late, z_late)
+
     block_chip = jnp.concatenate(
         [chip - 4 + jnp.arange(5, dtype=jnp.int32), chip - 4 + core + jnp.arange(4, dtype=jnp.int32)]
     )
@@ -421,47 +607,151 @@
     visible = (seg_query[:, None] == seg_keys[None, :]) & (offsets >= 0) & (offsets < WIN)
 
     bias = jnp.where(visible, 0.0, neg_big)
+    positions = (expert_pos * tok + jnp.arange(tok, dtype=jnp.int32)).astype(f32)
+    cosine, sine_tab = rope_tables(positions, QR)
+    cos_all = jnp.tile(cosine, (1, heads))
+    sin_all = jnp.tile(sine_tab, (1, heads))
+
+    (
+        blocks, got, inputs, inverse_one, up_low, slot_pick, slot_weight, grad_send, pair_c, bias,
+        cosine, sine_tab, cos_all, sin_all, perm_m, places, x_places,
+    ) = together(
+        blocks, got, inputs, inverse_one, up_low, slot_pick, slot_weight, grad_send, pair_c, bias,
+        cosine, sine_tab, cos_all, sin_all, perm_m, places, x_places,
+    )
+    grad_half = exchange(grad_send)
+    upstream = up_low.astype(f32)
+    q_parts = [
+        w.reshape(512, 1024) for w in (blocks[0], got[0], near_sib[0], swapped(got[0], "core"))
+    ]
+    l_parts = [
+        w.reshape(512, 1152) for w in (blocks[1], got[1], near_sib[1], swapped(got[1], "core"))
+    ]
+    own_c = lax.all_gather(pair_c, PLANE, axis=0, tiled=True)
+    up_pair = both_cores(up_low[:, :half], swapped(up_low[:, half:], "core"))
+
+    pick = jnp.eye(8, 64, dtype=bf16)
+    gain_parts = [matmul_nt(pick, w[:, 1088:]) for w in l_parts]
+    gain_rows = jnp.concatenate(
+        [join_outer(gain_parts[0], gain_parts[1]), join_outer(gain_parts[2], gain_parts[3])], axis=1
+    )
+    gain_one = gain_rows[0]
+    gain_two = gain_rows[1]
+    gain_mid = matmul(gain_rows.astype(bf16), perm_m)[2]
+
+    h_one = (inputs * inverse_one * gain_one).astype(bf16)
+    h_parts = near_outer(h_one[:, :half]) + near_outer(h_one[:, half:])
+    kv_all = sum(matmul(h, w) for h, w in zip(h_parts, l_parts))
+    h_parts = near_low(h_one[:, :half]) + near_low(h_one[:, half:])
+    q_nope = sum(matmul(h, w) for h, w in zip(h_parts, q_parts)).astype(bf16)
+    q_first = kv_all[:, :256]
+    q_second = kv_all[:, 256:512]
+    kv_pre = kv_all[:, 512:1088]
+    latent_raw = kv_pre[:, :LATENT]
+    latent_normed, inverse_mid = rms_forward(latent_raw, gain_mid)
+    latent = jnp.concatenate(
+        [
+            latent_normed,
+            rotate(kv_pre[:, LATENT:], cosine, sine_tab),
+            jnp.zeros((tok, WIDE - LATENT - QR), f32),
+        ],
+        axis=1,
+    ).astype(bf16)
+    latent, blocks, got = together(latent, blocks[2:], got[2:])
+    w_out_own = joined(blocks[0], got[0], z_pos, False, 1).reshape(half, heads * DV)
+    w_out_sib = swapped(w_out_own, "core")
+    x_own = joined(blocks[1], got[1], z_pos, True, 1).reshape(256, heads * (QN + DV))
+    x_sib = swapped(x_own, "core")
+    w_expand = jnp.concatenate(
+        [jnp.where(core == 0, x_own, x_sib), jnp.where(core == 0, x_sib, x_own)], axis=0
+    )
+    rope = jnp.concatenate(
+        [q_first * cos_all - q_second * sin_all, q_first * sin_all + q_second * cos_all], axis=1
+    ).astype(bf16)
+    shifts = [chip_shift(latent, k) for k in (4, 3, 2, 1)]
+    shifts, latent, q_nope, rope, w_expand = together(shifts, latent, q_nope, rope, w_expand)
+    own_blocks = jnp.stack(shifts + [latent])
+    sib_blocks = swapped(
+        lax.dynamic_slice_in_dim(own_blocks, 1 - core, 4, 0), "core"
+    )
+    window = jnp.concatenate([own_blocks, sib_blocks], axis=0).reshape(9 * tok, WIDE)
+    window, grad_half = together(window, grad_half)
     q_full, o_latent, o_heads, log_total = attend(
         score_scale, q_nope, rope, w_expand, window, bias
     )
-    attention = pair_sum(
-        jnp.concatenate([matmul_nt(o_heads, w_out_own), matmul_nt(o_heads, w_out_sib)], axis=1),
-        "tensor",
-    )
-    mid = inputs + attention
-    normed_two, inverse_two = rms_forward(mid, gain_two)
-    h_two = normed_two.astype(bf16)
-
-    h_two_true = matmul_nt(h_two, perm).astype(bf16)
-    expert_rows = exchange(matmul(slot_pick, h_two_true).astype(bf16))
-
-    fs = shared_gate.shape[1]
-    s_both = matmul(h_two[:, :half], own_c[:, : 2 * fs]) + matmul(h_two[:, half:], sib_c[:, : 2 * fs])
-    s_gate = s_both[:, :fs]
-    s_up = s_both[:, fs:]
+    o_part = jnp.concatenate(
+        [matmul_nt(o_heads, w_out_own), matmul_nt(o_heads, w_out_sib)], axis=1
+    ).astype(bf16)
+    o_part = lax.optimization_barrier(o_part)
+    mid = inputs + (o_part.astype(f32) + swapped(o_part, "tensor").astype(f32))
+    h_one_pair = both_cores(h_one[:, :half], swapped(h_one[:, half:], "core"))
+    h_orders = [matmul(h_one_pair, p).astype(bf16) for p in places]
+    mid, grad_half, h_orders = together(mid, grad_half, h_orders)
+    grad_other = swapped(grad_half, "tensor")
+
+    slots = 32 * SLOTS
+    h_two, inverse_two, send_rows = local_kernel(
+        dispatch_kernel,
+        "dispatch",
+        4,
+        [
+            scalar_spec(),
+            whole((tok, D)),
+            whole((1, D)),
+            pl.BlockSpec((slots // 4, tok), lambda i: (i, 0)),
+        ],
+        [
+            whole((tok, D)),
+            whole((tok, 128)),
+            pl.BlockSpec((slots // 4, D), lambda i: (i, 0)),
+        ],
+        [
+            jax.ShapeDtypeStruct((tok, D), bf16),
+            jax.ShapeDtypeStruct((tok, 128), f32),
+            jax.ShapeDtypeStruct((slots, D), bf16),
+        ],
+        [pltpu.VMEM((tok, D), bf16)],
+        flops=2 * slots * tok * D,
+        moved=6 << 20,
+    )(core_at, mid, gain_two[None, :], slot_pick)
+    inverse_two = inverse_two[:, :1]
+    expert_rows = exchange(send_rows)
+
+    h_two_pair = both_cores(h_two[:, :half], swapped(h_two[:, half:], "core"))
+    s_all = jnp.concatenate(
+        [matmul(h_two_pair, own_c[:, : 2 * fs]), matmul(up_pair, own_c[:, 2 * fs :])], axis=1
+    )
+    s_mine = s_all[:tok] + swapped(s_all[tok:].astype(bf16), "core").astype(f32)
+    s_gate = s_mine[:, :fs]
+    s_up = s_mine[:, fs : 2 * fs]
+    back_shidden = s_mine[:, 2 * fs :]
     s_sig = jax.nn.sigmoid(s_gate)
     s_active = s_gate * s_sig
     s_hidden = (s_active * s_up).astype(bf16)
-    s_part = jnp.concatenate(
-        [matmul_nt(s_hidden, own_c[:, 2 * fs :]), matmul_nt(s_hidden, sib_c[:, 2 * fs :])], axis=1
-    )
-    back_shidden = matmul(up_low[:, :half], own_c[:, 2 * fs :]) + matmul(
-        up_low[:, half:], sib_c[:, 2 * fs :]
-    )
     back_sgate = (back_shidden * s_up * s_sig * (1.0 + s_gate * (1.0 - s_sig))).astype(bf16)
     back_sup = (back_shidden * s_active).astype(bf16)
-    back_sboth = jnp.concatenate([back_sgate, back_sup], axis=1)
-    shared_back = jnp.concatenate(
-        [matmul_nt(back_sboth, own_c[:, : 2 * fs]), matmul_nt(back_sboth, sib_c[:, : 2 * fs])], axis=1
-    )
-    h_two_pair = both_cores(h_two[:, :half], swapped(h_two[:, half:], "core"))
-    up_pair = both_cores(up_low[:, :half], swapped(up_low[:, half:], "core"))
-    s_acts = jnp.concatenate([back_sboth, s_hidden], axis=1)
+    s_acts = jnp.concatenate([back_sgate, back_sup, s_hidden], axis=1)
     s_pair = both_cores(s_acts, swapped(s_acts, "core"))
     shared_rows = jnp.concatenate(
         [matmul_tn(h_two_pair, s_pair[:, : 2 * fs]), matmul_tn(up_pair, s_pair[:, 2 * fs :])], axis=1
     ).astype(bf16)
-
+    grad_rows = jnp.concatenate(
+        [jnp.where(second, grad_other, grad_half), jnp.where(second, grad_half, grad_other)], axis=1
+    )
+    expert_rows, s_pair, shared_rows, grad_rows = together(
+        expert_rows, s_pair, shared_rows, grad_rows
+    )
+    shared_part = lax.psum_scatter(shared_rows, PLANE, scatter_dimension=0, tiled=True)
+    wide_all = jnp.concatenate(
+        [
+            matmul_nt(s_pair[:, : 2 * fs], own_c[:, : 2 * fs]),
+            matmul_nt(s_pair[:, 2 * fs :], own_c[:, 2 * fs :]),
+        ],
+        axis=1,
+    )
+    wide_got = swapped(wide_all[tok:].astype(bf16), "core").astype(f32)
+    shared_back = jnp.concatenate([wide_all[:tok, :half], wide_got[:, :half]], axis=1)
+    s_part = jnp.concatenate([wide_all[:tok, half:], wide_got[:, half:]], axis=1)
     gate_pre = matmul(expert_rows, expert_gate[0])
     up_pre = matmul(expert_rows, expert_up[0])
     gate_sig = jax.nn.sigmoid(gate_pre)
@@ -473,28 +763,62 @@
     row_grad = (matmul_nt(back_gate, expert_gate[0]) + matmul_nt(back_up, expert_up[0])).astype(bf16)
     row_back = exchange(row_grad)
     e_part = matmul(hidden, expert_down[0]).astype(bf16)
-    expert_low = (
-        matmul_tn(expert_rows, back_gate).astype(bf16),
-        matmul_tn(expert_rows, back_up).astype(bf16),
-        matmul_tn(hidden, grad_rows).astype(bf16),
-    )
-    row_back = lax.optimization_barrier((row_back, shared_rows, expert_low, shared_back))[0]
-    shared_part = lax.psum_scatter(shared_rows, PLANE, scatter_dimension=0, tiled=True)
-    expert_other = tuple(swapped(g, "dp") for g in expert_low)
-    e_part = lax.optimization_barrier((e_part, row_back))[0]
+    gate_low = [
+        matmul_tn(expert_rows[:, :half], back_gate).astype(bf16),
+        matmul_tn(expert_rows[:, half:], back_gate).astype(bf16),
+    ]
+    up_low_grad = [
+        matmul_tn(expert_rows[:, :half], back_up).astype(bf16),
+        matmul_tn(expert_rows[:, half:], back_up).astype(bf16),
+    ]
+    down_low = [
+        matmul_tn(hidden, grad_rows[:, :1536]).astype(bf16),
+        matmul_tn(hidden, grad_rows[:, 1536:]).astype(bf16),
+    ]
+    down_got = swapped(down_low[0], "dp")
+    row_back, down_got, gate_low, up_low_grad, e_part, s_part, shared_back = together(
+        row_back, down_got, gate_low, up_low_grad, e_part, s_part, shared_back
+    )
     returned = exchange(e_part)
-    back_routed = matmul(matmul_tn(slot_pick, row_back).astype(bf16), perm)
-    back_two = pair_sum(shared_back + back_routed, "tensor")
+    back_part = local_kernel(
+        combine_kernel,
+        "combine",
+        4,
+        [
+            scalar_spec(),
+            pl.BlockSpec((slots // 4, tok), lambda i: (i, 0)),
+            pl.BlockSpec((slots // 4, D), lambda i: (i, 0)),
+            whole((tok, D)),
+        ],
+        whole((tok, D)),
+        jax.ShapeDtypeStruct((tok, D), bf16),
+        [pltpu.VMEM((tok, D), f32)],
+        flops=2 * slots * tok * D,
+        moved=6 << 20,
+    )(core_at, slot_pick, row_back, shared_back)
+    back_two = back_part.astype(f32) + swapped(back_part, "tensor").astype(f32)
     back_midnorm, grad_gain_two = rms_backward(mid, inverse_two, gain_two, back_two)
     back_mid = upstream + back_midnorm
     back_attn = back_mid.astype(bf16)
-    first_other, back_attn = lax.optimization_barrier((expert_other[0], back_attn))
+    back_attn, grad_gain_two, back_mid, gate_low, up_low_grad, down_low = together(
+        back_attn, grad_gain_two, back_mid, gate_low, up_low_grad, down_low
+    )
+    down_got = [down_got, swapped(down_low[1], "dp")]
+    gate_got = [swapped(part, "dp") for part in gate_low]
+    up_got = [swapped(part, "dp") for part in up_low_grad]
+
+    attn_pair = both_cores(back_attn[:, :half], swapped(back_attn[:, half:], "core"))
+    attn_orders = [matmul(attn_pair, p).astype(bf16) for p in places[1:]]
+    heads_pair = both_cores(o_heads, swapped(o_heads, "core"))
+    gain_low = grad_gain_two.astype(bf16)
+    gain_sum = add_low(gain_low[:half], swapped(gain_low[half:], "core"))
+    gain_col = matmul_tn(places[2], jnp.broadcast_to(gain_sum[:, None], (half, 128))).astype(bf16)
 
     back_heads = (
         matmul(back_attn[:, :half], w_out_own) + matmul(back_attn[:, half:], w_out_sib)
     ).astype(bf16)
     pad_lanes = jnp.zeros((tok, 64), f32)
-    grad_expand, back_qnope, back_rope, back_window = attend_back(
+    grad_expand, back_qnope, back_rope, back_own, back_sib = attend_back(
         score_scale,
         back_heads,
         w_expand,
@@ -507,20 +831,66 @@
         jnp.concatenate([cosine, cosine, pad_lanes], axis=1),
         jnp.concatenate([sine_tab, -sine_tab, pad_lanes], axis=1),
     )
-    back_blocks = back_window.reshape(9, tok, WIDE)
-    from_sib = swapped(back_blocks[5:].astype(bf16), "core").astype(f32)
+    back_qnope, back_rope, back_own, back_sib, grad_expand, down_got[1] = together(
+        back_qnope, back_rope, back_own, back_sib, grad_expand, down_got[1]
+    )
+    acts_q = jnp.concatenate([back_qnope, back_rope], axis=1)
+    expand_mine = lax.dynamic_slice_in_dim(grad_expand, core * 256, 256, 0)
+    expand_theirs = lax.dynamic_slice_in_dim(grad_expand, 256 - core * 256, 256, 0)
+    from_sib, acts_other, expand_other, acts_q, expand_mine, heads_pair, attn_orders, down_low = together(
+        swapped(back_sib, "core"),
+        swapped(acts_q, "core"),
+        swapped(expand_theirs, "core"),
+        acts_q,
+        expand_mine,
+        heads_pair,
+        attn_orders,
+        down_low,
+    )
+
+    from_sib = from_sib.astype(f32).reshape(4, tok, WIDE)
     pad_block = jnp.zeros((1, tok, WIDE), f32)
     from_sib = jnp.where(
         core == 0,
         jnp.concatenate([pad_block, from_sib], axis=0),
         jnp.concatenate([from_sib, pad_block], axis=0),
     )
-    chip_blocks = back_blocks[:5] + from_sib
-    back_latent = chip_blocks[4]
-    for index, k in enumerate((4, 3, 2, 1)):
-        back_latent = back_latent + chip_shift(chip_blocks[index].astype(bf16), -k).astype(f32)
-
-    back_queries = jnp.concatenate([back_qnope, back_rope], axis=1)
+    chip_blocks = back_own.reshape(5, tok, WIDE) + from_sib
+    shifts = [chip_shift(chip_blocks[4 - k].astype(bf16), -k) for k in (4, 3, 2, 1)]
+
+    acts_q = both_cores(acts_q, acts_other)
+    rows_x = add_low(expand_mine, expand_other)
+    rows_x = matmul_tn(x_places, rows_x).astype(bf16).reshape(4, 4, 64, 512)
+
+    def halves(part):
+        at = slice(0, 512) if part == 0 else slice(512, 1024)
+        q_first = matmul_tn(h_orders[0][:, at], acts_q[:, :896])
+        q_second = jnp.concatenate(
+            [
+                matmul_tn(h_orders[1][:, at], acts_q[:, 896:]),
+                matmul_tn(attn_orders[0][:, at], heads_pair[:, :256]),
+            ],
+            axis=1,
+        )
+        third = jnp.concatenate(
+            [matmul_tn(attn_orders[1][:, at], heads_pair[:, 256:]).astype(bf16), gain_col[at]], axis=1
+        )
+        rows = [r.astype(bf16).reshape(2, 4, 64, 896) for r in (q_first, q_second, third)]
+        return rows + [rows_x[2 * part : 2 * part + 2]]
+
+    first_steps = [steps_of("z", False), steps_of("z", True), steps_of("y", False), steps_of("y", True)]
+    down_sum = summed(down_low, down_got, 1)
+    sends = halves(0)
+    (
+        sends, rows_x, chip_last, shifts, gate_got[0], h_orders, attn_orders, down_sum, shared_part,
+    ) = together(
+        sends, rows_x, chip_blocks[4], shifts, gate_got[0], h_orders, attn_orders, down_sum,
+        shared_part,
+    )
+    got = [xored(r, *steps[0]) for r, steps in zip(sends, first_steps)]
+    keeps = halves(1)
+
+    back_latent = chip_last + sum(shift.astype(f32) for shift in shifts)
 
     back_raw, grad_gain_mid = rms_backward(
         latent_raw, inverse_mid, gain_mid, back_latent[:, :LATENT]
@@ -528,79 +898,171 @@
     back_kvpre = jnp.concatenate(
         [back_raw, rotate(back_latent[:, LATENT : LATENT + QR], cosine, -sine_tab)], axis=1
     ).astype(bf16)
-    shared_part, second_other, returned, back_queries = lax.optimization_barrier(
-        (shared_part, expert_other[1], returned, back_queries)
-    )
-    back_both = jnp.concatenate(
-        [back_queries, back_kvpre, jnp.zeros((tok, 64), bf16)], axis=1
-    )
-    back_one = pair_sum(
-        jnp.concatenate([matmul_nt(back_both, own_a), matmul_nt(back_both, sib_a)], axis=1),
-        "tensor",
-    )
-    back_innorm, grad_gain_one = rms_backward(inputs, inverse_one, gain_one, back_one)
-    input_grad = unpermute(back_mid + back_innorm)
-
-    routed = matmul_tn(weight_hi, returned) + matmul_tn(weight_lo, returned)
-    output = unpermute(mid) + pair_sum(unpermute(s_part) + routed, "tensor")
-
-    h_one_pair = both_cores(h_one[:, :half], swapped(h_one[:, half:], "core"))
-    attn_pair = both_cores(back_attn[:, :half], swapped(back_attn[:, half:], "core"))
-    heads_pair = both_cores(o_heads, swapped(o_heads, "core"))
-    back_pair = both_cores(back_both[:, :2112], swapped(back_both[:, :2112], "core"))
-    rows_ql = matmul_tn(h_one_pair, back_pair)
-    rows_out = matmul_tn(attn_pair, heads_pair)
-    expand_mine = lax.dynamic_slice_in_dim(grad_expand, core * 256, 256, 0)
-    expand_theirs = lax.dynamic_slice_in_dim(grad_expand, 256 - core * 256, 256, 0)
-    rows_expand = expand_mine.astype(f32) + swapped(expand_theirs, "core").astype(f32)
-    rows_expand = rows_expand.reshape(1024, 512)
-    mid_low = matmul_nt(perm_m, grad_gain_mid.astype(bf16)[None, :])
-    gain_cols = jnp.concatenate([grad_gain_one[:, None], grad_gain_two[:, None], mid_low], axis=1)
-    gain_low = gain_cols.astype(bf16)
-    rows_gain = gain_low[:half].astype(f32) + swapped(gain_low[half:], "core").astype(f32)
-    attn_rows = jnp.concatenate(
-        [rows_ql, jnp.pad(rows_gain, ((0, 0), (0, 61))), rows_expand, rows_out], axis=1
+    kv_pair = both_cores(back_kvpre, swapped(back_kvpre, "core"))
+    mid_low = grad_gain_mid.astype(bf16)
+    mid_sum = (mid_low.astype(f32) + swapped(mid_low, "core").astype(f32)).astype(bf16)
+    mid_col = matmul_nt(perm_m[:half], jnp.broadcast_to(mid_sum[None, :], (64, LATENT)))
+    mid_col = matmul_tn(places[2], mid_col.astype(bf16))
+    rows_l = jnp.concatenate([matmul_tn(h_orders[2], kv_pair), mid_col], axis=1)
+    rows_l = rows_l.astype(bf16).reshape(4, 4, 64, 640)
+
+    got, keeps, rows_l, gate_got[1], back_mid, returned, gate_low, up_low_grad = together(
+        got, keeps, rows_l, gate_got[1], back_mid, returned, gate_low, up_low_grad
+    )
+    out_low = local_kernel(
+        routed_kernel,
+        "routed",
+        4,
+        [
+            scalar_spec(),
+            pl.BlockSpec((slots // 4, tok), lambda i: (i, 0)),
+            pl.BlockSpec((slots // 4, D), lambda i: (i, 0)),
+            whole((tok, D)),
+        ],
+        whole((tok, D)),
+        jax.ShapeDtypeStruct((tok, D), bf16),
+        [pltpu.VMEM((tok, D), f32)],
+        flops=4 * slots * tok * D,
+        moved=6 << 20,
+    )(core_at, slot_weight, returned, s_part)
+    near = [add_low(k[0], g[0]) for k, g in zip(keeps, got)]
+    far = [add_low(k[1], g[1]) for k, g in zip(keeps, got)]
+
+    got = [xored(r, *steps[1]) for r, steps in zip(far, first_steps)]
+    got_l = xored(rows_l[:2], "y", 1)
+    got, near, got_l, rows_l, out_low, gate_low, back_qnope, back_rope, back_kvpre, up_got[0] = together(
+        got, near, got_l, rows_l, out_low, gate_low, back_qnope, back_rope, back_kvpre, up_got[0]
+    )
+    back_lane = jnp.concatenate([back_rope, back_kvpre, jnp.zeros((tok, 64), bf16)], axis=1)
+    q_back = [matmul_nt(back_qnope, w) for w in q_parts]
+    l_back = [matmul_nt(back_lane, w) for w in l_parts]
+    one_part = jnp.concatenate(
+        [
+            join_low(q_back[0], q_back[1]) + join_outer(l_back[0], l_back[1]),
+            join_low(q_back[2], q_back[3]) + join_outer(l_back[2], l_back[3]),
+        ],
+        axis=1,
     ).astype(bf16)
-    attn_part = lax.psum_scatter(attn_rows, PLANE, scatter_dimension=0, tiled=True)
-    attn_part, third_other = lax.optimization_barrier((attn_part, expert_other[2]))
-    attn_grads = finish_rows(attn_part, dp)
+
+    one_other = swapped(one_part, "tensor")
+    out_other = swapped(out_low, "tensor")
+    gate_sum = summed(gate_low, gate_got, 0)
+    rows = [add_low(n, g) for n, g in zip(near, got)]
+    near_l, far_l = add_low(rows_l[2], got_l[0]), add_low(rows_l[3], got_l[1])
+    got_l = xored(far_l, "y", 3)
+
+    def owned(blocks, axis):
+        blocks = blocks.reshape(8, 32, blocks.shape[2])
+        blocks = lax.all_to_all(blocks, (axis, "dp"), split_axis=0, concat_axis=0, tiled=True)
+        return jnp.sum(blocks.astype(f32), axis=0)
+
+    from_y = owned(jnp.concatenate(rows[:2], axis=2), "y")
+    got_l, near_l, rows, from_y, gate_sum, shared_part, one_part, out_other, out_low, up_got[1] = together(
+        got_l, near_l, rows, from_y, gate_sum, shared_part, one_part, out_other, out_low, up_got[1]
+    )
+    from_z = owned(jnp.concatenate(rows[2:] + [add_low(near_l, got_l)], axis=2), "z")
+    l_sum = from_z[:, 1408:]
+
+
+    got = [xored(r, *steps[1]) for r, steps in zip(far, first_steps)]
+    got_l = xored(rows_l[:2], "y", 1)
+    got, near, got_l, rows_l, out_low, gate_low, back_qnope, back_rope, back_kvpre, up_got[0] = together(
+        got, near, got_l, rows_l, out_low, gate_low, back_qnope, back_rope, back_kvpre, up_got[0]
+    )
+    back_lane = jnp.concatenate([back_rope, back_kvpre, jnp.zeros((tok, 64), bf16)], axis=1)
+    q_back = [matmul_nt(back_qnope, w) for w in q_parts]
+    l_back = [matmul_nt(back_lane, w) for w in l_parts]
+    one_part = jnp.concatenate(
+        [
+            join_low(q_back[0], q_back[1]) + join_outer(l_back[0], l_back[1]),
+            join_low(q_back[2], q_back[3]) + join_outer(l_back[2], l_back[3]),
+        ],
+        axis=1,
+    ).astype(bf16)
+
+    one_other = swapped(one_part, "tensor")
+    out_other = swapped(out_low, "tensor")
+    gate_sum = summed(gate_low, gate_got, 0)
+    rows = [add_low(n, g) for n, g in zip(near, got)]
+    near_l, far_l = add_low(rows_l[2], got_l[0]), add_low(rows_l[3], got_l[1])
+    got_l = xored(far_l, "y", 3)
+
+    def owned(blocks, axis):
+        blocks = blocks.reshape(8, 32, blocks.shape[2])
+        blocks = lax.all_to_all(blocks, (axis, "dp"), split_axis=0, concat_axis=0, tiled=True)
+        return jnp.sum(blocks.astype(f32), axis=0)
+
+    from_y = owned(jnp.concatenate(rows[:2], axis=2), "y")
+    got_l, near_l, rows, from_y, gate_sum, shared_part, one_part, out_other, out_low, up_got[1] = together(
+        got_l, near_l, rows, from_y, gate_sum, shared_part, one_part, out_other, out_low, up_got[1]
+    )
+    from_z = owned(jnp.concatenate(rows[2:] + [add_low(near_l, got_l)], axis=2), "z")
+    l_sum = from_z[:, 1408:]
+
+    back_one = one_part.astype(f32) + one_other.astype(f32)
+    back_innorm, _ = rms_backward(inputs, inverse_one, gain_one, back_one)
+    input_grad = local_kernel(
+        grad_kernel,
+        "input_order",
+        1,
+        [scalar_spec(), whole((tok, D))],
+        whole((tok, D)),
+        jax.ShapeDtypeStruct((tok, D), f32),
+    )(core_at, back_mid + back_innorm)
+
+    output = local_kernel(
+        leave_kernel,
+        "leave",
+        1,
+        [scalar_spec()] + [whole((tok, D))] * 3,
+        whole((tok, D)),
+        jax.ShapeDtypeStruct((tok, D), bf16),
+    )(core_at, mid, out_low, out_other)
+
     shared_grads = finish_rows(shared_part, dp)
-    expert_grads = tuple(
-        mine.astype(f32) + other.astype(f32)
-        for mine, other in zip(expert_low, (first_other, second_other, third_other))
-    )
-    latent_gain = attn_grads[:, 1536:2176]
-    replicated = latent_gain.at[:, 577].multiply(0.5).at[:, 576].multiply(0.5)
-    replicated = pair_sum(replicated, "tensor")
+    out_grads = jnp.concatenate([from_y[:, 1536:], from_z[:, :768]], axis=1)
+    weight_dots = jnp.sum(from_y[:, :1536] * pack[:, :1536].astype(f32), axis=1) + jnp.sum(
+        l_sum[:, :576] * pack[:, 1536:2112].astype(f32), axis=1
+    )
+    small = jnp.concatenate(
+        [
+            l_sum,
+            (weight_dots / prenorm.astype(f32))[:, None],
+            0.5 * from_z[:, 768:769],
+            jnp.zeros((32, 126), f32),
+        ],
+        axis=1,
+    )
+    small = small + swapped(small, "tensor")
     query_grad = jnp.concatenate(
         [
-            attn_grads[:, :1024].reshape(32, heads, QN),
-            attn_grads[:, 1024:1280].reshape(32, heads, 32),
-            attn_grads[:, 1280:1536].reshape(32, heads, 32),
+            from_y[:, :1024].reshape(32, heads, QN),
+            from_y[:, 1024:1280].reshape(32, heads, 32),
+            from_y[:, 1280:1536].reshape(32, heads, 32),
         ],
         axis=2,
     ).reshape(32, heads * (QN + QR))
-    latent_cols = replicated[:, :LATENT].reshape(32, 2, 16, 2, 8).transpose(0, 3, 2, 1, 4)
+    latent_cols = small[:, :LATENT].reshape(32, 2, 16, 2, 8).transpose(0, 3, 2, 1, 4)
     latent_grad = jnp.concatenate(
-        [latent_cols.reshape(32, LATENT), replicated[:, LATENT : LATENT + QR]], axis=1
+        [latent_cols.reshape(32, LATENT), small[:, LATENT : LATENT + QR]], axis=1
     )
 
     return (
-        output.astype(bf16),
+        output,
         input_grad,
-        replicated[:, 576],
+        small[:, 640],
         query_grad,
         latent_grad,
-        replicated[:8, 578],
-        attn_grads[:, 2176:2688].reshape(8, 2048),
-        attn_grads[:, 2688:].T,
-        replicated[:, 577],
+        small[:8, 576],
+        from_z[:, 896:1408].reshape(8, 2048),
+        out_grads.T,
+        small[:, 641],
         shared_grads[:, :fs],
         shared_grads[:, fs : 2 * fs],
         shared_grads[:, 2 * fs :].T,
-        expert_grads[0][None],
-        expert_grads[1][None],
-        expert_grads[2][None],
+        gate_sum[None],
+        summed(up_low_grad, up_got, 0)[None],
+        down_sum[None],
     )
 
 

time: 864 us -> 680 us (0.79)
  waiting for transfers between devices: 408 us -> 182 us
  starting transfers between devices: 69 us -> 136 us
  matrix products: 172 us -> 133 us
  other arithmetic: 75.3 us -> 100 us
  local copies, waits for them, and re-layouts: 74.4 us -> 50.5 us
  Pallas kernels: 36.6 us -> 49.9 us
    all_gather x3 -> x1, waiting for transfers between devices: 181 us -> 0.01 us  [shards(): own_c = lax.all_gather(pair_c, PLANE, axis=0, tiled=True)]
    all_to_all x4, waiting for transfers between devices: 78.9 us -> 8.21 us  [exchange(): lax.all_to_all(blocks, EXPERT, split_axis=0, concat_axis=0, tiled=True)]
    ppermute x0 -> x26, starting transfers between devices: none -> 41.1 us  [xored(): return lax.ppermute(block, axis, [(i, i ^ k) for i in range(4)])]
    dot_general x20 -> x19, matrix products: 71.1 us -> 39.5 us  [matmul_nt(): lax.dot_general(left_op, right_op, (((1,), (1,)), ((), ())), preferred_el...]
    ppermute x0 -> x26, waiting for transfers between devices: none -> 30.3 us  [xored(): return lax.ppermute(block, axis, [(i, i ^ k) for i in range(4)])]
    all_to_all x0 -> x2, waiting for transfers between devices: none -> 23.3 us  [owned(): lax.all_to_all(blocks, (axis, 'dp'), split_axis=0, concat_axis=0, tiled=T...]
    ppermute x27 -> x36, waiting for transfers between devices: 133 us -> 110 us  [swapped(): return lax.ppermute(block, axis, [(0, 1), (1, 0)])]
    convert_element_type x6 -> x20, other arithmetic: 3.5 us -> 24.5 us  [the longest x11 12.7 us: add_low(): return (left.astype(f32) + right.astype(f32)).astype(bf16)]
  transfers between devices with their start and end apart: 44 -> 78, of which waited for: 19 -> 23; matrix products, arithmetic and copies ran while one was open for 33% -> 33% of each run, Pallas kernels for 4% -> 7%
where the time goes in v3:
time: 680 us; the launch traced here: 669 us
  waiting for transfers between devices  182 us (27%)
  starting transfers between devices  136 us (20%)
  matrix products  133 us (20%)
  other arithmetic  100 us (15%)
  local copies, waits for them, and re-layouts  50.5 us (7%)
  Pallas kernels  49.9 us (7%)
  between operations  17.4 us (3%)
    ppermute x36, waiting for transfers between devices, swapped(): return lax.ppermute(block, axis, [(0, 1), (1, 0)])  110 us
    dot_general x24, matrix products, matmul(): return jnp.dot(left_op, right_op, preferred_element_type=f32)  48 us
    dot_general x20, matrix products, matmul_tn(): lax.dot_general(left_op, right_op, (((0,), (0,)), ((), ())), preferred_el...  45.3 us
    ppermute x26, starting transfers between devices, xored(): return lax.ppermute(block, axis, [(i, i ^ k) for i in range(4)])  41.1 us
    dot_general x19, matrix products, matmul_nt(): lax.dot_general(left_op, right_op, (((1,), (1,)), ((), ())), preferred_el...  39.5 us
    all_to_all x4, starting transfers between devices, exchange(): lax.all_to_all(blocks, EXPERT, split_axis=0, concat_axis=0, tiled=True)  36.9 us
    ppermute x26, waiting for transfers between devices, xored(): return lax.ppermute(block, axis, [(i, i ^ k) for i in range(4)])  30.3 us
    ppermute x36, starting transfers between devices, swapped(): return lax.ppermute(block, axis, [(0, 1), (1, 0)])  26.5 us
  transfers between devices with their start and end apart: 78, of which 23 were waited for; matrix products, arithmetic and copies ran while one was open for 33% of the time, Pallas kernels for 7%

profile of v3, /device:TPU:0, one launch (start us, length us, event | category | flops | bytes accessed | tf_op | source)
XLA Modules:
  0.0 669.3 jit_solution(14387106693950296888)
XLA Ops:
  31.1 3.1 collective-permute-start.4
  50.0 2.6 collective-permute-start.6
  65.3 2.7 collective-permute-start.11
  71.1 6.9 %collective-permute-done.13 = bf16[4,1,16,2048]{3,2,1,0:T(8,128)(2,1)S(1)} collective-permute-done((bf16[4,1,16,2048]{3,2,1,0:T(8,128)(2,1)S(1)}, bf16[4,1,16,2048]{3,2,1,0:T(8,128)(2,1)S(1)}, u32[]{:S(2)}, u32[]{:S(2)}) %collective-permute-start.13) | collective-permute-done | bytes 262176 | tf_op jit(solution)/shard_map/ppermute | solution.py:100
  79.4 2.7 collective-permute-start.14
  87.5 5.7 collective-permute-done.17
  93.2 5.1 collective-permute-done.16
  99.0 3.2 collective-permute-done.15
  105.2 4.8 all-to-all-start
  127.7 3.5 collective-permute-start.23
  131.3 4.6 collective-permute-start.22
  135.9 3.6 collective-permute-start.21
  145.3 3.4 collective-permute-start.20
  161.8 12.2 %attend.1 = (bf16[8,128,640]{2,1,0:T(8,128)(2,1)S(1)}, bf16[8,128,512]{2,1,0:T(8,128)(2,1)S(1)}, bf16[128,1024]{1,0:T(8,128)(2,1)S(1)}, f32[8,128,128]{2,1,0:T(8,128)S(1)}) custom-call(bf16[128,1024]{1,0:T(8,128)(2,1)S(1)} %copy-done.19, bf16[128,512]{1,0:T(8,128)(2,1)S(1)} %pad_maximum_fusion.53.rope_ref, bf16[512,2048]{1,0:T(8,128)(2,1)} %pad_maximum_fusion.4.w_ref, ...), custom_call_target="tpu_custom_call" | custom-call | flops 2831155200 | bytes 12582912 | tf_op jit(solution)/shard_map/attend/pallas_call | solution.py:374
  174.1 3.5 convolution_convert_fusion.22
  177.6 2.6 convolution_convert_fusion.21
  180.3 3.2 collective-permute-start.29
  186.5 9.4 %collective-permute-done.29 = bf16[128,2048]{1,0:T(8,128)(2,1)S(1)} collective-permute-done((bf16[128,2048]{1,0:T(8,128)(2,1)S(1)}, bf16[128,2048]{1,0:T(8,128)(2,1)S(1)}, u32[]{:S(2)}, u32[]{:S(2)}) %collective-permute-start.29) | collective-permute-done | bytes 524320 | tf_op jit(solution)/shard_map/ppermute | solution.py:29
  202.2 3.0 fusion.23
  205.2 4.9 fusion.2
  212.5 3.1 collective-permute-start.35
  215.6 14.0 %all-to-all-start.1 = ((bf16[32,32,2048]{2,1,0:T(8,128)(2,1)}), bf16[32,32,2048]{2,1,0:T(8,128)(2,1)}, u32[]{:S(2)}, u32[]{:S(2)}) async-start(bf16[32,32,2048]{2,1,0:T(8,128)(2,1)} %bitcast.226), calls=%async_computation.1 | async-start | bytes 8388608 | tf_op jit(solution)/shard_map/all_to_all | solution.py:580
  236.2 25.7 %collective-permute-done.35 = bf16[1024,1024]{1,0:T(8,128)(2,1)} collective-permute-done((bf16[1024,1024]{1,0:T(8,128)(2,1)}, bf16[1024,1024]{1,0:T(8,128)(2,1)}, u32[]{:S(2)}, u32[]{:S(2)}) %collective-permute-start.35) | collective-permute-done | bytes 2097184 | tf_op jit(solution)/shard_map/ppermute | solution.py:29
  270.6 2.7 convolution_convert_fusion
  273.3 4.1 pad_maximum_fusion
  277.4 5.0 all-to-all-done.1
  282.4 6.0 fusion.18
  288.4 5.0 fusion.12
  293.5 8.0 %multiply_convert_fusion = (bf16[1024,704]{0,1:T(8,128)(2,1)}, bf16[1024,704]{0,1:T(8,128)(2,1)S(1)}, bf16[1024,704]{0,1:T(8,128)(2,1)S(1)}) fusion(f32[1024,704]{0,1:T(8,128)S(1)} %fusion.12, f32[1024,704]{0,1:T(8,128)S(1)} %fusion.18, bf16[1024,2048]{1,0:T(8,128)(2,1)} %bitcast.48, bf16[1,2048,704]{1,2,0:T(8,128)(2,1)S(1)} %copy-done), kind=kOutput, calls=%fused_computation.37 | convolution fusion | flops 2963603456 | bytes 17170432 | tf_op jit(solution)/shard_map/dot_general | solution.py:39
  301.4 3.5 fusion.10
  305.0 5.4 add_convert_fusion
  310.4 9.0 %all-to-all-start.2 = ((bf16[32,32,2048]{2,1,0:T(8,128)(2,1)}), bf16[32,32,2048]{2,1,0:T(8,128)(2,1)}, u32[]{:S(2)}, u32[]{:S(2)}) async-start(bf16[32,32,2048]{2,1,0:T(8,128)(2,1)} %bitcast.248), calls=%async_computation.2 | async-start | bytes 8388608 | tf_op jit(solution)/shard_map/all_to_all | solution.py:580
  319.4 4.4 convolution_convert_fusion.3
  323.9 5.3 fusion.40
  333.9 5.0 convolution_convert_fusion.2
  339.2 4.5 fusion.46
  343.8 4.4 fusion.37
  348.3 4.4 fusion.43
  354.0 24.6 %collective-permute-done.36 = bf16[704,1536]{1,0:T(8,128)(2,1)} collective-permute-done((bf16[704,1536]{1,0:T(8,128)(2,1)S(1)}, bf16[704,1536]{1,0:T(8,128)(2,1)}, u32[]{:S(2)}, u32[]{:S(2)}) %collective-permute-start.36) | collective-permute-done | bytes 2162720 | tf_op jit(solution)/shard_map/ppermute | solution.py:29
  378.6 3.2 all-to-all-done.2
  381.8 4.2 combine.1
  386.0 2.9 collective-permute-start.38
  390.9 3.0 convolution_convert_fusion.10
  393.9 9.1 %all-to-all-start.3 = ((bf16[32,32,2048]{2,1,0:T(8,128)(2,1)}), bf16[32,32,2048]{2,1,0:T(8,128)(2,1)}, u32[]{:S(2)}, u32[]{:S(2)}) async-start(bf16[32,32,2048]{2,1,0:T(8,128)(2,1)} %bitcast.247), calls=%async_computation.4 | async-start | bytes 8388608 | tf_op jit(solution)/shard_map/all_to_all | solution.py:580
  412.7 23.7 %attend_back.1 = (bf16[512,2048]{1,0:T(8,128)(2,1)}, bf16[128,1024]{1,0:T(8,128)(2,1)S(1)}, bf16[128,512]{1,0:T(8,128)(2,1)S(1)}, f32[640,640]{1,0:T(8,128)}, bf16[512,640]{1,0:T(8,128)(2,1)S(1)}) custom-call(bf16[128,1024]{1,0:T(8,128)(2,1)S(1)} %fusion.53.bh_ref, bf16[512,2048]{1,0:T(8,128)(2,1)} %pad_maximum_fusion.4.w_ref, bf16[1152,640]{1,0:T(8,128)(2,1)} %bitcast.230, ...), custom_call_target="tpu_custom_call" | custom-call | flops 7549747200 | bytes 20971520 | tf_op jit(solution)/shard_map/attend_back/pallas_call | solution.py:406
  454.2 4.2 convert_add_fusion.2
  464.3 10.3 %collective-permute-done.46 = bf16[128,640]{1,0:T(8,128)(2,1)} collective-permute-done((bf16[128,640]{1,0:T(8,128)(2,1)}, bf16[128,640]{1,0:T(8,128)(2,1)}, u32[]{:S(2)}, u32[]{:S(2)}) %collective-permute-start.46) | collective-permute-done | bytes 163872 | tf_op jit(solution)/shard_map/ppermute | solution.py:35
  480.3 2.5 convolution_convert_fusion.6
  485.4 12.8 %collective-permute-done.57 = bf16[1024,704]{0,1:T(8,128)(2,1)} collective-permute-done((bf16[1024,704]{0,1:T(8,128)(2,1)}, bf16[1024,704]{0,1:T(8,128)(2,1)}, u32[]{:S(2)}, u32[]{:S(2)}) %collective-permute-start.57) | collective-permute-done | bytes 1441824 | tf_op jit(solution)/shard_map/ppermute | solution.py:29
  498.2 10.1 %collective-permute-start.54 = (bf16[2,4,64,512]{3,2,1,0:T(8,128)(2,1)}, bf16[2,4,64,512]{3,2,1,0:T(8,128)(2,1)}, u32[]{:S(2)}, u32[]{:S(2)}) collective-permute-start(bf16[2,4,64,512]{3,2,1,0:T(8,128)(2,1)} %slice.546), channel_id=1, source_target_pairs={{0,48},{16,32},{32,16},{48,0},{1,49},{17,33},{33,17},{49,1},{2,50}... | collective-permute-start | bytes 1572872 | tf_op jit(solution)/shard_map/ppermute | solution.py:100
  511.3 2.6 convolution_convert_fusion.5
  528.7 3.0 collective-permute-start.60
  533.5 12.3 %collective-permute-done.62 = bf16[1024,704]{0,1:T(8,128)(2,1)} collective-permute-done((bf16[1024,704]{0,1:T(8,128)(2,1)}, bf16[1024,704]{0,1:T(8,128)(2,1)}, u32[]{:S(2)}, u32[]{:S(2)}) %collective-permute-start.62) | collective-permute-done | bytes 1441824 | tf_op jit(solution)/shard_map/ppermute | solution.py:29
  545.9 4.5 routed.1.part_ref
  550.4 4.7 collective-permute-done.61
  556.5 17.1 %collective-permute-done.64 = bf16[1024,704]{0,1:T(8,128)(2,1)} collective-permute-done((bf16[1024,704]{0,1:T(8,128)(2,1)}, bf16[1024,704]{0,1:T(8,128)(2,1)}, u32[]{:S(2)}, u32[]{:S(2)}) %collective-permute-start.64) | collective-permute-done | bytes 1441824 | tf_op jit(solution)/shard_map/ppermute | solution.py:29
  586.8 2.6 collective-permute-start.67
  591.7 4.4 all-to-all-start.4
  596.1 4.7 convert_add_fusion.1
  602.5 18.8 %all-to-all-done.4 = bf16[8,32,1792]{2,1,0:T(8,128)(2,1)} async-done(((bf16[8,32,1792]{2,1,0:T(8,128)(2,1)}), bf16[8,32,1792]{2,1,0:T(8,128)(2,1)}, u32[]{:S(2)}, u32[]{:S(2)}) %all-to-all-start.4) | async-done | bytes 917536 | tf_op jit(solution)/shard_map/all_to_all | solution.py:992
  632.8 6.1 all-to-all-start.5
  640.2 4.7 convert_add_fusion
  646.8 4.5 all-to-all-done.5
  655.7 4.1 collective-permute-done.68
  (749 shorter events, 236.9 us)
Async XLA Ops:
  7.2 194.9 %all-gather.2.cloned.1.call-start = ((), (), s32[]{:S(2)}) async-start(), calls=%async_computation.7 | async-start | bytes 9191424 | tf_op jit(solution)/shard_map/all_gather | solution.py:630
  20.7 18.8 %collective-permute-start.5 = (bf16[32,4224]{1,0:T(8,128)(2,1)}, bf16[32,4224]{1,0:T(8,128)(2,1)}, u32[]{:S(2)}, u32[]{:S(2)}) collective-permute-start(bf16[32,4224]{1,0:T(8,128)(2,1)} %pad_maximum_fusion.40), channel_id=1, source_target_pairs={{0,64},{64,0},{1,65},{65,1},{2,66},{66,2},{3,67},{67,3},{4,68},{68... | collective-permute-start | bytes 811016 | tf_op jit(solution)/shard_map/ppermute | solution.py:29
  31.1 10.3 %collective-permute-start.4 = (bf16[1,1,16,2048]{3,2,1,0:T(8,128)(2,1)}, bf16[1,1,16,2048]{3,2,1,0:T(8,128)(2,1)}, u32[]{:S(2)}, u32[]{:S(2)}) collective-permute-start(bf16[1,1,16,2048]{3,2,1,0:T(8,128)(2,1)} %reshape.701), channel_id=1, source_target_pairs={{0,48},{16,32},{32,16},{48,0},{1,49},{17,33},{33,17},{49,1},{2,50}... | collective-permute-start | bytes 196616 | tf_op jit(solution)/shard_map/ppermute | solution.py:100
  46.9 15.4 %collective-permute-start.9 = (bf16[2,1,16,2048]{3,2,1,0:T(8,128)(2,1)S(1)}, bf16[2,1,16,2048]{3,2,1,0:T(8,128)(2,1)S(1)}, u32[]{:S(2)}, u32[]{:S(2)}) collective-permute-start(bf16[2,1,16,2048]{3,2,1,0:T(8,128)(2,1)S(1)} %pad_maximum_fusion.50), channel_id=1, source_target_pairs={{0,16},{16,0},{32,48},{48,32},{1,17},{17,1},{33,49},{49,33},{2,18}... | collective-permute-start | bytes 393224 | tf_op jit(solution)/shard_map/ppermute | solution.py:100
  50.0 12.4 %collective-permute-start.6 = (bf16[1,2,64,1024]{3,2,1,0:T(8,128)(2,1)S(1)}, bf16[1,2,64,1024]{3,2,1,0:T(8,128)(2,1)S(1)}, u32[]{:S(2)}, u32[]{:S(2)}) collective-permute-start(bf16[1,2,64,1024]{3,2,1,0:T(8,128)(2,1)S(1)} %pad_maximum_fusion.41), channel_id=1, source_target_pairs={{0,12},{4,8},{8,4},{12,0},{1,13},{5,9},{9,5},{13,1},{2,14},{6,10},... | collective-permute-start | bytes 786440 | tf_op jit(solution)/shard_map/ppermute | solution.py:100
  52.6 9.8 %collective-permute-start.8 = (bf16[2,1,64,1024]{3,2,1,0:T(8,128)(2,1)S(1)}, bf16[2,1,64,1024]{3,2,1,0:T(8,128)(2,1)S(1)}, u32[]{:S(2)}, u32[]{:S(2)}) collective-permute-start(bf16[2,1,64,1024]{3,2,1,0:T(8,128)(2,1)S(1)} %pad_maximum_fusion.42), channel_id=1, source_target_pairs={{0,48},{16,32},{32,16},{48,0},{1,49},{17,33},{33,17},{49,1},{2,50}... | collective-permute-start | bytes 786440 | tf_op jit(solution)/shard_map/ppermute | solution.py:100
  62.5 15.6 %collective-permute-start.12 = (bf16[4,1,64,1024]{3,2,1,0:T(8,128)(2,1)S(1)}, bf16[4,1,64,1024]{3,2,1,0:T(8,128)(2,1)S(1)}, u32[]{:S(2)}, u32[]{:S(2)}) collective-permute-start(bf16[4,1,64,1024]{3,2,1,0:T(8,128)(2,1)S(1)} %pad_maximum_fusion.24), channel_id=1, source_target_pairs={{0,4},{4,0},{8,12},{12,8},{1,5},{5,1},{9,13},{13,9},{2,6},{6,2},{1... | collective-permute-start | bytes 1572872 | tf_op jit(solution)/shard_map/ppermute | solution.py:100
  64.7 13.4 %collective-permute-start.10 = (bf16[1,4,64,1024]{3,2,1,0:T(8,128)(2,1)S(1)}, bf16[1,4,64,1024]{3,2,1,0:T(8,128)(2,1)S(1)}, u32[]{:S(2)}, u32[]{:S(2)}) collective-permute-start(bf16[1,4,64,1024]{3,2,1,0:T(8,128)(2,1)S(1)} %pad_maximum_fusion.23), channel_id=1, source_target_pairs={{0,16},{16,0},{32,48},{48,32},{1,17},{17,1},{33,49},{49,33},{2,18}... | collective-permute-start | bytes 1572872 | tf_op jit(solution)/shard_map/ppermute | solution.py:100
  65.3 12.8 %collective-permute-start.11 = (bf16[1,4,64,1152]{3,2,1,0:T(8,128)(2,1)S(1)}, bf16[1,4,64,1152]{3,2,1,0:T(8,128)(2,1)S(1)}, u32[]{:S(2)}, u32[]{:S(2)}) collective-permute-start(bf16[1,4,64,1152]{3,2,1,0:T(8,128)(2,1)S(1)} %pad_maximum_fusion.20), channel_id=1, source_target_pairs={{0,48},{16,32},{32,16},{48,0},{1,49},{17,33},{33,17},{49,1},{2,50}... | collective-permute-start | bytes 1769480 | tf_op jit(solution)/shard_map/ppermute | solution.py:100
  68.1 9.9 %collective-permute-start.13 = (bf16[4,1,16,2048]{3,2,1,0:T(8,128)(2,1)S(1)}, bf16[4,1,16,2048]{3,2,1,0:T(8,128)(2,1)S(1)}, u32[]{:S(2)}, u32[]{:S(2)}) collective-permute-start(bf16[4,1,16,2048]{3,2,1,0:T(8,128)(2,1)S(1)} %pad_maximum_fusion.43), channel_id=1, source_target_pairs={{0,12},{4,8},{8,4},{12,0},{1,13},{5,9},{9,5},{13,1},{2,14},{6,10},... | collective-permute-start | bytes 786440 | tf_op jit(solution)/shard_map/ppermute | solution.py:100
  78.3 20.0 %collective-permute-start.16 = (bf16[4,2,64,1024]{3,2,1,0:T(8,128)(2,1)S(1)}, bf16[4,2,64,1024]{3,2,1,0:T(8,128)(2,1)S(1)}, u32[]{:S(2)}, u32[]{:S(2)}) collective-permute-start(bf16[4,2,64,1024]{3,2,1,0:T(8,128)(2,1)S(1)} %pad_maximum_fusion.10), channel_id=1, source_target_pairs={{0,12},{4,8},{8,4},{12,0},{1,13},{5,9},{9,5},{13,1},{2,14},{6,10},... | collective-permute-start | bytes 3145736 | tf_op jit(solution)/shard_map/ppermute | solution.py:100
  79.4 19.6 %collective-permute-start.14 = (bf16[2,4,64,1024]{3,2,1,0:T(8,128)(2,1)S(1)}, bf16[2,4,64,1024]{3,2,1,0:T(8,128)(2,1)S(1)}, u32[]{:S(2)}, u32[]{:S(2)}) collective-permute-start(bf16[2,4,64,1024]{3,2,1,0:T(8,128)(2,1)S(1)} %pad_maximum_fusion.9), channel_id=1, source_target_pairs={{0,48},{16,32},{32,16},{48,0},{1,49},{17,33},{33,17},{49,1},{2,50}... | collective-permute-start | bytes 3145736 | tf_op jit(solution)/shard_map/ppermute | solution.py:100
  82.4 19.8 %collective-permute-start.15 = (bf16[2,4,64,1152]{3,2,1,0:T(8,128)(2,1)S(1)}, bf16[2,4,64,1152]{3,2,1,0:T(8,128)(2,1)S(1)}, u32[]{:S(2)}, u32[]{:S(2)}) collective-permute-start(bf16[2,4,64,1152]{3,2,1,0:T(8,128)(2,1)S(1)} %pad_maximum_fusion.7), channel_id=1, source_target_pairs={{0,16},{16,0},{32,48},{48,32},{1,17},{17,1},{33,49},{49,33},{2,18}... | collective-permute-start | bytes 3538952 | tf_op jit(solution)/shard_map/ppermute | solution.py:100
  83.9 9.3 %collective-permute-start.17 = (bf16[4,2,16,2048]{3,2,1,0:T(8,128)(2,1)S(1)}, bf16[4,2,16,2048]{3,2,1,0:T(8,128)(2,1)S(1)}, u32[]{:S(2)}, u32[]{:S(2)}) collective-permute-start(bf16[4,2,16,2048]{3,2,1,0:T(8,128)(2,1)S(1)} %pad_maximum_fusion.25), channel_id=1, source_target_pairs={{0,4},{4,0},{8,12},{12,8},{1,5},{5,1},{9,13},{13,9},{2,6},{6,2},{1... | collective-permute-start | bytes 1572872 | tf_op jit(solution)/shard_map/ppermute | solution.py:100
  104.5 12.9 %collective-permute-start.19 = (bf16[2,4,64,1152]{3,2,1,0:T(8,128)(2,1)}, bf16[2,4,64,1152]{3,2,1,0:T(8,128)(2,1)}, u32[]{:S(2)}, u32[]{:S(2)}) collective-permute-start(bf16[2,4,64,1152]{3,2,1,0:T(8,128)(2,1)} %copy-done.47), channel_id=1, source_target_pairs={{0,2},{2,0},{1,3},{3,1},{4,6},{6,4},{5,7},{7,5},{8,10},{10,8},{9,1... | collective-permute-start | bytes 3538952 | tf_op jit(solution)/shard_map/ppermute | solution.py:29
  104.6 40.6 %collective-permute-start.24 = (bf16[2,4,64,1024]{3,2,1,0:T(8,128)(2,1)}, bf16[2,4,64,1024]{3,2,1,0:T(8,128)(2,1)}, u32[]{:S(2)}, u32[]{:S(2)}) collective-permute-start(bf16[2,4,64,1024]{3,2,1,0:T(8,128)(2,1)} %copy-done.37), channel_id=1, source_target_pairs={{0,2},{2,0},{1,3},{3,1},{4,6},{6,4},{5,7},{7,5},{8,10},{10,8},{9,1... | collective-permute-start | bytes 3145736 | tf_op jit(solution)/shard_map/ppermute | solution.py:29
  105.1 13.4 %collective-permute-start.18 = (bf16[2,4,64,1152]{3,2,1,0:T(8,128)(2,1)}, bf16[2,4,64,1152]{3,2,1,0:T(8,128)(2,1)}, u32[]{:S(2)}, u32[]{:S(2)}) collective-permute-start(bf16[2,4,64,1152]{3,2,1,0:T(8,128)(2,1)} %copy-done.34), channel_id=1, source_target_pairs={{0,2},{2,0},{1,3},{3,1},{4,6},{6,4},{5,7},{7,5},{8,10},{10,8},{9,1... | collective-permute-start | bytes 3538952 | tf_op jit(solution)/shard_map/ppermute | solution.py:29
  105.2 54.0 %all-to-all-start = ((bf16[32,32,1024]{2,1,0:T(8,128)(2,1)}), bf16[32,32,1024]{2,1,0:T(8,128)(2,1)}, u32[]{:S(2)}, u32[]{:S(2)}) async-start(bf16[32,32,1024]{2,1,0:T(8,128)(2,1)} %bitcast.237), calls=%async_computation | async-start | bytes 4194304 | tf_op jit(solution)/shard_map/all_to_all | solution.py:580
  115.1 24.7 %collective-permute-start.25 = (bf16[2,4,64,1024]{3,2,1,0:T(8,128)(2,1)}, bf16[2,4,64,1024]{3,2,1,0:T(8,128)(2,1)}, u32[]{:S(2)}, u32[]{:S(2)}) collective-permute-start(bf16[2,4,64,1024]{3,2,1,0:T(8,128)(2,1)} %copy-done.54), channel_id=1, source_target_pairs={{0,2},{2,0},{1,3},{3,1},{4,6},{6,4},{5,7},{7,5},{8,10},{10,8},{9,1... | collective-permute-start | bytes 3145736 | tf_op jit(solution)/shard_map/ppermute | solution.py:29
  127.7 25.1 %collective-permute-start.23 = (bf16[128,640]{1,0:T(8,128)(2,1)S(1)}, bf16[128,640]{1,0:T(8,128)(2,1)S(1)}, u32[]{:S(2)}, u32[]{:S(2)}) collective-permute-start(bf16[128,640]{1,0:T(8,128)(2,1)S(1)} %pad_maximum_fusion.45), channel_id=1, source_target_pairs={{0,4},{4,8},{8,12},{12,16},{16,20},{20,24},{24,28},{28,32},{32,36}... | collective-permute-start | bytes 491528 | tf_op jit(solution)/shard_map/ppermute | solution.py:35
  131.3 21.6 %collective-permute-start.22 = (bf16[128,640]{1,0:T(8,128)(2,1)S(1)}, bf16[128,640]{1,0:T(8,128)(2,1)S(1)}, u32[]{:S(2)}, u32[]{:S(2)}) collective-permute-start(bf16[128,640]{1,0:T(8,128)(2,1)S(1)} %pad_maximum_fusion.45), channel_id=1, source_target_pairs={{0,8},{4,12},{8,16},{12,20},{16,24},{20,28},{24,32},{28,36},{32,40... | collective-permute-start | bytes 491528 | tf_op jit(solution)/shard_map/ppermute | solution.py:35
  135.9 17.0 %collective-permute-start.21 = (bf16[128,640]{1,0:T(8,128)(2,1)S(1)}, bf16[128,640]{1,0:T(8,128)(2,1)S(1)}, u32[]{:S(2)}, u32[]{:S(2)}) collective-permute-start(bf16[128,640]{1,0:T(8,128)(2,1)S(1)} %pad_maximum_fusion.45), channel_id=1, source_target_pairs={{0,12},{4,16},{8,20},{12,24},{16,28},{20,32},{24,36},{28,40},{32,4... | collective-permute-start | bytes 491528 | tf_op jit(solution)/shard_map/ppermute | solution.py:35
  139.8 11.1 %collective-permute-start.26 = (bf16[256,2048]{1,0:T(8,128)(2,1)S(1)}, bf16[256,2048]{1,0:T(8,128)(2,1)S(1)}, u32[]{:S(2)}, u32[]{:S(2)}) collective-permute-start(bf16[256,2048]{1,0:T(8,128)(2,1)S(1)} %bitcast.246), channel_id=1, source_target_pairs={{0,2},{2,0},{1,3},{3,1},{4,6},{6,4},{5,7},{7,5},{8,10},{10,8},{9,1... | collective-permute-start | bytes 3145736 | tf_op jit(solution)/shard_map/ppermute | solution.py:29
  150.9 26.6 %collective-permute-start.28 = (bf16[1024,1024]{1,0:T(8,128)(2,1)}, bf16[1024,1024]{1,0:T(8,128)(2,1)}, u32[]{:S(2)}, u32[]{:S(2)}) collective-permute-start(bf16[1024,1024]{1,0:T(8,128)(2,1)} %bitcast.46), channel_id=1, source_target_pairs={{0,2},{2,0},{1,3},{3,1},{4,6},{6,4},{5,7},{7,5},{8,10},{10,8},{9,1... | collective-permute-start | bytes 6291464 | tf_op jit(solution)/shard_map/ppermute | solution.py:29
  154.7 47.4 %collective-permute-start.32 = (bf16[128,1024]{1,0:T(8,128)(2,1)}, bf16[128,1024]{1,0:T(8,128)(2,1)}, u32[]{:S(2)}, u32[]{:S(2)}) collective-permute-start(bf16[128,1024]{1,0:T(8,128)(2,1)} %get-tuple-element.537), channel_id=1, source_target_pairs={{0,2},{2,0},{1,3},{3,1},{4,6},{6,4},{5,7},{7,5},{8,10},{10,8},{9,1... | collective-permute-start | bytes 786440 | tf_op jit(solution)/shard_map/ppermute | solution.py:29
  180.3 15.6 %collective-permute-start.29 = (bf16[128,2048]{1,0:T(8,128)(2,1)S(1)}, bf16[128,2048]{1,0:T(8,128)(2,1)S(1)}, u32[]{:S(2)}, u32[]{:S(2)}) collective-permute-start(bf16[128,2048]{1,0:T(8,128)(2,1)S(1)} %pad_maximum_fusion.26), channel_id=1, source_target_pairs={{0,1},{1,0},{2,3},{3,2},{4,5},{5,4},{6,7},{7,6},{8,9},{9,8},{10,11... | collective-permute-start | bytes 1572872 | tf_op jit(solution)/shard_map/ppermute | solution.py:29
  212.1 17.6 %collective-permute-start.33 = (bf16[128,4224]{1,0:T(8,128)(2,1)}, bf16[128,4224]{1,0:T(8,128)(2,1)}, u32[]{:S(2)}, u32[]{:S(2)}) collective-permute-start(bf16[128,4224]{1,0:T(8,128)(2,1)} %fusion.28), channel_id=1, source_target_pairs={{0,2},{2,0},{1,3},{3,1},{4,6},{6,4},{5,7},{7,5},{8,10},{10,8},{9,1... | collective-permute-start | bytes 3244040 | tf_op jit(solution)/shard_map/ppermute | solution.py:29
  212.5 49.4 %collective-permute-start.35 = (bf16[1024,1024]{1,0:T(8,128)(2,1)}, bf16[1024,1024]{1,0:T(8,128)(2,1)}, u32[]{:S(2)}, u32[]{:S(2)}) collective-permute-start(bf16[1024,1024]{1,0:T(8,128)(2,1)} %bitcast.45), channel_id=1, source_target_pairs={{0,1},{1,0},{2,3},{3,2},{4,5},{5,4},{6,7},{7,6},{8,9},{9,8},{10,11... | collective-permute-start | bytes 6291464 | tf_op jit(solution)/shard_map/ppermute | solution.py:29
  215.6 66.8 %all-to-all-start.1 = ((bf16[32,32,2048]{2,1,0:T(8,128)(2,1)}), bf16[32,32,2048]{2,1,0:T(8,128)(2,1)}, u32[]{:S(2)}, u32[]{:S(2)}) async-start(bf16[32,32,2048]{2,1,0:T(8,128)(2,1)} %bitcast.226), calls=%async_computation.1 | async-start | bytes 8388608 | tf_op jit(solution)/shard_map/all_to_all | solution.py:580
  229.6 245.1 %reduce-scatter.2.cloned.1.call-start = ((), (), s32[]{:S(2)}) async-start(), calls=%async_computation.8 | async-start | bytes 9191424 | tf_op jit(solution)/shard_map/reduce_scatter | solution.py:744
  233.9 33.0 %collective-permute-start.34 = (bf16[128,4224]{1,0:T(8,128)(2,1)}, bf16[128,4224]{1,0:T(8,128)(2,1)}, u32[]{:S(2)}, u32[]{:S(2)}) collective-permute-start(bf16[128,4224]{1,0:T(8,128)(2,1)} %pad_maximum_fusion.8), channel_id=1, source_target_pairs={{0,2},{2,0},{1,3},{3,1},{4,6},{6,4},{5,7},{7,5},{8,10},{10,8},{9,1... | collective-permute-start | bytes 3244040 | tf_op jit(solution)/shard_map/ppermute | solution.py:29
  235.9 153.1 %collective-permute-start.43 = (bf16[128,1024]{1,0:T(8,128)(2,1)S(1)}, bf16[128,1024]{1,0:T(8,128)(2,1)}, u32[]{:S(2)}, u32[]{:S(2)}) collective-permute-start(bf16[128,1024]{1,0:T(8,128)(2,1)S(1)} %get-tuple-element.290), channel_id=1, source_target_pairs={{0,2},{2,0},{1,3},{3,1},{4,6},{6,4},{5,7},{7,5},{8,10},{10,8},{9,1... | collective-permute-start | bytes 786440 | tf_op jit(solution)/shard_map/ppermute | solution.py:29
  310.4 71.5 %all-to-all-start.2 = ((bf16[32,32,2048]{2,1,0:T(8,128)(2,1)}), bf16[32,32,2048]{2,1,0:T(8,128)(2,1)}, u32[]{:S(2)}, u32[]{:S(2)}) async-start(bf16[32,32,2048]{2,1,0:T(8,128)(2,1)} %bitcast.248), calls=%async_computation.2 | async-start | bytes 8388608 | tf_op jit(solution)/shard_map/all_to_all | solution.py:580
  329.2 49.4 %collective-permute-start.36 = (bf16[704,1536]{1,0:T(8,128)(2,1)S(1)}, bf16[704,1536]{1,0:T(8,128)(2,1)}, u32[]{:S(2)}, u32[]{:S(2)}) collective-permute-start(bf16[704,1536]{1,0:T(8,128)(2,1)S(1)} %convolution_convert_fusion.3), channel_id=1, source_target_pairs={{0,64},{64,0},{1,65},{65,1},{2,66},{66,2},{3,67},{67,3},{4,68},{68... | collective-permute-start | bytes 6488072 | tf_op jit(solution)/shard_map/ppermute | solution.py:29
  339.0 13.7 %collective-permute-start.37 = (bf16[128,2048]{1,0:T(8,128)(2,1)S(1)}, bf16[128,2048]{1,0:T(8,128)(2,1)S(1)}, u32[]{:S(2)}, u32[]{:S(2)}) collective-permute-start(bf16[128,2048]{1,0:T(8,128)(2,1)S(1)} %pad_maximum_fusion.22), channel_id=1, source_target_pairs={{0,2},{2,0},{1,3},{3,1},{4,6},{6,4},{5,7},{7,5},{8,10},{10,8},{9,1... | collective-permute-start | bytes 1572872 | tf_op jit(solution)/shard_map/ppermute | solution.py:29
  386.0 17.0 %collective-permute-start.38 = (bf16[128,2048]{1,0:T(8,128)(2,1)S(1)}, bf16[128,2048]{1,0:T(8,128)(2,1)S(1)}, u32[]{:S(2)}, u32[]{:S(2)}) collective-permute-start(bf16[128,2048]{1,0:T(8,128)(2,1)S(1)} %combine.1), channel_id=1, source_target_pairs={{0,1},{1,0},{2,3},{3,2},{4,5},{5,4},{6,7},{7,6},{8,9},{9,8},{10,11... | collective-permute-start | bytes 1572872 | tf_op jit(solution)/shard_map/ppermute | solution.py:29
  393.9 125.5 %all-to-all-start.3 = ((bf16[32,32,2048]{2,1,0:T(8,128)(2,1)}), bf16[32,32,2048]{2,1,0:T(8,128)(2,1)}, u32[]{:S(2)}, u32[]{:S(2)}) async-start(bf16[32,32,2048]{2,1,0:T(8,128)(2,1)} %bitcast.247), calls=%async_computation.4 | async-start | bytes 8388608 | tf_op jit(solution)/shard_map/all_to_all | solution.py:580
  405.5 30.9 %collective-permute-start.45 = (bf16[1024]{0:T(1024)(128)(2,1)S(1)}, bf16[1024]{0:T(1024)(128)(2,1)S(1)}, u32[]{:S(2)}, u32[]{:S(2)}) collective-permute-start(bf16[1024]{0:T(1024)(128)(2,1)S(1)} %slice.675), channel_id=1, source_target_pairs={{0,2},{2,0},{1,3},{3,1},{4,6},{6,4},{5,7},{7,5},{8,10},{10,8},{9,1... | collective-permute-start | bytes 6152 | tf_op jit(solution)/shard_map/ppermute | solution.py:29
  405.7 33.9 %collective-permute-start.44 = (bf16[128,1024]{1,0:T(8,128)(2,1)S(1)}, bf16[128,1024]{1,0:T(8,128)(2,1)S(1)}, u32[]{:S(2)}, u32[]{:S(2)}) collective-permute-start(bf16[128,1024]{1,0:T(8,128)(2,1)S(1)} %get-tuple-element.533), channel_id=1, source_target_pairs={{0,2},{2,0},{1,3},{3,1},{4,6},{6,4},{5,7},{7,5},{8,10},{10,8},{9,1... | collective-permute-start | bytes 786440 | tf_op jit(solution)/shard_map/ppermute | solution.py:29
  406.1 31.2 %collective-permute-start.39 = (bf16[704,512]{1,0:T(8,128)(2,1)S(1)}, bf16[704,512]{1,0:T(8,128)(2,1)S(1)}, u32[]{:S(2)}, u32[]{:S(2)}) collective-permute-start(bf16[704,512]{1,0:T(8,128)(2,1)S(1)} %copy-done.96), channel_id=1, source_target_pairs={{0,64},{64,0},{1,65},{65,1},{2,66},{66,2},{3,67},{67,3},{4,68},{68... | collective-permute-start | bytes 2162696 | tf_op jit(solution)/shard_map/ppermute | solution.py:29
  406.1 58.2 %collective-permute-start.50 = (bf16[1024,704]{0,1:T(8,128)(2,1)}, bf16[1024,704]{0,1:T(8,128)(2,1)}, u32[]{:S(2)}, u32[]{:S(2)}) collective-permute-start(bf16[1024,704]{0,1:T(8,128)(2,1)} %fusion.40), channel_id=1, source_target_pairs={{0,64},{64,0},{1,65},{65,1},{2,66},{66,2},{3,67},{67,3},{4,68},{68... | collective-permute-start | bytes 4325384 | tf_op jit(solution)/shard_map/ppermute | solution.py:29
  443.7 20.6 %collective-permute-start.49 = (bf16[128,640]{1,0:T(8,128)(2,1)}, bf16[128,640]{1,0:T(8,128)(2,1)}, u32[]{:S(2)}, u32[]{:S(2)}) collective-permute-start(bf16[128,640]{1,0:T(8,128)(2,1)} %get-tuple-element.511), channel_id=1, source_target_pairs={{4,0},{8,4},{12,8},{16,12},{20,16},{24,20},{28,24},{32,28},{36,32}... | collective-permute-start | bytes 491528 | tf_op jit(solution)/shard_map/ppermute | solution.py:35
  445.0 19.3 %collective-permute-start.48 = (bf16[128,640]{1,0:T(8,128)(2,1)}, bf16[128,640]{1,0:T(8,128)(2,1)}, u32[]{:S(2)}, u32[]{:S(2)}) collective-permute-start(bf16[128,640]{1,0:T(8,128)(2,1)} %get-tuple-element.512), channel_id=1, source_target_pairs={{8,0},{12,4},{16,8},{20,12},{24,16},{28,20},{32,24},{36,28},{40,32... | collective-permute-start | bytes 491528 | tf_op jit(solution)/shard_map/ppermute | solution.py:35
  446.3 18.0 %collective-permute-start.47 = (bf16[128,640]{1,0:T(8,128)(2,1)}, bf16[128,640]{1,0:T(8,128)(2,1)}, u32[]{:S(2)}, u32[]{:S(2)}) collective-permute-start(bf16[128,640]{1,0:T(8,128)(2,1)} %get-tuple-element.513), channel_id=1, source_target_pairs={{12,0},{16,4},{20,8},{24,12},{28,16},{32,20},{36,24},{40,28},{44,3... | collective-permute-start | bytes 491528 | tf_op jit(solution)/shard_map/ppermute | solution.py:35
  447.6 27.0 %collective-permute-start.46 = (bf16[128,640]{1,0:T(8,128)(2,1)}, bf16[128,640]{1,0:T(8,128)(2,1)}, u32[]{:S(2)}, u32[]{:S(2)}) collective-permute-start(bf16[128,640]{1,0:T(8,128)(2,1)} %get-tuple-element.514), channel_id=1, source_target_pairs={{16,0},{20,4},{24,8},{28,12},{32,16},{36,20},{40,24},{44,28},{48,3... | collective-permute-start | bytes 491528 | tf_op jit(solution)/shard_map/ppermute | solution.py:35
  464.3 33.9 %collective-permute-start.57 = (bf16[1024,704]{0,1:T(8,128)(2,1)}, bf16[1024,704]{0,1:T(8,128)(2,1)}, u32[]{:S(2)}, u32[]{:S(2)}) collective-permute-start(bf16[1024,704]{0,1:T(8,128)(2,1)} %fusion.46), channel_id=1, source_target_pairs={{0,64},{64,0},{1,65},{65,1},{2,66},{66,2},{3,67},{67,3},{4,68},{68... | collective-permute-start | bytes 4325384 | tf_op jit(solution)/shard_map/ppermute | solution.py:29
  476.6 34.3 %collective-permute-start.55 = (bf16[128,576]{1,0:T(8,128)(2,1)S(1)}, bf16[128,576]{1,0:T(8,128)(2,1)S(1)}, u32[]{:S(2)}, u32[]{:S(2)}) collective-permute-start(bf16[128,576]{1,0:T(8,128)(2,1)S(1)} %pad_maximum_fusion.46), channel_id=1, source_target_pairs={{0,2},{2,0},{1,3},{3,1},{4,6},{6,4},{5,7},{7,5},{8,10},{10,8},{9,1... | collective-permute-start | bytes 442376 | tf_op jit(solution)/shard_map/ppermute | solution.py:29
  484.0 35.4 %collective-permute-start.51 = (bf16[2,4,64,896]{3,2,1,0:T(8,128)(2,1)}, bf16[2,4,64,896]{3,2,1,0:T(8,128)(2,1)}, u32[]{:S(2)}, u32[]{:S(2)}) collective-permute-start(bf16[2,4,64,896]{3,2,1,0:T(8,128)(2,1)} %bitcast.55), channel_id=1, source_target_pairs={{0,4},{4,0},{8,12},{12,8},{1,5},{5,1},{9,13},{13,9},{2,6},{6,2},{1... | collective-permute-start | bytes 2752520 | tf_op jit(solution)/shard_map/ppermute | solution.py:100
  484.0 35.4 %collective-permute-start.52 = (bf16[2,4,64,896]{3,2,1,0:T(8,128)(2,1)}, bf16[2,4,64,896]{3,2,1,0:T(8,128)(2,1)}, u32[]{:S(2)}, u32[]{:S(2)}) collective-permute-start(bf16[2,4,64,896]{3,2,1,0:T(8,128)(2,1)} %pad_maximum_fusion.15), channel_id=1, source_target_pairs={{0,12},{4,8},{8,4},{12,0},{1,13},{5,9},{9,5},{13,1},{2,14},{6,10},... | collective-permute-start | bytes 2752520 | tf_op jit(solution)/shard_map/ppermute | solution.py:100
  484.0 35.4 %collective-permute-start.53 = (bf16[2,4,64,896]{3,2,1,0:T(8,128)(2,1)}, bf16[2,4,64,896]{3,2,1,0:T(8,128)(2,1)}, u32[]{:S(2)}, u32[]{:S(2)}) collective-permute-start(bf16[2,4,64,896]{3,2,1,0:T(8,128)(2,1)} %bitcast.58), channel_id=1, source_target_pairs={{0,16},{16,0},{32,48},{48,32},{1,17},{17,1},{33,49},{49,33},{2,18}... | collective-permute-start | bytes 2752520 | tf_op jit(solution)/shard_map/ppermute | solution.py:100
  498.2 20.6 %collective-permute-start.54 = (bf16[2,4,64,512]{3,2,1,0:T(8,128)(2,1)}, bf16[2,4,64,512]{3,2,1,0:T(8,128)(2,1)}, u32[]{:S(2)}, u32[]{:S(2)}) collective-permute-start(bf16[2,4,64,512]{3,2,1,0:T(8,128)(2,1)} %slice.546), channel_id=1, source_target_pairs={{0,48},{16,32},{32,16},{48,0},{1,49},{17,33},{33,17},{49,1},{2,50}... | collective-permute-start | bytes 1572872 | tf_op jit(solution)/shard_map/ppermute | solution.py:100
  511.0 34.9 %collective-permute-start.62 = (bf16[1024,704]{0,1:T(8,128)(2,1)}, bf16[1024,704]{0,1:T(8,128)(2,1)}, u32[]{:S(2)}, u32[]{:S(2)}) collective-permute-start(bf16[1024,704]{0,1:T(8,128)(2,1)} %fusion.37), channel_id=1, source_target_pairs={{0,64},{64,0},{1,65},{65,1},{2,66},{66,2},{3,67},{67,3},{4,68},{68... | collective-permute-start | bytes 4325384 | tf_op jit(solution)/shard_map/ppermute | solution.py:29
  518.9 54.7 %collective-permute-start.64 = (bf16[1024,704]{0,1:T(8,128)(2,1)}, bf16[1024,704]{0,1:T(8,128)(2,1)}, u32[]{:S(2)}, u32[]{:S(2)}) collective-permute-start(bf16[1024,704]{0,1:T(8,128)(2,1)} %fusion.43), channel_id=1, source_target_pairs={{0,64},{64,0},{1,65},{65,1},{2,66},{66,2},{3,67},{67,3},{4,68},{68... | collective-permute-start | bytes 4325384 | tf_op jit(solution)/shard_map/ppermute | solution.py:29
  521.7 33.4 %collective-permute-start.58 = (bf16[4,64,896]{2,1,0:T(8,128)(2,1)S(1)}, bf16[4,64,896]{2,1,0:T(8,128)(2,1)S(1)}, u32[]{:S(2)}, u32[]{:S(2)}) collective-permute-start(bf16[4,64,896]{2,1,0:T(8,128)(2,1)S(1)} %get-tuple-element.498), channel_id=1, source_target_pairs={{0,12},{4,8},{8,4},{12,0},{1,13},{5,9},{9,5},{13,1},{2,14},{6,10},... | collective-permute-start | bytes 1376264 | tf_op jit(solution)/shard_map/ppermute | solution.py:100
  526.4 28.7 %collective-permute-start.59 = (bf16[4,64,896]{2,1,0:T(8,128)(2,1)S(1)}, bf16[4,64,896]{2,1,0:T(8,128)(2,1)S(1)}, u32[]{:S(2)}, u32[]{:S(2)}) collective-permute-start(bf16[4,64,896]{2,1,0:T(8,128)(2,1)S(1)} %get-tuple-element.496), channel_id=1, source_target_pairs={{0,4},{4,0},{8,12},{12,8},{1,5},{5,1},{9,13},{13,9},{2,6},{6,2},{1... | collective-permute-start | bytes 1376264 | tf_op jit(solution)/shard_map/ppermute | solution.py:100
  528.7 26.4 %collective-permute-start.60 = (bf16[4,64,896]{2,1,0:T(8,128)(2,1)S(1)}, bf16[4,64,896]{2,1,0:T(8,128)(2,1)S(1)}, u32[]{:S(2)}, u32[]{:S(2)}) collective-permute-start(bf16[4,64,896]{2,1,0:T(8,128)(2,1)S(1)} %get-tuple-element.494), channel_id=1, source_target_pairs={{0,48},{16,32},{32,16},{48,0},{1,49},{17,33},{33,17},{49,1},{2,50}... | collective-permute-start | bytes 1376264 | tf_op jit(solution)/shard_map/ppermute | solution.py:100
  545.9 9.2 %collective-permute-start.61 = (bf16[4,64,512]{2,1,0:T(8,128)(2,1)S(1)}, bf16[4,64,512]{2,1,0:T(8,128)(2,1)S(1)}, u32[]{:S(2)}, u32[]{:S(2)}) collective-permute-start(bf16[4,64,512]{2,1,0:T(8,128)(2,1)S(1)} %get-tuple-element.502), channel_id=1, source_target_pairs={{0,16},{16,0},{32,48},{48,32},{1,17},{17,1},{33,49},{49,33},{2,18}... | collective-permute-start | bytes 786440 | tf_op jit(solution)/shard_map/ppermute | solution.py:100
  556.3 17.3 %collective-permute-start.63 = (bf16[2,4,64,640]{3,2,1,0:T(8,128)(2,1)S(1)}, bf16[2,4,64,640]{3,2,1,0:T(8,128)(2,1)S(1)}, u32[]{:S(2)}, u32[]{:S(2)}) collective-permute-start(bf16[2,4,64,640]{3,2,1,0:T(8,128)(2,1)S(1)} %slice.578), channel_id=1, source_target_pairs={{0,16},{16,0},{32,48},{48,32},{1,17},{17,1},{33,49},{49,33},{2,18}... | collective-permute-start | bytes 1966088 | tf_op jit(solution)/shard_map/ppermute | solution.py:100
  586.3 36.4 %collective-permute-start.65 = (bf16[4,64,640]{2,1,0:T(8,128)(2,1)}, bf16[4,64,640]{2,1,0:T(8,128)(2,1)}, u32[]{:S(2)}, u32[]{:S(2)}) collective-permute-start(bf16[4,64,640]{2,1,0:T(8,128)(2,1)} %get-tuple-element.492), channel_id=1, source_target_pairs={{0,48},{16,32},{32,16},{48,0},{1,49},{17,33},{33,17},{49,1},{2,50}... | collective-permute-start | bytes 983048 | tf_op jit(solution)/shard_map/ppermute | solution.py:100
  586.8 36.2 %collective-permute-start.67 = (bf16[128,2048]{1,0:T(8,128)(2,1)S(1)}, bf16[128,2048]{1,0:T(8,128)(2,1)}, u32[]{:S(2)}, u32[]{:S(2)}) collective-permute-start(bf16[128,2048]{1,0:T(8,128)(2,1)S(1)} %pad_maximum_fusion.32), channel_id=1, source_target_pairs={{0,1},{1,0},{2,3},{3,2},{4,5},{5,4},{6,7},{7,6},{8,9},{9,8},{10,11... | collective-permute-start | bytes 1572872 | tf_op jit(solution)/shard_map/ppermute | solution.py:29
  589.4 33.4 %collective-permute-start.66 = (bf16[128,2048]{1,0:T(8,128)(2,1)S(1)}, bf16[128,2048]{1,0:T(8,128)(2,1)S(1)}, u32[]{:S(2)}, u32[]{:S(2)}) collective-permute-start(bf16[128,2048]{1,0:T(8,128)(2,1)S(1)} %routed.1.part_ref), channel_id=1, source_target_pairs={{0,1},{1,0},{2,3},{3,2},{4,5},{5,4},{6,7},{7,6},{8,9},{9,8},{10,11... | collective-permute-start | bytes 1572872 | tf_op jit(solution)/shard_map/ppermute | solution.py:29
  591.7 29.6 %all-to-all-start.4 = ((bf16[8,32,1792]{2,1,0:T(8,128)(2,1)}), bf16[8,32,1792]{2,1,0:T(8,128)(2,1)}, u32[]{:S(2)}, u32[]{:S(2)}) async-start(bf16[8,32,1792]{2,1,0:T(8,128)(2,1)} %bitcast.85), calls=%async_computation.5 | async-start | bytes 1835008 | tf_op jit(solution)/shard_map/all_to_all | solution.py:992
  629.0 15.9 %collective-permute-start.69 = (bf16[32,4224]{1,0:T(8,128)(2,1)}, bf16[32,4224]{1,0:T(8,128)(2,1)}, u32[]{:S(2)}, u32[]{:S(2)}) collective-permute-start(bf16[32,4224]{1,0:T(8,128)(2,1)} %dynamic-slice_bitcast_fusion), channel_id=1, source_target_pairs={{0,64},{64,0},{1,65},{65,1},{2,66},{66,2},{3,67},{67,3},{4,68},{68... | collective-permute-start | bytes 811016 | tf_op jit(solution)/shard_map/ppermute | solution.py:29
  632.8 18.5 %all-to-all-start.5 = ((bf16[8,32,2048]{2,1,0:T(8,128)(2,1)}), bf16[8,32,2048]{2,1,0:T(8,128)(2,1)}, u32[]{:S(2)}, u32[]{:S(2)}) async-start(bf16[8,32,2048]{2,1,0:T(8,128)(2,1)} %bitcast.249), calls=%async_computation.6 | async-start | bytes 2097152 | tf_op jit(solution)/shard_map/all_to_all | solution.py:992
  (186 other events, 1679.8 us)
Sparse Core Ops, SparseCore 0:
  104.6 93.4 all-gather.1
  282.5 161.1 reduce-scatter.1

commit v4 on v3

--- a/solution.py
+++ b/solution.py
@@ -35,6 +35,13 @@
     return lax.ppermute(block, PLANE, route)
 
 
+def core_shift(block, first, second):
+    route = [
+        (2 * i + c, 2 * (i + k) + c) for c, k in ((0, first), (1, second)) for i in range(16 - k)
+    ]
+    return lax.ppermute(block, EXPERT, route)
+
+
 def matmul(left_op, right_op):
     return jnp.dot(left_op, right_op, preferred_element_type=f32)
 
@@ -127,20 +134,6 @@
     ]
 
 
-def steps_of(axis, cross):
-    return ((axis, 3), (axis, 1)) if cross else ((axis, 1), (axis, 3))
-
-
-def stream_places(size, first, cross, y_pos, z_pos):
-    index = jnp.arange(size, dtype=jnp.int32)
-    part = size // 16
-    order = jnp.asarray((3, 2, 0, 1) if cross else (1, 2, 0, 3), jnp.int32)
-    one, two = order[index // (4 * part)], index // part % 4
-    y_at, z_at = (two, one ^ z_pos) if first == "z" else (one ^ y_pos, two)
-    at = (y_at * 4 + z_at) * part + index % part
-    return (index[:, None] == at[None, :]).astype(bf16)
-
-
 def summed(mine, other, dim):
     return jnp.concatenate(mine, axis=dim).astype(f32) + jnp.concatenate(other, axis=dim).astype(f32)
 
@@ -176,7 +169,7 @@
 
 
 WIDE = 640
-VMEM_BYTES = 48 * 1024 * 1024
+VMEM_BYTES = 56 * 1024 * 1024
 
 
 def rope_places(head):
@@ -336,6 +329,80 @@
     @pl.when(step == pl.num_programs(0) - 1)
     def _():
         out_ref[...] = total_ref[...].astype(bf16)
+
+
+def expert_kernel(
+    second_ref, rows_ref, half_ref, first_ref, then_ref, gate_ref, up_ref, down_ref,
+    grads_ref, hidden_ref, back_gate_ref, back_up_ref, row_ref,
+):
+    rows = rows_ref[...]
+    second = second_ref[0] == 1
+    half = half_ref[...]
+    other = jnp.where(pl.program_id(0) == 0, first_ref[...], then_ref[...])
+    low = jnp.where(second, other, half)
+    high = jnp.where(second, half, other)
+    grads_ref[:, :1024] = low
+    grads_ref[:, 1024:] = high
+    gate_pre = matmul_nt(rows, gate_ref[...])
+    up_pre = matmul_nt(rows, up_ref[...])
+    back_hidden = matmul_nt(low, down_ref[:, :1024]) + matmul_nt(high, down_ref[:, 1024:])
+    sig = jax.nn.sigmoid(gate_pre)
+    active = gate_pre * sig
+    hidden_ref[...] = (active * up_pre).astype(bf16)
+    back_gate = (back_hidden * up_pre * sig * (1.0 + gate_pre * (1.0 - sig))).astype(bf16)
+    back_up = (back_hidden * active).astype(bf16)
+    back_gate_ref[...] = back_gate
+    back_up_ref[...] = back_up
+    row_ref[...] = (matmul(back_gate, gate_ref[...]) + matmul(back_up, up_ref[...])).astype(bf16)
+
+
+def shared_acts_kernel(all_ref, got_ref, acts_ref):
+    width = acts_ref.shape[1] // 3
+    gate, up, back = (
+        all_ref[:, i * width : (i + 1) * width] + got_ref[:, i * width : (i + 1) * width].astype(f32)
+        for i in range(3)
+    )
+    sig = jax.nn.sigmoid(gate)
+    active = gate * sig
+    acts_ref[:, :width] = (back * up * sig * (1.0 + gate * (1.0 - sig))).astype(bf16)
+    acts_ref[:, width : 2 * width] = (back * active).astype(bf16)
+    acts_ref[:, 2 * width :] = (active * up).astype(bf16)
+
+
+def shared_rows_kernel(h_own_ref, h_sib_ref, g_ref, own_ref, sib_ref, out_ref):
+    acts = jnp.concatenate([own_ref[...], sib_ref[...]], axis=0)
+    last = pl.program_id(0) == pl.num_programs(0) - 1
+
+    @pl.when(last)
+    def _():
+        out_ref[...] = matmul_tn(g_ref[...], acts).astype(bf16)
+
+    @pl.when(jnp.logical_not(last))
+    def _():
+        h_two = jnp.concatenate([h_own_ref[...], h_sib_ref[...]], axis=0)
+        out_ref[...] = matmul_tn(h_two, acts).astype(bf16)
+
+
+def shared_wide_kernel(own_ref, sib_ref, w_ref, back_ref, part_ref, theirs_ref, total_ref):
+    step = pl.program_id(0)
+    tok = own_ref.shape[0]
+    acts = jnp.concatenate([own_ref[...], sib_ref[...]], axis=0)
+    wide = matmul_nt(acts, w_ref[...])
+
+    @pl.when(step == 0)
+    def _():
+        total_ref[...] = wide
+
+    @pl.when(step == 1)
+    def _():
+        total = total_ref[...] + wide
+        back_ref[...] = total[:tok]
+        theirs_ref[:, :1024] = total[tok:].astype(bf16)
+
+    @pl.when(step == 2)
+    def _():
+        part_ref[...] = wide[:tok]
+        theirs_ref[:, 1024:] = wide[tok:].astype(bf16)
 
 
 def leave_kernel(core_ref, mid_ref, part_ref, other_ref, out_ref):
@@ -492,7 +559,9 @@
         ],
         axis=1,
     )
-    pair = gather_dp(pack, dp)
+    pair, shared_gate, shared_up, shared_down, y_late, z_late, segments = together(
+        gather_dp(pack, dp), shared_gate, shared_up, shared_down, y_pos, z_pos, segments
+    )
     pack_c = jnp.concatenate([shared_gate, shared_up, shared_down.T], axis=1)
 
     place = jnp.arange(D, dtype=jnp.int32)
@@ -536,7 +605,7 @@
     pair_c = gather_dp(pack_c, dp)
     blocks, got, pair_c, core_at, hidden_in, cotangent, routes, segments, y_late, z_late = together(
         chip_rows, gather_step(chip_rows, firsts, False), pair_c, core_at, hidden_in, cotangent,
-        routes, segments, y_pos, z_pos,
+        routes, segments, y_late, z_late,
     )
     blocks = pairs(blocks, got, firsts)
     blocks, got = together(blocks, gather_step(blocks, firsts, True))
@@ -584,12 +653,6 @@
     second = lax.axis_index("tensor") == 1
     grad_cols = jnp.where(second, cotangent[:, half:], cotangent[:, :half])
     grad_send = (matmul(weight_hi, grad_cols) + matmul(weight_lo, grad_cols)).astype(bf16)
-    places = [
-        stream_places(half, first, cross, y_late, z_late)
-        for first, cross in (("z", False), ("z", True), ("y", False))
-    ]
-    x_places = stream_places(256, "y", True, y_late, z_late)
-
     block_chip = jnp.concatenate(
         [chip - 4 + jnp.arange(5, dtype=jnp.int32), chip - 4 + core + jnp.arange(4, dtype=jnp.int32)]
     )
@@ -614,10 +677,10 @@
 
     (
         blocks, got, inputs, inverse_one, up_low, slot_pick, slot_weight, grad_send, pair_c, bias,
-        cosine, sine_tab, cos_all, sin_all, perm_m, places, x_places,
+        cosine, sine_tab, cos_all, sin_all, perm_m,
     ) = together(
         blocks, got, inputs, inverse_one, up_low, slot_pick, slot_weight, grad_send, pair_c, bias,
-        cosine, sine_tab, cos_all, sin_all, perm_m, places, x_places,
+        cosine, sine_tab, cos_all, sin_all, perm_m,
     )
     grad_half = exchange(grad_send)
     upstream = up_low.astype(f32)
@@ -668,11 +731,26 @@
     rope = jnp.concatenate(
         [q_first * cos_all - q_second * sin_all, q_first * sin_all + q_second * cos_all], axis=1
     ).astype(bf16)
-    shifts = [chip_shift(latent, k) for k in (4, 3, 2, 1)]
-    shifts, latent, q_nope, rope, w_expand = together(shifts, latent, q_nope, rope, w_expand)
-    own_blocks = jnp.stack(shifts + [latent])
-    sib_blocks = swapped(
-        lax.dynamic_slice_in_dim(own_blocks, 1 - core, 4, 0), "core"
+    latent_other = swapped(latent, "core")
+    both = jnp.stack(
+        [jnp.where(core == 0, latent, latent_other), jnp.where(core == 0, latent_other, latent)]
+    )
+    nearer, farther, both, q_nope, rope, w_expand = together(
+        core_shift(both, 1, 3), core_shift(both, 2, 4), both, q_nope, rope, w_expand
+    )
+    held = jnp.stack([farther, nearer])
+    held_other = swapped(held, "core")
+    chips = jnp.concatenate(
+        [
+            jnp.where(core == 0, held_other, held),
+            jnp.where(core == 0, held, held_other),
+            both[None],
+        ],
+        axis=0,
+    )
+    own_blocks = lax.dynamic_index_in_dim(chips, core, 1, keepdims=False)
+    sib_blocks = lax.dynamic_slice_in_dim(
+        lax.dynamic_index_in_dim(chips, 1 - core, 1, keepdims=False), core, 4, 0
     )
     window = jnp.concatenate([own_blocks, sib_blocks], axis=0).reshape(9 * tok, WIDE)
     window, grad_half = together(window, grad_half)
@@ -682,12 +760,11 @@
     o_part = jnp.concatenate(
         [matmul_nt(o_heads, w_out_own), matmul_nt(o_heads, w_out_sib)], axis=1
     ).astype(bf16)
-    o_part = lax.optimization_barrier(o_part)
+    o_part, grad_first = together(o_part, swapped(grad_half[:512], "tensor"))
     mid = inputs + (o_part.astype(f32) + swapped(o_part, "tensor").astype(f32))
     h_one_pair = both_cores(h_one[:, :half], swapped(h_one[:, half:], "core"))
-    h_orders = [matmul(h_one_pair, p).astype(bf16) for p in places]
-    mid, grad_half, h_orders = together(mid, grad_half, h_orders)
-    grad_other = swapped(grad_half, "tensor")
+    mid, grad_half, h_one_pair = together(mid, grad_half, h_one_pair)
+    grad_then = swapped(grad_half[512:], "tensor")
 
     slots = 32 * SLOTS
     h_two, inverse_two, send_rows = local_kernel(
@@ -717,65 +794,113 @@
     inverse_two = inverse_two[:, :1]
     expert_rows = exchange(send_rows)
 
-    h_two_pair = both_cores(h_two[:, :half], swapped(h_two[:, half:], "core"))
+    h_two_other = swapped(h_two[:, half:], "core")
+    h_two_pair = both_cores(h_two[:, :half], h_two_other)
     s_all = jnp.concatenate(
         [matmul(h_two_pair, own_c[:, : 2 * fs]), matmul(up_pair, own_c[:, 2 * fs :])], axis=1
     )
-    s_mine = s_all[:tok] + swapped(s_all[tok:].astype(bf16), "core").astype(f32)
-    s_gate = s_mine[:, :fs]
-    s_up = s_mine[:, fs : 2 * fs]
-    back_shidden = s_mine[:, 2 * fs :]
-    s_sig = jax.nn.sigmoid(s_gate)
-    s_active = s_gate * s_sig
-    s_hidden = (s_active * s_up).astype(bf16)
-    back_sgate = (back_shidden * s_up * s_sig * (1.0 + s_gate * (1.0 - s_sig))).astype(bf16)
-    back_sup = (back_shidden * s_active).astype(bf16)
-    s_acts = jnp.concatenate([back_sgate, back_sup, s_hidden], axis=1)
-    s_pair = both_cores(s_acts, swapped(s_acts, "core"))
-    shared_rows = jnp.concatenate(
-        [matmul_tn(h_two_pair, s_pair[:, : 2 * fs]), matmul_tn(up_pair, s_pair[:, 2 * fs :])], axis=1
-    ).astype(bf16)
-    grad_rows = jnp.concatenate(
-        [jnp.where(second, grad_other, grad_half), jnp.where(second, grad_half, grad_other)], axis=1
-    )
-    expert_rows, s_pair, shared_rows, grad_rows = together(
-        expert_rows, s_pair, shared_rows, grad_rows
+    s_acts = local_kernel(
+        shared_acts_kernel,
+        "shared_acts",
+        1,
+        [whole((tok, 3 * fs)), whole((tok, 3 * fs))],
+        whole((tok, 3 * fs)),
+        jax.ShapeDtypeStruct((tok, 3 * fs), bf16),
+    )(s_all, swapped(s_all[tok:].astype(bf16), "core"))
+    s_other = swapped(s_acts, "core")
+
+    def third(rows):
+        return pl.BlockSpec((rows, fs), lambda i: (0, i))
+
+    shared_rows = local_kernel(
+        shared_rows_kernel,
+        "shared_rows",
+        3,
+        [whole((tok, half)), whole((tok, half)), whole((2 * tok, half)), third(tok), third(tok)],
+        third(half),
+        jax.ShapeDtypeStruct((half, 3 * fs), bf16),
+        flops=4 * tok * half * 3 * fs,
+        moved=12 << 20,
+    )(h_two[:, :half], h_two_other, up_pair, s_acts, s_other)
+    expert_rows, s_acts, s_other, shared_rows, grad_then = together(
+        expert_rows, s_acts, s_other, shared_rows, grad_then
     )
     shared_part = lax.psum_scatter(shared_rows, PLANE, scatter_dimension=0, tiled=True)
-    wide_all = jnp.concatenate(
-        [
-            matmul_nt(s_pair[:, : 2 * fs], own_c[:, : 2 * fs]),
-            matmul_nt(s_pair[:, 2 * fs :], own_c[:, 2 * fs :]),
-        ],
-        axis=1,
-    )
-    wide_got = swapped(wide_all[tok:].astype(bf16), "core").astype(f32)
-    shared_back = jnp.concatenate([wide_all[:tok, :half], wide_got[:, :half]], axis=1)
-    s_part = jnp.concatenate([wide_all[:tok, half:], wide_got[:, half:]], axis=1)
-    gate_pre = matmul(expert_rows, expert_gate[0])
-    up_pre = matmul(expert_rows, expert_up[0])
-    gate_sig = jax.nn.sigmoid(gate_pre)
-    active = gate_pre * gate_sig
-    hidden = (active * up_pre).astype(bf16)
-    back_hidden = matmul_nt(grad_rows, expert_down[0])
-    back_gate = (back_hidden * up_pre * gate_sig * (1.0 + gate_pre * (1.0 - gate_sig))).astype(bf16)
-    back_up = (back_hidden * active).astype(bf16)
-    row_grad = (matmul_nt(back_gate, expert_gate[0]) + matmul_nt(back_up, expert_up[0])).astype(bf16)
+    hidden_units = expert_gate.shape[2]
+
+    def rows_of(width):
+        return pl.BlockSpec((slots // 2, width), lambda i: (i, 0))
+
+    grad_rows, hidden, back_gate, back_up, row_grad = local_kernel(
+        expert_kernel,
+        "experts",
+        2,
+        [
+            scalar_spec(),
+            rows_of(D),
+            rows_of(half),
+            whole((slots // 2, half)),
+            whole((slots // 2, half)),
+            whole((hidden_units, D)),
+            whole((hidden_units, D)),
+            whole((hidden_units, D)),
+        ],
+        [rows_of(D), rows_of(hidden_units), rows_of(hidden_units), rows_of(hidden_units), rows_of(D)],
+        [
+            jax.ShapeDtypeStruct((slots, D), bf16),
+            jax.ShapeDtypeStruct((slots, hidden_units), bf16),
+            jax.ShapeDtypeStruct((slots, hidden_units), bf16),
+            jax.ShapeDtypeStruct((slots, hidden_units), bf16),
+            jax.ShapeDtypeStruct((slots, D), bf16),
+        ],
+        flops=10 * slots * D * hidden_units,
+        moved=26 << 20,
+    )(
+        second.astype(jnp.int32).reshape(1),
+        expert_rows,
+        grad_half,
+        grad_first,
+        grad_then,
+        expert_gate[0].T,
+        expert_up[0].T,
+        expert_down[0],
+    )
     row_back = exchange(row_grad)
-    e_part = matmul(hidden, expert_down[0]).astype(bf16)
-    gate_low = [
-        matmul_tn(expert_rows[:, :half], back_gate).astype(bf16),
-        matmul_tn(expert_rows[:, half:], back_gate).astype(bf16),
-    ]
-    up_low_grad = [
-        matmul_tn(expert_rows[:, :half], back_up).astype(bf16),
-        matmul_tn(expert_rows[:, half:], back_up).astype(bf16),
-    ]
     down_low = [
         matmul_tn(hidden, grad_rows[:, :1536]).astype(bf16),
         matmul_tn(hidden, grad_rows[:, 1536:]).astype(bf16),
     ]
     down_got = swapped(down_low[0], "dp")
+    down_low[0], s_acts, s_other, hidden, back_gate, back_up = together(
+        down_low[0], s_acts, s_other, hidden, back_gate, back_up
+    )
+    back_mine, part_mine, wide_theirs = local_kernel(
+        shared_wide_kernel,
+        "shared_wide",
+        3,
+        [third(tok), third(tok), third(half)],
+        [whole((tok, half)), whole((tok, half)), whole((tok, D))],
+        [
+            jax.ShapeDtypeStruct((tok, half), f32),
+            jax.ShapeDtypeStruct((tok, half), f32),
+            jax.ShapeDtypeStruct((tok, D), bf16),
+        ],
+        [pltpu.VMEM((2 * tok, half), f32)],
+        flops=4 * tok * half * 3 * fs,
+        moved=12 << 20,
+    )(s_acts, s_other, own_c)
+    wide_got = swapped(wide_theirs, "core").astype(f32)
+    shared_back = jnp.concatenate([back_mine, wide_got[:, :half]], axis=1)
+    s_part = jnp.concatenate([part_mine, wide_got[:, half:]], axis=1)
+
+    e_part = matmul(hidden, expert_down[0]).astype(bf16)
+    gate_low = [
+        matmul_tn(expert_rows[:, a:b], back_gate).astype(bf16)
+        for a, b in ((0, 512), (512, 1280), (1280, D))
+    ]
+    up_low_grad = [
+        matmul_tn(expert_rows[:, a:b], back_up).astype(bf16) for a, b in ((0, half), (half, D))
+    ]
     row_back, down_got, gate_low, up_low_grad, e_part, s_part, shared_back = together(
         row_back, down_got, gate_low, up_low_grad, e_part, s_part, shared_back
     )
@@ -808,11 +933,10 @@
     up_got = [swapped(part, "dp") for part in up_low_grad]
 
     attn_pair = both_cores(back_attn[:, :half], swapped(back_attn[:, half:], "core"))
-    attn_orders = [matmul(attn_pair, p).astype(bf16) for p in places[1:]]
     heads_pair = both_cores(o_heads, swapped(o_heads, "core"))
     gain_low = grad_gain_two.astype(bf16)
     gain_sum = add_low(gain_low[:half], swapped(gain_low[half:], "core"))
-    gain_col = matmul_tn(places[2], jnp.broadcast_to(gain_sum[:, None], (half, 128))).astype(bf16)
+    gain_col = jnp.broadcast_to(gain_sum[:, None], (half, 128))
 
     back_heads = (
         matmul(back_attn[:, :half], w_out_own) + matmul(back_attn[:, half:], w_out_sib)
@@ -831,20 +955,20 @@
         jnp.concatenate([cosine, cosine, pad_lanes], axis=1),
         jnp.concatenate([sine_tab, -sine_tab, pad_lanes], axis=1),
     )
-    back_qnope, back_rope, back_own, back_sib, grad_expand, down_got[1] = together(
-        back_qnope, back_rope, back_own, back_sib, grad_expand, down_got[1]
+    back_qnope, back_rope, back_own, back_sib, grad_expand, down_got[1], gate_got[0] = together(
+        back_qnope, back_rope, back_own, back_sib, grad_expand, down_got[1], gate_got[0]
     )
     acts_q = jnp.concatenate([back_qnope, back_rope], axis=1)
     expand_mine = lax.dynamic_slice_in_dim(grad_expand, core * 256, 256, 0)
     expand_theirs = lax.dynamic_slice_in_dim(grad_expand, 256 - core * 256, 256, 0)
-    from_sib, acts_other, expand_other, acts_q, expand_mine, heads_pair, attn_orders, down_low = together(
+    from_sib, acts_other, expand_other, acts_q, expand_mine, heads_pair, attn_pair, down_low = together(
         swapped(back_sib, "core"),
         swapped(acts_q, "core"),
         swapped(expand_theirs, "core"),
         acts_q,
         expand_mine,
         heads_pair,
-        attn_orders,
+        attn_pair,
         down_low,
     )
 
@@ -860,35 +984,19 @@
 
     acts_q = both_cores(acts_q, acts_other)
     rows_x = add_low(expand_mine, expand_other)
-    rows_x = matmul_tn(x_places, rows_x).astype(bf16).reshape(4, 4, 64, 512)
-
-    def halves(part):
-        at = slice(0, 512) if part == 0 else slice(512, 1024)
-        q_first = matmul_tn(h_orders[0][:, at], acts_q[:, :896])
-        q_second = jnp.concatenate(
-            [
-                matmul_tn(h_orders[1][:, at], acts_q[:, 896:]),
-                matmul_tn(attn_orders[0][:, at], heads_pair[:, :256]),
-            ],
-            axis=1,
-        )
-        third = jnp.concatenate(
-            [matmul_tn(attn_orders[1][:, at], heads_pair[:, 256:]).astype(bf16), gain_col[at]], axis=1
-        )
-        rows = [r.astype(bf16).reshape(2, 4, 64, 896) for r in (q_first, q_second, third)]
-        return rows + [rows_x[2 * part : 2 * part + 2]]
-
-    first_steps = [steps_of("z", False), steps_of("z", True), steps_of("y", False), steps_of("y", True)]
-    down_sum = summed(down_low, down_got, 1)
-    sends = halves(0)
-    (
-        sends, rows_x, chip_last, shifts, gate_got[0], h_orders, attn_orders, down_sum, shared_part,
-    ) = together(
-        sends, rows_x, chip_blocks[4], shifts, gate_got[0], h_orders, attn_orders, down_sum,
-        shared_part,
-    )
-    got = [xored(r, *steps[0]) for r, steps in zip(sends, first_steps)]
-    keeps = halves(1)
+    chip_last, shifts, acts_q, rows_x, shared_part, returned, gate_got[1] = together(
+        chip_blocks[4], shifts, acts_q, rows_x, shared_part, returned, gate_got[1]
+    )
+    weight_rows = jnp.concatenate(
+        [
+            matmul_tn(h_one_pair, acts_q).astype(bf16),
+            matmul_tn(attn_pair, heads_pair).astype(bf16),
+            gain_col,
+            rows_x.reshape(half, 512),
+        ],
+        axis=1,
+    )
+    weight_part = lax.psum_scatter(weight_rows, PLANE, scatter_dimension=0, tiled=True)
 
     back_latent = chip_last + sum(shift.astype(f32) for shift in shifts)
 
@@ -902,12 +1010,17 @@
     mid_low = grad_gain_mid.astype(bf16)
     mid_sum = (mid_low.astype(f32) + swapped(mid_low, "core").astype(f32)).astype(bf16)
     mid_col = matmul_nt(perm_m[:half], jnp.broadcast_to(mid_sum[None, :], (64, LATENT)))
-    mid_col = matmul_tn(places[2], mid_col.astype(bf16))
-    rows_l = jnp.concatenate([matmul_tn(h_orders[2], kv_pair), mid_col], axis=1)
-    rows_l = rows_l.astype(bf16).reshape(4, 4, 64, 640)
-
-    got, keeps, rows_l, gate_got[1], back_mid, returned, gate_low, up_low_grad = together(
-        got, keeps, rows_l, gate_got[1], back_mid, returned, gate_low, up_low_grad
+    rows_l = jnp.concatenate([matmul_tn(h_one_pair, kv_pair), mid_col], axis=1).astype(bf16)
+    (
+        rows_l, gate_got[2], returned, back_mid, gate_low, up_low_grad, back_qnope, back_rope, down_low,
+        shared_part,
+    ) = together(
+        rows_l, gate_got[2], returned, back_mid, gate_low, up_low_grad, back_qnope, back_rope, down_low,
+        shared_part,
+    )
+    down_sum = summed(down_low, down_got, 1)
+    l_blocks = lax.all_to_all(
+        rows_l.reshape(16, 64, 640), PLANE, split_axis=0, concat_axis=0, tiled=True
     )
     out_low = local_kernel(
         routed_kernel,
@@ -925,14 +1038,6 @@
         flops=4 * slots * tok * D,
         moved=6 << 20,
     )(core_at, slot_weight, returned, s_part)
-    near = [add_low(k[0], g[0]) for k, g in zip(keeps, got)]
-    far = [add_low(k[1], g[1]) for k, g in zip(keeps, got)]
-
-    got = [xored(r, *steps[1]) for r, steps in zip(far, first_steps)]
-    got_l = xored(rows_l[:2], "y", 1)
-    got, near, got_l, rows_l, out_low, gate_low, back_qnope, back_rope, back_kvpre, up_got[0] = together(
-        got, near, got_l, rows_l, out_low, gate_low, back_qnope, back_rope, back_kvpre, up_got[0]
-    )
     back_lane = jnp.concatenate([back_rope, back_kvpre, jnp.zeros((tok, 64), bf16)], axis=1)
     q_back = [matmul_nt(back_qnope, w) for w in q_parts]
     l_back = [matmul_nt(back_lane, w) for w in l_parts]
@@ -946,58 +1051,19 @@
 
     one_other = swapped(one_part, "tensor")
     out_other = swapped(out_low, "tensor")
+    l_blocks, up_got[0], one_part, out_low, down_sum, shared_part = together(
+        l_blocks, up_got[0], one_part, out_low, down_sum, shared_part
+    )
+    shared_mine = mine_of(shared_part.reshape(2, 32, 3 * fs), dp)
+    shared_other = swapped(theirs_of(shared_part.reshape(2, 32, 3 * fs), dp), "dp")
     gate_sum = summed(gate_low, gate_got, 0)
-    rows = [add_low(n, g) for n, g in zip(near, got)]
-    near_l, far_l = add_low(rows_l[2], got_l[0]), add_low(rows_l[3], got_l[1])
-    got_l = xored(far_l, "y", 3)
-
-    def owned(blocks, axis):
-        blocks = blocks.reshape(8, 32, blocks.shape[2])
-        blocks = lax.all_to_all(blocks, (axis, "dp"), split_axis=0, concat_axis=0, tiled=True)
-        return jnp.sum(blocks.astype(f32), axis=0)
-
-    from_y = owned(jnp.concatenate(rows[:2], axis=2), "y")
-    got_l, near_l, rows, from_y, gate_sum, shared_part, one_part, out_other, out_low, up_got[1] = together(
-        got_l, near_l, rows, from_y, gate_sum, shared_part, one_part, out_other, out_low, up_got[1]
-    )
-    from_z = owned(jnp.concatenate(rows[2:] + [add_low(near_l, got_l)], axis=2), "z")
-    l_sum = from_z[:, 1408:]
-
-
-    got = [xored(r, *steps[1]) for r, steps in zip(far, first_steps)]
-    got_l = xored(rows_l[:2], "y", 1)
-    got, near, got_l, rows_l, out_low, gate_low, back_qnope, back_rope, back_kvpre, up_got[0] = together(
-        got, near, got_l, rows_l, out_low, gate_low, back_qnope, back_rope, back_kvpre, up_got[0]
-    )
-    back_lane = jnp.concatenate([back_rope, back_kvpre, jnp.zeros((tok, 64), bf16)], axis=1)
-    q_back = [matmul_nt(back_qnope, w) for w in q_parts]
-    l_back = [matmul_nt(back_lane, w) for w in l_parts]
-    one_part = jnp.concatenate(
-        [
-            join_low(q_back[0], q_back[1]) + join_outer(l_back[0], l_back[1]),
-            join_low(q_back[2], q_back[3]) + join_outer(l_back[2], l_back[3]),
-        ],
-        axis=1,
-    ).astype(bf16)
-
-    one_other = swapped(one_part, "tensor")
-    out_other = swapped(out_low, "tensor")
-    gate_sum = summed(gate_low, gate_got, 0)
-    rows = [add_low(n, g) for n, g in zip(near, got)]
-    near_l, far_l = add_low(rows_l[2], got_l[0]), add_low(rows_l[3], got_l[1])
-    got_l = xored(far_l, "y", 3)
-
-    def owned(blocks, axis):
-        blocks = blocks.reshape(8, 32, blocks.shape[2])
-        blocks = lax.all_to_all(blocks, (axis, "dp"), split_axis=0, concat_axis=0, tiled=True)
-        return jnp.sum(blocks.astype(f32), axis=0)
-
-    from_y = owned(jnp.concatenate(rows[:2], axis=2), "y")
-    got_l, near_l, rows, from_y, gate_sum, shared_part, one_part, out_other, out_low, up_got[1] = together(
-        got_l, near_l, rows, from_y, gate_sum, shared_part, one_part, out_other, out_low, up_got[1]
-    )
-    from_z = owned(jnp.concatenate(rows[2:] + [add_low(near_l, got_l)], axis=2), "z")
-    l_sum = from_z[:, 1408:]
+    l_part = jnp.sum(l_blocks.astype(f32), axis=0).astype(bf16)
+    weight_part, l_part, up_got[1], gate_sum, shared_mine, shared_other = together(
+        weight_part, l_part, up_got[1], gate_sum, shared_mine, shared_other
+    )
+    shared_grads = shared_mine.astype(f32) + shared_other.astype(f32)
+    sums = finish_rows(jnp.concatenate([weight_part, l_part], axis=1), dp)
+    l_sum = sums[:, 3200:]
 
     back_one = one_part.astype(f32) + one_other.astype(f32)
     back_innorm, _ = rms_backward(inputs, inverse_one, gain_one, back_one)
@@ -1019,16 +1085,14 @@
         jax.ShapeDtypeStruct((tok, D), bf16),
     )(core_at, mid, out_low, out_other)
 
-    shared_grads = finish_rows(shared_part, dp)
-    out_grads = jnp.concatenate([from_y[:, 1536:], from_z[:, :768]], axis=1)
-    weight_dots = jnp.sum(from_y[:, :1536] * pack[:, :1536].astype(f32), axis=1) + jnp.sum(
+    weight_dots = jnp.sum(sums[:, :1536] * pack[:, :1536].astype(f32), axis=1) + jnp.sum(
         l_sum[:, :576] * pack[:, 1536:2112].astype(f32), axis=1
     )
     small = jnp.concatenate(
         [
             l_sum,
             (weight_dots / prenorm.astype(f32))[:, None],
-            0.5 * from_z[:, 768:769],
+            0.5 * sums[:, 2560:2561],
             jnp.zeros((32, 126), f32),
         ],
         axis=1,
@@ -1036,9 +1100,9 @@
     small = small + swapped(small, "tensor")
     query_grad = jnp.concatenate(
         [
-            from_y[:, :1024].reshape(32, heads, QN),
-            from_y[:, 1024:1280].reshape(32, heads, 32),
-            from_y[:, 1280:1536].reshape(32, heads, 32),
+            sums[:, :1024].reshape(32, heads, QN),
+            sums[:, 1024:1280].reshape(32, heads, 32),
+            sums[:, 1280:1536].reshape(32, heads, 32),
         ],
         axis=2,
     ).reshape(32, heads * (QN + QR))
@@ -1054,8 +1118,8 @@
         query_grad,
         latent_grad,
         small[:8, 576],
-        from_z[:, 896:1408].reshape(8, 2048),
-        out_grads.T,
+        sums[:, 2688:3200].reshape(8, 2048),
+        sums[:, 1536:2560].T,
         small[:, 641],
         shared_grads[:, :fs],
         shared_grads[:, fs : 2 * fs],

time: 680 us -> 614 us (0.903)
  Pallas kernels: 49.9 us -> 106 us
  matrix products: 133 us -> 77.6 us
  other arithmetic: 100 us -> 63.9 us
  waiting for transfers between devices: 182 us -> 170 us
  local copies, waits for them, and re-layouts: 50.5 us -> 41.9 us
  starting transfers between devices: 136 us -> 129 us
    pallas_call x0 -> x4, Pallas kernels: none -> 44 us  [the longest x1 26.1 us: shards(): local_kernel(expert_kernel, 'experts', 2, [scalar_spec(), rows_of(D), row...]
    all_to_all x2 -> x1, waiting for transfers between devices: 23.3 us -> 0.01 us  [shards(): lax.all_to_all(rows_l.reshape(16, 64, 640), PLANE, split_axis=0, concat_a...]
    dot_general x19 -> x15, matrix products: 39.5 us -> 17.7 us  [matmul_nt(): lax.dot_general(left_op, right_op, (((1,), (1,)), ((), ())), preferred_el...]
    ppermute x36 -> x40, waiting for transfers between devices: 110 us -> 132 us  [swapped(): return lax.ppermute(block, axis, [(0, 1), (1, 0)])]
    dot_general x24 -> x17, matrix products: 48 us -> 28.6 us  [matmul(): return jnp.dot(left_op, right_op, preferred_element_type=f32)]
    ppermute x26 -> x16, starting transfers between devices: 41.1 us -> 23.5 us  [xored(): return lax.ppermute(block, axis, [(i, i ^ k) for i in range(4)])]
    ppermute x8 -> x4, starting transfers between devices: 20.7 us -> 5.17 us  [chip_shift(): return lax.ppermute(block, PLANE, route)]
    dot_general x20 -> x10, matrix products: 45.3 us -> 31.3 us  [matmul_tn(): lax.dot_general(left_op, right_op, (((0,), (0,)), ((), ())), preferred_el...]
  transfers between devices with their start and end apart: 78 -> 70, of which waited for: 23 -> 31; matrix products, arithmetic and copies ran while one was open for 33% -> 25% of each run, Pallas kernels for 7% -> 18%
where the time goes in v4:
time: 614 us; the launch traced here: 605 us
  waiting for transfers between devices  170 us (28%)
  starting transfers between devices  129 us (21%)
  Pallas kernels  106 us (17%)
  matrix products  77.6 us (13%)
  other arithmetic  63.9 us (10%)
  local copies, waits for them, and re-layouts  41.9 us (7%)
  between operations  16.1 us (3%)
    ppermute x40, waiting for transfers between devices, swapped(): return lax.ppermute(block, axis, [(0, 1), (1, 0)])  132 us
    all_to_all x4, starting transfers between devices, exchange(): lax.all_to_all(blocks, EXPERT, split_axis=0, concat_axis=0, tiled=True)  37.9 us
    ppermute x40, starting transfers between devices, swapped(): return lax.ppermute(block, axis, [(0, 1), (1, 0)])  36.1 us
    dot_general x10, matrix products, matmul_tn(): lax.dot_general(left_op, right_op, (((0,), (0,)), ((), ())), preferred_el...  31.3 us
    dot_general x17, matrix products, matmul(): return jnp.dot(left_op, right_op, preferred_element_type=f32)  28.6 us
    ppermute x16, waiting for transfers between devices, xored(): return lax.ppermute(block, axis, [(i, i ^ k) for i in range(4)])  26.8 us
    pallas_call x1, Pallas kernels, shards(): local_kernel(expert_kernel, 'experts', 2, [scalar_spec(), rows_of(D), row...  26.1 us
    pallas_call x1, Pallas kernels, attend_back(): pl.pallas_call(functools.partial(attend_back_kernel, scale), grid=(heads,...  24.4 us
  transfers between devices with their start and end apart: 70, of which 31 were waited for; matrix products, arithmetic and copies ran while one was open for 25% of the time, Pallas kernels for 18%

profile of v4, /device:TPU:0, one launch (start us, length us, event | category | flops | bytes accessed | tf_op | source)
XLA Modules:
  0.0 604.7 jit_solution(11614629576900977269)
XLA Ops:
  21.2 3.3 collective-permute-start.4
  28.3 2.6 collective-permute-start.2
  30.9 2.5 collective-permute-done.5
  37.0 2.6 collective-permute-start.6
  44.8 2.5 collective-permute-done.8
  49.4 3.4 collective-permute-start.11
  53.7 9.6 %collective-permute-done.13 = bf16[4,1,16,2048]{3,2,1,0:T(8,128)(2,1)S(1)} collective-permute-done((bf16[4,1,16,2048]{3,2,1,0:T(8,128)(2,1)S(1)}, bf16[4,1,16,2048]{3,2,1,0:T(8,128)(2,1)S(1)}, u32[]{:S(2)}, u32[]{:S(2)}) %collective-permute-start.13) | collective-permute-done | bytes 262176 | tf_op jit(solution)/shard_map/ppermute | solution.py:107
  67.9 2.6 collective-permute-start.17
  70.5 2.7 enter.1
  74.3 3.3 collective-permute-done.17
  77.6 5.5 collective-permute-done.16
  83.2 4.3 collective-permute-done.15
  89.8 4.9 all-to-all-start
  119.0 5.1 collective-permute-start.22
  124.1 2.5 collective-permute-start.21
  129.9 3.5 collective-permute-done.21
  142.4 3.1 collective-permute-start.28
  145.5 13.6 %attend.1 = (bf16[8,128,640]{2,1,0:T(8,128)(2,1)}, bf16[8,128,512]{2,1,0:T(8,128)(2,1)}, bf16[128,1024]{1,0:T(8,128)(2,1)}, f32[8,128,128]{2,1,0:T(8,128)}) custom-call(bf16[128,1024]{1,0:T(8,128)(2,1)} %fusion.31.qn_ref, bf16[128,512]{1,0:T(8,128)(2,1)} %pad_maximum_fusion.40.rope_ref, bf16[512,2048]{1,0:T(8,128)(2,1)} %pad_maximum_fusion.2.w_ref, ...), custom_call_target="tpu_custom_call" | custom-call | flops 2831155200 | bytes 12582912 | tf_op jit(solution)/shard_map/attend/pallas_call | solution.py:441
  163.5 5.8 collective-permute-done.28.first_ref
  169.4 3.1 collective-permute-start.29
  175.0 9.3 %collective-permute-done.29 = bf16[128,2048]{1,0:T(8,128)(2,1)S(1)} collective-permute-done((bf16[128,2048]{1,0:T(8,128)(2,1)S(1)}, bf16[128,2048]{1,0:T(8,128)(2,1)S(1)}, u32[]{:S(2)}, u32[]{:S(2)}) %collective-permute-start.29) | collective-permute-done | bytes 524320 | tf_op jit(solution)/shard_map/ppermute | solution.py:29
  185.4 5.3 dispatch.1
  190.7 14.5 %all-to-all-start.1 = ((bf16[32,32,2048]{2,1,0:T(8,128)(2,1)}), bf16[32,32,2048]{2,1,0:T(8,128)(2,1)}, u32[]{:S(2)}, u32[]{:S(2)}) async-start(bf16[32,32,2048]{2,1,0:T(8,128)(2,1)} %bitcast.194), calls=%async_computation.1 | async-start | bytes 8388608 | tf_op jit(solution)/shard_map/all_to_all | solution.py:649
  205.2 11.5 %reduce-scatter.3.cloned.1.call-start = ((), (), s32[]{:S(2)}) async-start(), calls=%async_computation.8 | async-start | bytes 9191424 | tf_op jit(solution)/shard_map/reduce_scatter | solution.py:828
  218.7 3.0 fusion.5
  221.7 4.4 fusion
  230.0 3.4 shared_acts.1.own_ref
  235.9 3.1 collective-permute-start.35
  241.8 6.8 %shared_rows.1 = bf16[1024,4224]{1,0:T(8,128)(2,1)} custom-call(bf16[128,1024]{1,0:T(8,128)(2,1)} %copy-done.48, bf16[128,1024]{1,0:T(8,128)(2,1)} %collective-permute-done.31.h_sib_ref, bf16[256,1024]{1,0:T(8,128)(2,1)} %pad_maximum_fusion.22.g_ref, bf16[128,4224]{1,0:T(8,128)(2,1)} %shared_acts.1.own_ref, bf16[128,4224]{1,0:T(8,128)(2,1)} %copy-done.14), custom_call_target="tpu_custom_call" | custom-call | flops 2214592512 | bytes 12582912 | tf_op jit(solution)/shard_map/shared_rows/pallas_call | solution.py:815
  248.6 14.4 %collective-permute-done.35.then_ref = bf16[512,1024]{1,0:T(8,128)(2,1)} collective-permute-done((bf16[512,1024]{1,0:T(8,128)(2,1)}, bf16[512,1024]{1,0:T(8,128)(2,1)}, u32[]{:S(2)}, u32[]{:S(2)}) %collective-permute-start.35) | collective-permute-done | bytes 1048608 | tf_op jit(solution)/shard_map/ppermute | solution.py:29
  263.1 26.1 %experts.1 = (bf16[1024,2048]{1,0:T(8,128)(2,1)}, bf16[1024,704]{1,0:T(8,128)(2,1)}, bf16[1024,704]{1,0:T(8,128)(2,1)}, bf16[1024,704]{1,0:T(8,128)(2,1)}, bf16[1024,2048]{1,0:T(8,128)(2,1)}) custom-call(s32[1]{0:T(128)} %bitcast.45.second_ref, bf16[1024,2048]{1,0:T(8,128)(2,1)} %bitcast.47.rows_ref, bf16[1024,1024]{1,0:T(8,128)(2,1)} %bitcast.43.half_ref, ...), custom_call_target="tpu_custom_call" | custom-call | flops 14763950080 | bytes 27262976 | tf_op jit(solution)/shard_map/experts/pallas_call | solution.py:834
  289.3 7.4 %all-to-all-start.2 = ((bf16[32,32,2048]{2,1,0:T(8,128)(2,1)}), bf16[32,32,2048]{2,1,0:T(8,128)(2,1)}, u32[]{:S(2)}, u32[]{:S(2)}) async-start(bf16[32,32,2048]{2,1,0:T(8,128)(2,1)} %bitcast.195), calls=%async_computation.2 | async-start | bytes 8388608 | tf_op jit(solution)/shard_map/all_to_all | solution.py:649
  296.7 4.9 convolution_convert_fusion.2
  303.6 7.7 %shared_wide.1 = (f32[128,1024]{1,0:T(8,128)}, f32[128,1024]{1,0:T(8,128)}, bf16[128,2048]{1,0:T(8,128)(2,1)}) custom-call(bf16[128,4224]{1,0:T(8,128)(2,1)} %shared_acts.1.own_ref, bf16[128,4224]{1,0:T(8,128)(2,1)} %copy-done.14, bf16[1024,4224]{1,0:T(8,128)(2,1)} %all-gather.2.cloned.1.call-done.w_ref), custom_call_target="tpu_custom_call" | custom-call | flops 2214592512 | bytes 12582912 | tf_op jit(solution)/shard_map/shared_wide/pallas_call | solution.py:877
  311.3 3.7 fusion.27
  315.0 3.9 fusion.24
  318.9 4.6 fusion.17
  323.5 4.9 convolution_convert_fusion.1
  328.4 3.1 convolution_convert_fusion.6
  331.5 4.4 fusion.14
  339.1 12.4 %collective-permute-done.36 = bf16[704,1536]{1,0:T(8,128)(2,1)} collective-permute-done((bf16[704,1536]{1,0:T(8,128)(2,1)S(1)}, bf16[704,1536]{1,0:T(8,128)(2,1)}, u32[]{:S(2)}, u32[]{:S(2)}) %collective-permute-start.36) | collective-permute-done | bytes 2162720 | tf_op jit(solution)/shard_map/ppermute | solution.py:29
  351.4 6.2 %all-to-all-done.2 = bf16[32,32,2048]{2,1,0:T(8,128)(2,1)} async-done(((bf16[32,32,2048]{2,1,0:T(8,128)(2,1)}), bf16[32,32,2048]{2,1,0:T(8,128)(2,1)}, u32[]{:S(2)}, u32[]{:S(2)}) %all-to-all-start.2) | async-done | bytes 4194336 | tf_op jit(solution)/shard_map/all_to_all | solution.py:649
  357.7 5.4 combine.1
  363.1 2.9 collective-permute-start.38
  366.9 3.1 convolution_convert_fusion.5
  369.9 11.1 %all-to-all-start.3 = ((bf16[32,32,2048]{2,1,0:T(8,128)(2,1)}), bf16[32,32,2048]{2,1,0:T(8,128)(2,1)}, u32[]{:S(2)}, u32[]{:S(2)}) async-start(bf16[32,32,2048]{2,1,0:T(8,128)(2,1)} %bitcast.193), calls=%async_computation.4 | async-start | bytes 8388608 | tf_op jit(solution)/shard_map/all_to_all | solution.py:649
  383.5 2.6 fusion.130
  388.6 2.8 fusion.32.bh_ref
  391.3 24.4 %attend_back.1 = (bf16[512,2048]{1,0:T(8,128)(2,1)}, bf16[128,1024]{1,0:T(8,128)(2,1)}, bf16[128,512]{1,0:T(8,128)(2,1)}, f32[640,640]{1,0:T(8,128)}, bf16[512,640]{1,0:T(8,128)(2,1)}) custom-call(bf16[128,1024]{1,0:T(8,128)(2,1)} %fusion.32.bh_ref, bf16[512,2048]{1,0:T(8,128)(2,1)} %pad_maximum_fusion.2.w_ref, bf16[1152,640]{1,0:T(8,128)(2,1)} %bitcast.200, ...), custom_call_target="tpu_custom_call" | custom-call | flops 7549747200 | bytes 20971520 | tf_op jit(solution)/shard_map/attend_back/pallas_call | solution.py:473
  415.8 4.1 collective-permute-done.40
  437.0 15.1 %collective-permute-done.50 = bf16[768,704]{0,1:T(8,128)(2,1)S(1)} collective-permute-done((bf16[768,704]{0,1:T(8,128)(2,1)S(1)}, bf16[768,704]{0,1:T(8,128)(2,1)S(1)}, u32[]{:S(2)}, u32[]{:S(2)}) %collective-permute-start.50) | collective-permute-done | bytes 1081376 | tf_op jit(solution)/shard_map/ppermute | solution.py:29
  460.2 3.3 pad_maximum_fusion
  472.3 18.4 %collective-permute-done.53 = bf16[768,704]{0,1:T(8,128)(2,1)} collective-permute-done((bf16[768,704]{0,1:T(8,128)(2,1)}, bf16[768,704]{0,1:T(8,128)(2,1)}, u32[]{:S(2)}, u32[]{:S(2)}) %collective-permute-start.53) | collective-permute-done | bytes 1081376 | tf_op jit(solution)/shard_map/ppermute | solution.py:29
  492.2 7.2 %all-to-all-start.4 = ((bf16[16,64,640]{2,1,0:T(8,128)(2,1)}), bf16[16,64,640]{2,1,0:T(8,128)(2,1)}, u32[]{:S(2)}, u32[]{:S(2)}) async-start(bf16[16,64,640]{2,1,0:T(8,128)(2,1)} %bitcast.189), calls=%async_computation.5 | async-start | bytes 2621440 | tf_op jit(solution)/shard_map/all_to_all | solution.py:1022
  511.9 5.6 routed.1.part_ref
  517.6 2.7 collective-permute-start.55
  520.3 4.4 convert_add_fusion.2
  524.7 4.0 convert_add_fusion.1
  531.0 32.6 %collective-permute-done.56 = bf16[128,2048]{1,0:T(8,128)(2,1)S(1)} collective-permute-done((bf16[128,2048]{1,0:T(8,128)(2,1)S(1)}, bf16[128,2048]{1,0:T(8,128)(2,1)S(1)}, u32[]{:S(2)}, u32[]{:S(2)}) %collective-permute-start.56) | collective-permute-done | bytes 524320 | tf_op jit(solution)/shard_map/ppermute | solution.py:29
  565.3 2.5 input_order.1
  569.3 5.6 collective-permute-done.55.other_ref
  574.9 2.7 leave.1
  582.8 4.7 convert_add_fusion
  592.7 2.8 collective-permute-done.61
  (552 shorter events, 169.1 us)
Async XLA Ops:
  7.2 211.5 %all-gather.2.cloned.1.call-start = ((), (), s32[]{:S(2)}) async-start(), calls=%async_computation.7 | async-start | bytes 9191424 | tf_op jit(solution)/shard_map/all_gather | solution.py:693
  13.6 7.4 %collective-permute-start = (bf16[32,3712]{1,0:T(8,128)(2,1)S(1)}, bf16[32,3712]{1,0:T(8,128)(2,1)S(1)}, u32[]{:S(2)}, u32[]{:S(2)}) collective-permute-start(bf16[32,3712]{1,0:T(8,128)(2,1)S(1)} %concatenate.224), channel_id=1, source_target_pairs={{0,64},{64,0},{1,65},{65,1},{2,66},{66,2},{3,67},{67,3},{4,68},{68... | collective-permute-start | bytes 712712 | tf_op jit(solution)/shard_map/ppermute | solution.py:29
  21.2 13.1 %collective-permute-start.4 = (bf16[1,1,16,2048]{3,2,1,0:T(8,128)(2,1)S(1)}, bf16[1,1,16,2048]{3,2,1,0:T(8,128)(2,1)S(1)}, u32[]{:S(2)}, u32[]{:S(2)}) collective-permute-start(bf16[1,1,16,2048]{3,2,1,0:T(8,128)(2,1)S(1)} %reshape.460), channel_id=1, source_target_pairs={{0,48},{16,32},{32,16},{48,0},{1,49},{17,33},{33,17},{49,1},{2,50}... | collective-permute-start | bytes 196616 | tf_op jit(solution)/shard_map/ppermute | solution.py:107
  24.6 9.8 %collective-permute-start.3 = (bf16[1,1,64,1024]{3,2,1,0:T(8,128)(2,1)S(1)}, bf16[1,1,64,1024]{3,2,1,0:T(8,128)(2,1)S(1)}, u32[]{:S(2)}, u32[]{:S(2)}) collective-permute-start(bf16[1,1,64,1024]{3,2,1,0:T(8,128)(2,1)S(1)} %get-tuple-element.208), channel_id=1, source_target_pairs={{0,16},{16,0},{32,48},{48,32},{1,17},{17,1},{33,49},{49,33},{2,18}... | collective-permute-start | bytes 393224 | tf_op jit(solution)/shard_map/ppermute | solution.py:107
  24.7 9.6 %collective-permute-start.1 = (bf16[1,1,64,1024]{3,2,1,0:T(8,128)(2,1)S(1)}, bf16[1,1,64,1024]{3,2,1,0:T(8,128)(2,1)S(1)}, u32[]{:S(2)}, u32[]{:S(2)}) collective-permute-start(bf16[1,1,64,1024]{3,2,1,0:T(8,128)(2,1)S(1)} %get-tuple-element.204), channel_id=1, source_target_pairs={{0,4},{4,0},{8,12},{12,8},{1,5},{5,1},{9,13},{13,9},{2,6},{6,2},{1... | collective-permute-start | bytes 393224 | tf_op jit(solution)/shard_map/ppermute | solution.py:107
  26.7 6.7 %collective-permute-start.5 = (bf16[32,4224]{1,0:T(8,128)(2,1)S(1)}, bf16[32,4224]{1,0:T(8,128)(2,1)S(1)}, u32[]{:S(2)}, u32[]{:S(2)}) collective-permute-start(bf16[32,4224]{1,0:T(8,128)(2,1)S(1)} %pad_maximum_fusion.30), channel_id=1, source_target_pairs={{0,64},{64,0},{1,65},{65,1},{2,66},{66,2},{3,67},{67,3},{4,68},{68... | collective-permute-start | bytes 811016 | tf_op jit(solution)/shard_map/ppermute | solution.py:29
  28.3 6.4 %collective-permute-start.2 = (bf16[1,1,64,1152]{3,2,1,0:T(8,128)(2,1)S(1)}, bf16[1,1,64,1152]{3,2,1,0:T(8,128)(2,1)S(1)}, u32[]{:S(2)}, u32[]{:S(2)}) collective-permute-start(bf16[1,1,64,1152]{3,2,1,0:T(8,128)(2,1)S(1)} %slice_bitcast_fusion.6), channel_id=1, source_target_pairs={{0,12},{4,8},{8,4},{12,0},{1,13},{5,9},{9,5},{13,1},{2,14},{6,10},... | collective-permute-start | bytes 442376 | tf_op jit(solution)/shard_map/ppermute | solution.py:107
  34.9 9.8 %collective-permute-start.9 = (bf16[2,1,16,2048]{3,2,1,0:T(8,128)(2,1)S(1)}, bf16[2,1,16,2048]{3,2,1,0:T(8,128)(2,1)S(1)}, u32[]{:S(2)}, u32[]{:S(2)}) collective-permute-start(bf16[2,1,16,2048]{3,2,1,0:T(8,128)(2,1)S(1)} %pad_maximum_fusion.37), channel_id=1, source_target_pairs={{0,16},{16,0},{32,48},{48,32},{1,17},{17,1},{33,49},{49,33},{2,18}... | collective-permute-start | bytes 393224 | tf_op jit(solution)/shard_map/ppermute | solution.py:107
  37.0 7.8 %collective-permute-start.6 = (bf16[1,2,64,1024]{3,2,1,0:T(8,128)(2,1)S(1)}, bf16[1,2,64,1024]{3,2,1,0:T(8,128)(2,1)S(1)}, u32[]{:S(2)}, u32[]{:S(2)}) collective-permute-start(bf16[1,2,64,1024]{3,2,1,0:T(8,128)(2,1)S(1)} %pad_maximum_fusion.31), channel_id=1, source_target_pairs={{0,12},{4,8},{8,4},{12,0},{1,13},{5,9},{9,5},{13,1},{2,14},{6,10},... | collective-permute-start | bytes 786440 | tf_op jit(solution)/shard_map/ppermute | solution.py:107
  39.6 7.7 %collective-permute-start.8 = (bf16[2,1,64,1024]{3,2,1,0:T(8,128)(2,1)S(1)}, bf16[2,1,64,1024]{3,2,1,0:T(8,128)(2,1)S(1)}, u32[]{:S(2)}, u32[]{:S(2)}) collective-permute-start(bf16[2,1,64,1024]{3,2,1,0:T(8,128)(2,1)S(1)} %pad_maximum_fusion.32), channel_id=1, source_target_pairs={{0,48},{16,32},{32,16},{48,0},{1,49},{17,33},{33,17},{49,1},{2,50}... | collective-permute-start | bytes 786440 | tf_op jit(solution)/shard_map/ppermute | solution.py:107
  40.0 8.1 %collective-permute-start.7 = (bf16[1,2,64,1152]{3,2,1,0:T(8,128)(2,1)S(1)}, bf16[1,2,64,1152]{3,2,1,0:T(8,128)(2,1)S(1)}, u32[]{:S(2)}, u32[]{:S(2)}) collective-permute-start(bf16[1,2,64,1152]{3,2,1,0:T(8,128)(2,1)S(1)} %pad_maximum_fusion.29), channel_id=1, source_target_pairs={{0,4},{4,0},{8,12},{12,8},{1,5},{5,1},{9,13},{13,9},{2,6},{6,2},{1... | collective-permute-start | bytes 884744 | tf_op jit(solution)/shard_map/ppermute | solution.py:107
  48.2 15.0 %collective-permute-start.12 = (bf16[4,1,64,1024]{3,2,1,0:T(8,128)(2,1)S(1)}, bf16[4,1,64,1024]{3,2,1,0:T(8,128)(2,1)S(1)}, u32[]{:S(2)}, u32[]{:S(2)}) collective-permute-start(bf16[4,1,64,1024]{3,2,1,0:T(8,128)(2,1)S(1)} %pad_maximum_fusion.18), channel_id=1, source_target_pairs={{0,4},{4,0},{8,12},{12,8},{1,5},{5,1},{9,13},{13,9},{2,6},{6,2},{1... | collective-permute-start | bytes 1572872 | tf_op jit(solution)/shard_map/ppermute | solution.py:107
  49.4 14.3 %collective-permute-start.11 = (bf16[1,4,64,1152]{3,2,1,0:T(8,128)(2,1)S(1)}, bf16[1,4,64,1152]{3,2,1,0:T(8,128)(2,1)S(1)}, u32[]{:S(2)}, u32[]{:S(2)}) collective-permute-start(bf16[1,4,64,1152]{3,2,1,0:T(8,128)(2,1)S(1)} %pad_maximum_fusion.15), channel_id=1, source_target_pairs={{0,48},{16,32},{32,16},{48,0},{1,49},{17,33},{33,17},{49,1},{2,50}... | collective-permute-start | bytes 1769480 | tf_op jit(solution)/shard_map/ppermute | solution.py:107
  52.9 10.8 %collective-permute-start.10 = (bf16[1,4,64,1024]{3,2,1,0:T(8,128)(2,1)S(1)}, bf16[1,4,64,1024]{3,2,1,0:T(8,128)(2,1)S(1)}, u32[]{:S(2)}, u32[]{:S(2)}) collective-permute-start(bf16[1,4,64,1024]{3,2,1,0:T(8,128)(2,1)S(1)} %pad_maximum_fusion.17), channel_id=1, source_target_pairs={{0,16},{16,0},{32,48},{48,32},{1,17},{17,1},{33,49},{49,33},{2,18}... | collective-permute-start | bytes 1572872 | tf_op jit(solution)/shard_map/ppermute | solution.py:107
  53.0 10.2 %collective-permute-start.13 = (bf16[4,1,16,2048]{3,2,1,0:T(8,128)(2,1)S(1)}, bf16[4,1,16,2048]{3,2,1,0:T(8,128)(2,1)S(1)}, u32[]{:S(2)}, u32[]{:S(2)}) collective-permute-start(bf16[4,1,16,2048]{3,2,1,0:T(8,128)(2,1)S(1)} %pad_maximum_fusion.33), channel_id=1, source_target_pairs={{0,12},{4,8},{8,4},{12,0},{1,13},{5,9},{9,5},{13,1},{2,14},{6,10},... | collective-permute-start | bytes 786440 | tf_op jit(solution)/shard_map/ppermute | solution.py:107
  63.9 19.2 %collective-permute-start.16 = (bf16[4,2,64,1024]{3,2,1,0:T(8,128)(2,1)S(1)}, bf16[4,2,64,1024]{3,2,1,0:T(8,128)(2,1)S(1)}, u32[]{:S(2)}, u32[]{:S(2)}) collective-permute-start(bf16[4,2,64,1024]{3,2,1,0:T(8,128)(2,1)S(1)} %pad_maximum_fusion.9), channel_id=1, source_target_pairs={{0,12},{4,8},{8,4},{12,0},{1,13},{5,9},{9,5},{13,1},{2,14},{6,10},... | collective-permute-start | bytes 3145736 | tf_op jit(solution)/shard_map/ppermute | solution.py:107
  65.2 17.9 %collective-permute-start.14 = (bf16[2,4,64,1024]{3,2,1,0:T(8,128)(2,1)}, bf16[2,4,64,1024]{3,2,1,0:T(8,128)(2,1)S(1)}, u32[]{:S(2)}, u32[]{:S(2)}) collective-permute-start(bf16[2,4,64,1024]{3,2,1,0:T(8,128)(2,1)} %pad_maximum_fusion.8), channel_id=1, source_target_pairs={{0,48},{16,32},{32,16},{48,0},{1,49},{17,33},{33,17},{49,1},{2,50}... | collective-permute-start | bytes 3145736 | tf_op jit(solution)/shard_map/ppermute | solution.py:107
  67.7 19.8 %collective-permute-start.15 = (bf16[2,4,64,1152]{3,2,1,0:T(8,128)(2,1)S(1)}, bf16[2,4,64,1152]{3,2,1,0:T(8,128)(2,1)S(1)}, u32[]{:S(2)}, u32[]{:S(2)}) collective-permute-start(bf16[2,4,64,1152]{3,2,1,0:T(8,128)(2,1)S(1)} %pad_maximum_fusion.7), channel_id=1, source_target_pairs={{0,16},{16,0},{32,48},{48,32},{1,17},{17,1},{33,49},{49,33},{2,18}... | collective-permute-start | bytes 3538952 | tf_op jit(solution)/shard_map/ppermute | solution.py:107
  67.9 9.7 %collective-permute-start.17 = (bf16[4,2,16,2048]{3,2,1,0:T(8,128)(2,1)S(1)}, bf16[4,2,16,2048]{3,2,1,0:T(8,128)(2,1)S(1)}, u32[]{:S(2)}, u32[]{:S(2)}) collective-permute-start(bf16[4,2,16,2048]{3,2,1,0:T(8,128)(2,1)S(1)} %pad_maximum_fusion.19), channel_id=1, source_target_pairs={{0,4},{4,0},{8,12},{12,8},{1,5},{5,1},{9,13},{13,9},{2,6},{6,2},{1... | collective-permute-start | bytes 1572872 | tf_op jit(solution)/shard_map/ppermute | solution.py:107
  88.8 11.3 %collective-permute-start.19 = (bf16[2,4,64,1152]{3,2,1,0:T(8,128)(2,1)S(1)}, bf16[2,4,64,1152]{3,2,1,0:T(8,128)(2,1)}, u32[]{:S(2)}, u32[]{:S(2)}) collective-permute-start(bf16[2,4,64,1152]{3,2,1,0:T(8,128)(2,1)S(1)} %collective-permute-done.15), channel_id=1, source_target_pairs={{0,2},{2,0},{1,3},{3,1},{4,6},{6,4},{5,7},{7,5},{8,10},{10,8},{9,1... | collective-permute-start | bytes 3538952 | tf_op jit(solution)/shard_map/ppermute | solution.py:29
  89.0 26.9 %collective-permute-start.23 = (bf16[2,4,64,1024]{3,2,1,0:T(8,128)(2,1)}, bf16[2,4,64,1024]{3,2,1,0:T(8,128)(2,1)}, u32[]{:S(2)}, u32[]{:S(2)}) collective-permute-start(bf16[2,4,64,1024]{3,2,1,0:T(8,128)(2,1)} %pad_maximum_fusion.8), channel_id=1, source_target_pairs={{0,2},{2,0},{1,3},{3,1},{4,6},{6,4},{5,7},{7,5},{8,10},{10,8},{9,1... | collective-permute-start | bytes 3145736 | tf_op jit(solution)/shard_map/ppermute | solution.py:29
  89.4 11.9 %collective-permute-start.18 = (bf16[2,4,64,1152]{3,2,1,0:T(8,128)(2,1)S(1)}, bf16[2,4,64,1152]{3,2,1,0:T(8,128)(2,1)}, u32[]{:S(2)}, u32[]{:S(2)}) collective-permute-start(bf16[2,4,64,1152]{3,2,1,0:T(8,128)(2,1)S(1)} %pad_maximum_fusion.7), channel_id=1, source_target_pairs={{0,2},{2,0},{1,3},{3,1},{4,6},{6,4},{5,7},{7,5},{8,10},{10,8},{9,1... | collective-permute-start | bytes 3538952 | tf_op jit(solution)/shard_map/ppermute | solution.py:29
  89.8 51.0 %all-to-all-start = ((bf16[32,32,1024]{2,1,0:T(8,128)(2,1)}), bf16[32,32,1024]{2,1,0:T(8,128)(2,1)}, u32[]{:S(2)}, u32[]{:S(2)}) async-start(bf16[32,32,1024]{2,1,0:T(8,128)(2,1)} %bitcast.183), calls=%async_computation | async-start | bytes 4194304 | tf_op jit(solution)/shard_map/all_to_all | solution.py:649
  98.2 14.1 %collective-permute-start.24 = (bf16[2,4,64,1024]{3,2,1,0:T(8,128)(2,1)}, bf16[2,4,64,1024]{3,2,1,0:T(8,128)(2,1)}, u32[]{:S(2)}, u32[]{:S(2)}) collective-permute-start(bf16[2,4,64,1024]{3,2,1,0:T(8,128)(2,1)} %copy-done.16), channel_id=1, source_target_pairs={{0,2},{2,0},{1,3},{3,1},{4,6},{6,4},{5,7},{7,5},{8,10},{10,8},{9,1... | collective-permute-start | bytes 3145736 | tf_op jit(solution)/shard_map/ppermute | solution.py:29
  109.5 9.4 %collective-permute-start.20 = (bf16[128,640]{1,0:T(8,128)(2,1)S(1)}, bf16[128,640]{1,0:T(8,128)(2,1)S(1)}, u32[]{:S(2)}, u32[]{:S(2)}) collective-permute-start(bf16[128,640]{1,0:T(8,128)(2,1)S(1)} %pad_maximum_fusion.35), channel_id=1, source_target_pairs={{0,2},{2,0},{1,3},{3,1},{4,6},{6,4},{5,7},{7,5},{8,10},{10,8},{9,1... | collective-permute-start | bytes 491528 | tf_op jit(solution)/shard_map/ppermute | solution.py:29
  110.3 16.3 %collective-permute-start.25 = (bf16[256,2048]{1,0:T(8,128)(2,1)S(1)}, bf16[256,2048]{1,0:T(8,128)(2,1)S(1)}, u32[]{:S(2)}, u32[]{:S(2)}) collective-permute-start(bf16[256,2048]{1,0:T(8,128)(2,1)S(1)} %bitcast.192), channel_id=1, source_target_pairs={{0,2},{2,0},{1,3},{3,1},{4,6},{6,4},{5,7},{7,5},{8,10},{10,8},{9,1... | collective-permute-start | bytes 3145736 | tf_op jit(solution)/shard_map/ppermute | solution.py:29
  112.0 49.0 %collective-permute-start.27 = (bf16[1024,1024]{1,0:T(8,128)(2,1)S(1)}, bf16[1024,1024]{1,0:T(8,128)(2,1)}, u32[]{:S(2)}, u32[]{:S(2)}) collective-permute-start(bf16[1024,1024]{1,0:T(8,128)(2,1)S(1)} %bitcast.177), channel_id=1, source_target_pairs={{0,2},{2,0},{1,3},{3,1},{4,6},{6,4},{5,7},{7,5},{8,10},{10,8},{9,1... | collective-permute-start | bytes 6291464 | tf_op jit(solution)/shard_map/ppermute | solution.py:29
  119.0 10.9 %collective-permute-start.22 = (bf16[2,128,640]{2,1,0:T(8,128)(2,1)S(1)}, bf16[2,128,640]{2,1,0:T(8,128)(2,1)S(1)}, u32[]{:S(2)}, u32[]{:S(2)}) collective-permute-start(bf16[2,128,640]{2,1,0:T(8,128)(2,1)S(1)} %pad_maximum_fusion.28), channel_id=1, source_target_pairs={{0,8},{4,12},{8,16},{12,20},{16,24},{20,28},{24,32},{28,36},{32,40... | collective-permute-start | bytes 983048 | tf_op jit(solution)/shard_map/ppermute | solution.py:42
  124.1 9.3 %collective-permute-start.21 = (bf16[2,128,640]{2,1,0:T(8,128)(2,1)S(1)}, bf16[2,128,640]{2,1,0:T(8,128)(2,1)S(1)}, u32[]{:S(2)}, u32[]{:S(2)}) collective-permute-start(bf16[2,128,640]{2,1,0:T(8,128)(2,1)S(1)} %pad_maximum_fusion.28), channel_id=1, source_target_pairs={{0,4},{4,8},{8,12},{12,16},{16,20},{20,24},{24,28},{28,32},{32,36}... | collective-permute-start | bytes 983048 | tf_op jit(solution)/shard_map/ppermute | solution.py:42
  134.3 3.3 collective-permute-start.26
  142.4 27.0 %collective-permute-start.28 = (bf16[512,1024]{1,0:T(8,128)(2,1)S(1)}, bf16[512,1024]{1,0:T(8,128)(2,1)S(1)}, u32[]{:S(2)}, u32[]{:S(2)}) collective-permute-start(bf16[512,1024]{1,0:T(8,128)(2,1)S(1)} %slice.352), channel_id=1, source_target_pairs={{0,1},{1,0},{2,3},{3,2},{4,5},{5,4},{6,7},{7,6},{8,9},{9,8},{10,11... | collective-permute-start | bytes 3145736 | tf_op jit(solution)/shard_map/ppermute | solution.py:29
  169.4 14.9 %collective-permute-start.29 = (bf16[128,2048]{1,0:T(8,128)(2,1)S(1)}, bf16[128,2048]{1,0:T(8,128)(2,1)S(1)}, u32[]{:S(2)}, u32[]{:S(2)}) collective-permute-start(bf16[128,2048]{1,0:T(8,128)(2,1)S(1)} %pad_maximum_fusion.20), channel_id=1, source_target_pairs={{0,1},{1,0},{2,3},{3,2},{4,5},{5,4},{6,7},{7,6},{8,9},{9,8},{10,11... | collective-permute-start | bytes 1572872 | tf_op jit(solution)/shard_map/ppermute | solution.py:29
  173.4 45.2 %collective-permute-start.32 = (bf16[128,1024]{1,0:T(8,128)(2,1)}, bf16[128,1024]{1,0:T(8,128)(2,1)}, u32[]{:S(2)}, u32[]{:S(2)}) collective-permute-start(bf16[128,1024]{1,0:T(8,128)(2,1)} %get-tuple-element.501), channel_id=1, source_target_pairs={{0,2},{2,0},{1,3},{3,1},{4,6},{6,4},{5,7},{7,5},{8,10},{10,8},{9,1... | collective-permute-start | bytes 786440 | tf_op jit(solution)/shard_map/ppermute | solution.py:29
  190.7 72.4 %all-to-all-start.1 = ((bf16[32,32,2048]{2,1,0:T(8,128)(2,1)}), bf16[32,32,2048]{2,1,0:T(8,128)(2,1)}, u32[]{:S(2)}, u32[]{:S(2)}) async-start(bf16[32,32,2048]{2,1,0:T(8,128)(2,1)} %bitcast.194), calls=%async_computation.1 | async-start | bytes 8388608 | tf_op jit(solution)/shard_map/all_to_all | solution.py:649
  205.2 249.9 %reduce-scatter.3.cloned.1.call-start = ((), (), s32[]{:S(2)}) async-start(), calls=%async_computation.8 | async-start | bytes 9191424 | tf_op jit(solution)/shard_map/reduce_scatter | solution.py:828
  218.5 3.2 collective-permute-start.31
  233.4 7.4 %collective-permute-start.34 = (bf16[128,4224]{1,0:T(8,128)(2,1)}, bf16[128,4224]{1,0:T(8,128)(2,1)S(1)}, u32[]{:S(2)}, u32[]{:S(2)}) collective-permute-start(bf16[128,4224]{1,0:T(8,128)(2,1)} %shared_acts.1.own_ref), channel_id=1, source_target_pairs={{0,2},{2,0},{1,3},{3,1},{4,6},{6,4},{5,7},{7,5},{8,10},{10,8},{9,1... | collective-permute-start | bytes 3244040 | tf_op jit(solution)/shard_map/ppermute | solution.py:29
  235.9 27.1 %collective-permute-start.35 = (bf16[512,1024]{1,0:T(8,128)(2,1)}, bf16[512,1024]{1,0:T(8,128)(2,1)}, u32[]{:S(2)}, u32[]{:S(2)}) collective-permute-start(bf16[512,1024]{1,0:T(8,128)(2,1)} %slice.364), channel_id=1, source_target_pairs={{0,1},{1,0},{2,3},{3,2},{4,5},{5,4},{6,7},{7,6},{8,9},{9,8},{10,11... | collective-permute-start | bytes 3145736 | tf_op jit(solution)/shard_map/ppermute | solution.py:29
  289.3 68.4 %all-to-all-start.2 = ((bf16[32,32,2048]{2,1,0:T(8,128)(2,1)}), bf16[32,32,2048]{2,1,0:T(8,128)(2,1)}, u32[]{:S(2)}, u32[]{:S(2)}) async-start(bf16[32,32,2048]{2,1,0:T(8,128)(2,1)} %bitcast.195), calls=%async_computation.2 | async-start | bytes 8388608 | tf_op jit(solution)/shard_map/all_to_all | solution.py:649
  301.6 49.9 %collective-permute-start.36 = (bf16[704,1536]{1,0:T(8,128)(2,1)S(1)}, bf16[704,1536]{1,0:T(8,128)(2,1)}, u32[]{:S(2)}, u32[]{:S(2)}) collective-permute-start(bf16[704,1536]{1,0:T(8,128)(2,1)S(1)} %convolution_convert_fusion.2), channel_id=1, source_target_pairs={{0,64},{64,0},{1,65},{65,1},{2,66},{66,2},{3,67},{67,3},{4,68},{68... | collective-permute-start | bytes 6488072 | tf_op jit(solution)/shard_map/ppermute | solution.py:29
  311.3 24.7 %collective-permute-start.37 = (bf16[128,2048]{1,0:T(8,128)(2,1)}, bf16[128,2048]{1,0:T(8,128)(2,1)S(1)}, u32[]{:S(2)}, u32[]{:S(2)}) collective-permute-start(bf16[128,2048]{1,0:T(8,128)(2,1)} %get-tuple-element.294), channel_id=1, source_target_pairs={{0,2},{2,0},{1,3},{3,1},{4,6},{6,4},{5,7},{7,5},{8,10},{10,8},{9,1... | collective-permute-start | bytes 1572872 | tf_op jit(solution)/shard_map/ppermute | solution.py:29
  363.1 18.3 %collective-permute-start.38 = (bf16[128,2048]{1,0:T(8,128)(2,1)}, bf16[128,2048]{1,0:T(8,128)(2,1)}, u32[]{:S(2)}, u32[]{:S(2)}) collective-permute-start(bf16[128,2048]{1,0:T(8,128)(2,1)} %combine.1), channel_id=1, source_target_pairs={{0,1},{1,0},{2,3},{3,2},{4,5},{5,4},{6,7},{7,6},{8,9},{9,8},{10,11... | collective-permute-start | bytes 1572872 | tf_op jit(solution)/shard_map/ppermute | solution.py:29
  369.9 85.2 %all-to-all-start.3 = ((bf16[32,32,2048]{2,1,0:T(8,128)(2,1)}), bf16[32,32,2048]{2,1,0:T(8,128)(2,1)}, u32[]{:S(2)}, u32[]{:S(2)}) async-start(bf16[32,32,2048]{2,1,0:T(8,128)(2,1)} %bitcast.193), calls=%async_computation.4 | async-start | bytes 8388608 | tf_op jit(solution)/shard_map/all_to_all | solution.py:649
  381.1 198.4 %reduce-scatter.5.cloned.1.call-start = ((), (), s32[]{:S(2)}) async-start(), calls=%async_computation.9 | async-start | bytes 6963200 | tf_op jit(solution)/shard_map/reduce_scatter | solution.py:999
  386.1 29.7 %collective-permute-start.39 = (bf16[704,512]{1,0:T(8,128)(2,1)S(1)}, bf16[704,512]{1,0:T(8,128)(2,1)S(1)}, u32[]{:S(2)}, u32[]{:S(2)}) collective-permute-start(bf16[704,512]{1,0:T(8,128)(2,1)S(1)} %copy-done.52), channel_id=1, source_target_pairs={{0,64},{64,0},{1,65},{65,1},{2,66},{66,2},{3,67},{67,3},{4,68},{68... | collective-permute-start | bytes 2162696 | tf_op jit(solution)/shard_map/ppermute | solution.py:29
  386.1 33.7 %collective-permute-start.40 = (bf16[512,704]{0,1:T(8,128)(2,1)S(1)}, bf16[512,704]{0,1:T(8,128)(2,1)S(1)}, u32[]{:S(2)}, u32[]{:S(2)}) collective-permute-start(bf16[512,704]{0,1:T(8,128)(2,1)S(1)} %copy-done.50), channel_id=1, source_target_pairs={{0,64},{64,0},{1,65},{65,1},{2,66},{66,2},{3,67},{67,3},{4,68},{68... | collective-permute-start | bytes 2162696 | tf_op jit(solution)/shard_map/ppermute | solution.py:29
  422.6 5.0 collective-permute-start.43
  422.7 3.0 collective-permute-start.44
  423.4 3.5 collective-permute-start.45
  423.8 3.8 collective-permute-start.41
  425.9 26.2 %collective-permute-start.50 = (bf16[768,704]{0,1:T(8,128)(2,1)S(1)}, bf16[768,704]{0,1:T(8,128)(2,1)S(1)}, u32[]{:S(2)}, u32[]{:S(2)}) collective-permute-start(bf16[768,704]{0,1:T(8,128)(2,1)S(1)} %copy-done.42), channel_id=1, source_target_pairs={{0,64},{64,0},{1,65},{65,1},{2,66},{66,2},{3,67},{67,3},{4,68},{68... | collective-permute-start | bytes 3244040 | tf_op jit(solution)/shard_map/ppermute | solution.py:29
  428.0 25.1 %collective-permute-start.49 = (bf16[128,640]{1,0:T(8,128)(2,1)S(1)}, bf16[128,640]{1,0:T(8,128)(2,1)S(1)}, u32[]{:S(2)}, u32[]{:S(2)}) collective-permute-start(bf16[128,640]{1,0:T(8,128)(2,1)S(1)} %get-tuple-element.471), channel_id=1, source_target_pairs={{4,0},{8,4},{12,8},{16,12},{20,16},{24,20},{28,24},{32,28},{36,32}... | collective-permute-start | bytes 491528 | tf_op jit(solution)/shard_map/ppermute | solution.py:35
  429.3 24.5 %collective-permute-start.48 = (bf16[128,640]{1,0:T(8,128)(2,1)S(1)}, bf16[128,640]{1,0:T(8,128)(2,1)S(1)}, u32[]{:S(2)}, u32[]{:S(2)}) collective-permute-start(bf16[128,640]{1,0:T(8,128)(2,1)S(1)} %get-tuple-element.472), channel_id=1, source_target_pairs={{8,0},{12,4},{16,8},{20,12},{24,16},{28,20},{32,24},{36,28},{40,32... | collective-permute-start | bytes 491528 | tf_op jit(solution)/shard_map/ppermute | solution.py:35
  430.6 23.8 %collective-permute-start.47 = (bf16[128,640]{1,0:T(8,128)(2,1)S(1)}, bf16[128,640]{1,0:T(8,128)(2,1)S(1)}, u32[]{:S(2)}, u32[]{:S(2)}) collective-permute-start(bf16[128,640]{1,0:T(8,128)(2,1)S(1)} %get-tuple-element.473), channel_id=1, source_target_pairs={{12,0},{16,4},{20,8},{24,12},{28,16},{32,20},{36,24},{40,28},{44,3... | collective-permute-start | bytes 491528 | tf_op jit(solution)/shard_map/ppermute | solution.py:35
  431.9 23.2 %collective-permute-start.46 = (bf16[128,640]{1,0:T(8,128)(2,1)S(1)}, bf16[128,640]{1,0:T(8,128)(2,1)}, u32[]{:S(2)}, u32[]{:S(2)}) collective-permute-start(bf16[128,640]{1,0:T(8,128)(2,1)S(1)} %get-tuple-element.474), channel_id=1, source_target_pairs={{16,0},{20,4},{24,8},{28,12},{32,16},{36,20},{40,24},{44,28},{48,3... | collective-permute-start | bytes 491528 | tf_op jit(solution)/shard_map/ppermute | solution.py:35
  463.6 27.1 %collective-permute-start.53 = (bf16[768,704]{0,1:T(8,128)(2,1)}, bf16[768,704]{0,1:T(8,128)(2,1)}, u32[]{:S(2)}, u32[]{:S(2)}) collective-permute-start(bf16[768,704]{0,1:T(8,128)(2,1)} %fusion.27), channel_id=1, source_target_pairs={{0,64},{64,0},{1,65},{65,1},{2,66},{66,2},{3,67},{67,3},{4,68},{68... | collective-permute-start | bytes 3244040 | tf_op jit(solution)/shard_map/ppermute | solution.py:29
  463.9 64.8 %collective-permute-start.54 = (bf16[1024,704]{0,1:T(8,128)(2,1)}, bf16[1024,704]{0,1:T(8,128)(2,1)}, u32[]{:S(2)}, u32[]{:S(2)}) collective-permute-start(bf16[1024,704]{0,1:T(8,128)(2,1)} %fusion.14), channel_id=1, source_target_pairs={{0,64},{64,0},{1,65},{65,1},{2,66},{66,2},{3,67},{67,3},{4,68},{68... | collective-permute-start | bytes 4325384 | tf_op jit(solution)/shard_map/ppermute | solution.py:29
  465.7 112.0 %collective-permute-start.58 = (bf16[1024,704]{0,1:T(8,128)(2,1)}, bf16[1024,704]{0,1:T(8,128)(2,1)}, u32[]{:S(2)}, u32[]{:S(2)}) collective-permute-start(bf16[1024,704]{0,1:T(8,128)(2,1)} %fusion.17), channel_id=1, source_target_pairs={{0,64},{64,0},{1,65},{65,1},{2,66},{66,2},{3,67},{67,3},{4,68},{68... | collective-permute-start | bytes 4325384 | tf_op jit(solution)/shard_map/ppermute | solution.py:29
  492.2 36.6 %all-to-all-start.4 = ((bf16[16,64,640]{2,1,0:T(8,128)(2,1)}), bf16[16,64,640]{2,1,0:T(8,128)(2,1)}, u32[]{:S(2)}, u32[]{:S(2)}) async-start(bf16[16,64,640]{2,1,0:T(8,128)(2,1)} %bitcast.189), calls=%async_computation.5 | async-start | bytes 2621440 | tf_op jit(solution)/shard_map/all_to_all | solution.py:1022
  510.9 52.7 %collective-permute-start.56 = (bf16[128,2048]{1,0:T(8,128)(2,1)S(1)}, bf16[128,2048]{1,0:T(8,128)(2,1)S(1)}, u32[]{:S(2)}, u32[]{:S(2)}) collective-permute-start(bf16[128,2048]{1,0:T(8,128)(2,1)S(1)} %pad_maximum_fusion.25), channel_id=1, source_target_pairs={{0,1},{1,0},{2,3},{3,2},{4,5},{5,4},{6,7},{7,6},{8,9},{9,8},{10,11... | collective-permute-start | bytes 1572872 | tf_op jit(solution)/shard_map/ppermute | solution.py:29
  517.6 57.3 %collective-permute-start.55 = (bf16[128,2048]{1,0:T(8,128)(2,1)}, bf16[128,2048]{1,0:T(8,128)(2,1)}, u32[]{:S(2)}, u32[]{:S(2)}) collective-permute-start(bf16[128,2048]{1,0:T(8,128)(2,1)} %routed.1.part_ref), channel_id=1, source_target_pairs={{0,1},{1,0},{2,3},{3,2},{4,5},{5,4},{6,7},{7,6},{8,9},{9,8},{10,11... | collective-permute-start | bytes 1572872 | tf_op jit(solution)/shard_map/ppermute | solution.py:29
  530.7 48.8 %collective-permute-start.59 = (bf16[32,4224]{1,0:T(8,128)(2,1)}, bf16[32,4224]{1,0:T(8,128)(2,1)}, u32[]{:S(2)}, u32[]{:S(2)}) collective-permute-start(bf16[32,4224]{1,0:T(8,128)(2,1)} %get-tuple-element.482), channel_id=1, source_target_pairs={{0,64},{64,0},{1,65},{65,1},{2,66},{66,2},{3,67},{67,3},{4,68},{68... | collective-permute-start | bytes 811016 | tf_op jit(solution)/shard_map/ppermute | solution.py:29
  580.5 6.9 %collective-permute-start.60 = (bf16[32,3840]{1,0:T(8,128)(2,1)S(1)}, bf16[32,3840]{1,0:T(8,128)(2,1)S(1)}, u32[]{:S(2)}, u32[]{:S(2)}) collective-permute-start(bf16[32,3840]{1,0:T(8,128)(2,1)S(1)} %dynamic-slice_bitcast_fusion.4), channel_id=1, source_target_pairs={{0,64},{64,0},{1,65},{65,1},{2,66},{66,2},{3,67},{67,3},{4,68},{68... | collective-permute-start | bytes 737288 | tf_op jit(solution)/shard_map/ppermute | solution.py:29
  589.4 6.1 %collective-permute-start.61 = (f32[32,768]{1,0:T(8,128)S(1)}, f32[32,768]{1,0:T(8,128)S(1)}, u32[]{:S(2)}, u32[]{:S(2)}) collective-permute-start(f32[32,768]{1,0:T(8,128)S(1)} %maximum_maximum_fusion), channel_id=1, source_target_pairs={{0,1},{1,0},{2,3},{3,2},{4,5},{5,4},{6,7},{7,6},{8,9},{9,8},{10,11... | collective-permute-start | bytes 294920 | tf_op jit(solution)/shard_map/ppermute | solution.py:29
  (112 other events, 814.5 us)
Sparse Core Ops, SparseCore 0:
  89.0 90.4 all-gather.1
  263.2 161.8 reduce-scatter.2
  463.7 91.4 reduce-scatter.4
